TPU v7x, 32 devices: a whole 2x2x4 slice. The times are simulated.
32 devices in a mesh: expert: 8 (over z, y), half: 4 (over x, core).
Axes of the slice: x: 2, y: 2, z: 4, core: 2. Of those that a mesh axis runs over, the one named last changes fastest.
Arguments:
- tokens: bfloat16 [1568, 1024], P('expert', 'half'), may hold values from -128 to 128
- slot_params: bfloat16 [1024, 16], P('half'), may hold values from -0.5 to 0.5
- w_up: bfloat16 [8, 1024, 4096], P('expert', None, 'half'), may hold values from -0.1875 to 0.1875
- w_down: bfloat16 [8, 4096, 1024], P('expert', 'half'), may hold values from -0.09375 to 0.09375
- cotangent: bfloat16 [1568, 1024], P('expert', 'half'), may hold values from -6 to 6
Outputs:
- mixed: bfloat16 [1568, 1024], P('expert', 'half')
- grad_tokens: bfloat16 [1568, 1024], P('expert', 'half')
- grad_params: float32 [1024, 16], P('half')
All inputs are finite; a program needn't handle non-finite values.
Results may differ from a plain program's by a relative error of at most 0.017.
Values may be sent and summed in bfloat16 or wider, within the bound.
No kernel may reach another device: no remote copies, remote signals or barrier semaphores. Data moves between devices by JAX's collectives and lax.ppermute only.
A program may use at most 64 MiB of HBM per device.

v0:
```python
import jax
import jax.numpy as jnp
from jax import lax
from jax.sharding import PartitionSpec as P

SEQ = 196
SLOTS = 2


def gelu_grad(preact, upstream):
    pullback = jax.vjp(jax.nn.gelu, preact)[1]
    return pullback(upstream)[0]


def softmax_back(probabilities, upstream, over_axis):
    inner = jnp.sum(probabilities * upstream, axis=over_axis, keepdims=True)
    return probabilities * (upstream - inner)


def local(tokens, slot_params, w_up, w_down, cotangent):
    feat_quarter = tokens.shape[1]
    images = tokens.shape[0] // SEQ
    columns = slot_params.shape[1]
    experts = columns // SLOTS
    up_matrix = w_up[0]
    down_matrix = w_down[0]
    inputs = tokens.reshape(images, SEQ, feat_quarter)
    upstream = cotangent.reshape(images, SEQ, feat_quarter)
    partial_logits = jnp.einsum(
        "imf,fc->imc", inputs, slot_params, preferred_element_type=jnp.float32
    )
    logits = lax.psum(partial_logits, "half")
    dispatch = jax.nn.softmax(logits, axis=1)
    combine = jax.nn.softmax(logits, axis=2)
    dispatch_bf = dispatch.astype(jnp.bfloat16).reshape(images, SEQ, experts, SLOTS)
    combine_bf = combine.astype(jnp.bfloat16).reshape(images, SEQ, experts, SLOTS)
    slot_in = jnp.einsum(
        "imes,imf->sife", dispatch_bf, inputs, preferred_element_type=jnp.float32
    ).astype(jnp.bfloat16)
    received = lax.all_to_all(slot_in, "expert", split_axis=3, concat_axis=3, tiled=True)
    up_slice = up_matrix
    preact = jnp.einsum(
        "sifr,fk->sirk",
        lax.all_gather(received, "half", axis=2, tiled=True),
        up_slice,
        preferred_element_type=jnp.float32,
    )
    hidden = jax.nn.gelu(preact).astype(jnp.bfloat16)
    down_slice = down_matrix
    summed = lax.psum(
        jnp.einsum("kf,sirk->fsir", down_slice, hidden, preferred_element_type=jnp.float32).astype(
            jnp.bfloat16
        ),
        "half",
    ).astype(jnp.float32)
    slot_out = lax.dynamic_slice_in_dim(
        summed, lax.axis_index("half") * feat_quarter, feat_quarter, 0
    )
    returned = lax.all_to_all(
        slot_out.astype(jnp.bfloat16), "expert", split_axis=3, concat_axis=3, tiled=True
    )
    mixed = jnp.einsum(
        "imes,fsie->imf", combine_bf, returned, preferred_element_type=jnp.float32
    ).astype(jnp.bfloat16)
    grad_slot_out = jnp.einsum(
        "imes,imf->sife", combine_bf, upstream, preferred_element_type=jnp.float32
    ).astype(jnp.bfloat16)
    combine_part = jnp.einsum(
        "imf,fsie->imes", upstream, returned, preferred_element_type=jnp.float32
    ).reshape(images, SEQ, columns)
    grad_received = lax.all_to_all(grad_slot_out, "expert", split_axis=3, concat_axis=3, tiled=True)
    down_slice = down_matrix
    grad_hidden = jnp.einsum(
        "sifr,kf->sirk",
        lax.all_gather(grad_received, "half", axis=2, tiled=True),
        down_slice,
        preferred_element_type=jnp.float32,
    )
    grad_preact = gelu_grad(preact, grad_hidden).astype(jnp.bfloat16)
    up_slice = up_matrix
    summed_grad = lax.psum(
        jnp.einsum(
            "fk,sirk->fsir", up_slice, grad_preact, preferred_element_type=jnp.float32
        ).astype(jnp.bfloat16),
        "half",
    ).astype(jnp.float32)
    grad_slot_in = lax.dynamic_slice_in_dim(
        summed_grad, lax.axis_index("half") * feat_quarter, feat_quarter, 0
    )
    grad_returned = lax.all_to_all(
        grad_slot_in.astype(jnp.bfloat16), "expert", split_axis=3, concat_axis=3, tiled=True
    )
    dispatch_part = jnp.einsum(
        "imf,fsie->imes", inputs, grad_returned, preferred_element_type=jnp.float32
    ).reshape(images, SEQ, columns)
    local_grad = softmax_back(combine, combine_part, 2) + softmax_back(dispatch, dispatch_part, 1)
    grad_logits = lax.psum(local_grad.astype(jnp.bfloat16), "half")
    token_term = jnp.einsum(
        "imes,fsie->imf", dispatch_bf, grad_returned, preferred_element_type=jnp.float32
    )
    logit_term = jnp.einsum(
        "imc,fc->imf", grad_logits, slot_params, preferred_element_type=jnp.float32
    )
    grad_tokens = (token_term + logit_term).astype(jnp.bfloat16).reshape(images * SEQ, feat_quarter)
    params_part = jnp.einsum("imf,imc->fc", inputs, grad_logits, preferred_element_type=jnp.float32)
    grad_params = lax.psum(params_part, "expert")
    return (mixed.reshape(images * SEQ, feat_quarter), grad_tokens, grad_params)


def solution(mesh):
    in_specs = (
        P("expert", "half"),
        P("half", None),
        P("expert", None, "half"),
        P("expert", "half", None),
        P("expert", "half"),
    )
    out_specs = (P("expert", "half"), P("expert", "half"), P("half", None))
    return jax.shard_map(local, mesh=mesh, in_specs=in_specs, out_specs=out_specs, check_vma=False)
```

profile of v0, /device:TPU:0, one launch (start us, length us, event | category | flops | bytes accessed | tf_op | source)
XLA Modules:
  0.0 160.1 jit_solution(4971879648403036365)
XLA Ops:
  7.2 1.2 convolution_bitcast_fusion.5
  8.4 12.7 %psum.35 = f32[1,196,16]{1,2,0:T(8,128)S(1)} all-reduce(f32[1,196,16]{1,2,0:T(8,128)S(1)} %convolution_bitcast_fusion.5), channel_id=1, replica_groups=mesh['expert'=8,'half'=4] {'half'}, use_global_device_ids=true, to_apply=%region_0.0 | all-reduce | flops 3136 | bytes 25088 | tf_op jit(solution)/shard_map/psum | solution.py:32
  21.2 0.2 fusion.58
  21.5 1.0 fusion.22
  22.5 0.6 copy.15
  23.1 5.8 %all-to-all-start = ((bf16[2,1,256,8]{2,0,1,3:T(2,128)(2,1)}), bf16[2,1,256,8]{2,0,1,3:T(2,128)(2,1)S(1)}, u32[]{:S(2)}, u32[]{:S(2)}) async-start(bf16[2,1,256,8]{2,0,1,3:T(2,128)(2,1)} %copy.15), calls=%async_computation | async-start | bytes 16384 | tf_op jit(solution)/shard_map/all_to_all | solution.py:40
  29.0 1.0 fusion.23
  30.0 0.6 copy.21
  30.6 4.9 %all-to-all-done = bf16[2,1,256,8]{2,0,1,3:T(2,128)(2,1)S(1)} async-done(((bf16[2,1,256,8]{2,0,1,3:T(2,128)(2,1)}), bf16[2,1,256,8]{2,0,1,3:T(2,128)(2,1)S(1)}, u32[]{:S(2)}, u32[]{:S(2)}) %all-to-all-start) | async-done | bytes 8224 | tf_op jit(solution)/shard_map/all_to_all | solution.py:40
  35.5 3.3 %all-to-all-start.2 = ((bf16[2,1,256,8]{2,0,1,3:T(2,128)(2,1)}), bf16[2,1,256,8]{2,0,1,3:T(2,128)(2,1)S(1)}, u32[]{:S(2)}, u32[]{:S(2)}) async-start(bf16[2,1,256,8]{2,0,1,3:T(2,128)(2,1)} %copy.21), calls=%async_computation.2 | async-start | bytes 16384 | tf_op jit(solution)/shard_map/all_to_all | solution.py:71
  38.9 5.2 %all_gather.6 = bf16[2,1,1024,8]{2,3,0,1:T(8,128)(2,1)S(1)} all-gather(bf16[2,1,256,8]{2,3,0,1:T(8,128)(2,1)S(1)} %copy.16), channel_id=1, replica_groups=mesh['expert'=8,'half'=4] {'half'}, dimensions={2}, use_global_device_ids=true | all-gather | bytes 40960 | tf_op jit(solution)/shard_map/all_gather | solution.py:44
  44.1 1.2 all-to-all-done.2
  45.3 5.2 %all_gather.7 = bf16[2,1,1024,8]{2,3,0,1:T(8,128)(2,1)S(1)} all-gather(bf16[2,1,256,8]{2,3,0,1:T(8,128)(2,1)S(1)} %copy.22), channel_id=1, replica_groups=mesh['expert'=8,'half'=4] {'half'}, dimensions={2}, use_global_device_ids=true | all-gather | bytes 40960 | tf_op jit(solution)/shard_map/all_gather | solution.py:75
  50.4 2.0 %fusion.6 = f32[2,8,1024]{2,1,0:T(8,128)S(1)} fusion(bf16[1,1024,1024]{2,1,0:T(8,128)(2,1)} %param.7, bf16[2,1,1024,8]{2,3,0,1:T(8,128)(2,1)S(1)} %all_gather.6), kind=kOutput, calls=%fused_computation.6 | convolution fusion | flops 33554432 | bytes 2195456 | tf_op jit(solution)/shard_map/sifr,fk->sirk/dot_general | solution.py:42
  52.4 1.0 fusion.16
  53.4 3.4 %fusion.19 = bf16[1024,2,1,8]{0,3,1,2:T(8,128)(2,1)} fusion(bf16[1,1024,1024]{2,1,0:T(8,128)(2,1)} %param.7, f32[2,8,1024]{2,1,0:T(8,128)S(1)} %fusion.6, bf16[1,1024,1024]{2,1,0:T(8,128)(2,1)S(1)} %copy-done, bf16[2,1,1024,8]{2,3,0,1:T(8,128)(2,1)S(1)} %all_gather.7), kind=kOutput, calls=%fused_computation.16 | convolution fusion | flops 67452928 | bytes 4325376 | tf_op jit(solution)/shard_map/fk,sirk->fsir/dot_general | solution.py:82
  56.9 30.5 %all-reduce.3.cloned.1.call-done = (bf16[1024,2,1,8]{0,3,1,2:T(8,128)(2,1)}, bf16[1024,2,1,8]{0,3,1,2:T(8,128)(2,1)}) async-done(((bf16[1024,2,1,8]{0,3,1,2:T(8,128)(2,1)}, bf16[1024,2,1,8]{0,3,1,2:T(8,128)(2,1)}), (bf16[1024,2,1,8]{0,3,1,2:T(8,128)(2,1)}, bf16[1024,2,1,8]{0,3,1,2:T(8,128)(2,1)})) %all-reduce.3.cloned.1.call-update) | async-done | bytes 65552 | tf_op jit(solution)/shard_map/psum | solution.py:50
  87.4 0.7 convert_convert_fusion
  88.1 0.6 copy.23
  88.7 5.5 %all-to-all-start.3 = ((bf16[256,2,1,8]{0,1,2,3:T(2,128)(2,1)}), bf16[256,2,1,8]{0,1,2,3:T(2,128)(2,1)S(1)}, u32[]{:S(2)}, u32[]{:S(2)}) async-start(bf16[256,2,1,8]{0,1,2,3:T(2,128)(2,1)} %copy.23), calls=%async_computation.3 | async-start | bytes 16384 | tf_op jit(solution)/shard_map/all_to_all | solution.py:90
  94.2 0.7 convert_convert_fusion.1
  94.9 0.6 copy.17
  95.5 5.2 %all-to-all-done.3 = bf16[256,2,1,8]{0,1,2,3:T(2,128)(2,1)S(1)} async-done(((bf16[256,2,1,8]{0,1,2,3:T(2,128)(2,1)}), bf16[256,2,1,8]{0,1,2,3:T(2,128)(2,1)S(1)}, u32[]{:S(2)}, u32[]{:S(2)}) %all-to-all-start.3) | async-done | bytes 8224 | tf_op jit(solution)/shard_map/all_to_all | solution.py:90
  100.7 3.3 %all-to-all-start.1 = ((bf16[256,2,1,8]{0,1,2,3:T(2,128)(2,1)}), bf16[256,2,1,8]{0,1,2,3:T(2,128)(2,1)S(1)}, u32[]{:S(2)}, u32[]{:S(2)}) async-start(bf16[256,2,1,8]{0,1,2,3:T(2,128)(2,1)} %copy.17), calls=%async_computation.1 | async-start | bytes 16384 | tf_op jit(solution)/shard_map/all_to_all | solution.py:59
  104.3 6.2 %all-to-all-done.1 = bf16[256,2,1,8]{0,1,2,3:T(2,128)(2,1)S(1)} async-done(((bf16[256,2,1,8]{0,1,2,3:T(2,128)(2,1)}), bf16[256,2,1,8]{0,1,2,3:T(2,128)(2,1)S(1)}, u32[]{:S(2)}, u32[]{:S(2)}) %all-to-all-start.1) | async-done | bytes 8224 | tf_op jit(solution)/shard_map/all_to_all | solution.py:59
  110.7 0.2 multiply_reduce_fusion.1
  111.0 6.1 %psum.38 = bf16[196,16]{0,1:T(8,128)(2,1)S(1)} all-reduce(bf16[196,16]{0,1:T(8,128)(2,1)S(1)} %fusion.59), channel_id=1, replica_groups=mesh['expert'=8,'half'=4] {'half'}, use_global_device_ids=true, to_apply=%region_9.0 | all-reduce | flops 3136 | bytes 12544 | tf_op jit(solution)/shard_map/psum | solution.py:97
  117.1 0.1 convolution_bitcast_fusion.2
  117.3 0.2 convolution_bitcast_fusion
  117.5 0.9 fusion.9
  118.4 34.0 %psum.39 = f32[256,16]{0,1:T(8,128)} all-reduce(f32[256,16]{0,1:T(8,128)S(1)} %convolution_bitcast_fusion.2), channel_id=1, replica_groups=mesh['expert'=8,'half'=4] {'expert'}, use_global_device_ids=true, to_apply=%region_10.0 | all-reduce | flops 4096 | bytes 32768 | tf_op jit(solution)/shard_map/psum | solution.py:106
  152.3 0.9 fusion.8
  (23 shorter events, 0.8 us)
Async XLA Ops:
  7.2 45.2 %copy-start = (bf16[1,1024,1024]{2,1,0:T(8,128)(2,1)S(1)}, bf16[1,1024,1024]{2,1,0:T(8,128)(2,1)}, u32[]{:S(2)}) copy-start(bf16[1,1024,1024]{2,1,0:T(8,128)(2,1)} %param.8) | copy-start | bytes 6291460
  23.1 12.3 %all-to-all-start = ((bf16[2,1,256,8]{2,0,1,3:T(2,128)(2,1)}), bf16[2,1,256,8]{2,0,1,3:T(2,128)(2,1)S(1)}, u32[]{:S(2)}, u32[]{:S(2)}) async-start(bf16[2,1,256,8]{2,0,1,3:T(2,128)(2,1)} %copy.15), calls=%async_computation | async-start | bytes 16384 | tf_op jit(solution)/shard_map/all_to_all | solution.py:40
  35.5 9.8 %all-to-all-start.2 = ((bf16[2,1,256,8]{2,0,1,3:T(2,128)(2,1)}), bf16[2,1,256,8]{2,0,1,3:T(2,128)(2,1)S(1)}, u32[]{:S(2)}, u32[]{:S(2)}) async-start(bf16[2,1,256,8]{2,0,1,3:T(2,128)(2,1)} %copy.21), calls=%async_computation.2 | async-start | bytes 16384 | tf_op jit(solution)/shard_map/all_to_all | solution.py:71
  38.8 48.6 %all-reduce.3.cloned.1.call-start = ((), (), s32[]{:S(2)}) async-start(), calls=%async_computation.4 | async-start | bytes 131072 | tf_op jit(solution)/shard_map/psum | solution.py:50
  53.4 50.6 %copy-start.1 = (bf16[196,256]{1,0:T(8,128)(2,1)S(1)}, bf16[196,256]{1,0:T(8,128)(2,1)}, u32[]{:S(2)}) copy-start(bf16[196,256]{1,0:T(8,128)(2,1)} %param.5) | copy-start | bytes 301060
  53.4 57.1 %copy-start.2 = (bf16[196,256]{1,0:T(8,128)(2,1)S(1)}, bf16[196,256]{1,0:T(8,128)(2,1)}, u32[]{:S(2)}) copy-start(bf16[196,256]{1,0:T(8,128)(2,1)} %param.9) | copy-start | bytes 301060
  53.4 64.1 %copy-start.3 = (bf16[256,16]{0,1:T(8,128)(2,1)S(1)}, bf16[256,16]{0,1:T(8,128)(2,1)}, u32[]{:S(2)}) copy-start(bf16[256,16]{0,1:T(8,128)(2,1)} %param.6) | copy-start | bytes 24580
  88.7 12.0 %all-to-all-start.3 = ((bf16[256,2,1,8]{0,1,2,3:T(2,128)(2,1)}), bf16[256,2,1,8]{0,1,2,3:T(2,128)(2,1)S(1)}, u32[]{:S(2)}, u32[]{:S(2)}) async-start(bf16[256,2,1,8]{0,1,2,3:T(2,128)(2,1)} %copy.23), calls=%async_computation.3 | async-start | bytes 16384 | tf_op jit(solution)/shard_map/all_to_all | solution.py:90
  100.7 9.8 %all-to-all-start.1 = ((bf16[256,2,1,8]{0,1,2,3:T(2,128)(2,1)}), bf16[256,2,1,8]{0,1,2,3:T(2,128)(2,1)S(1)}, u32[]{:S(2)}, u32[]{:S(2)}) async-start(bf16[256,2,1,8]{0,1,2,3:T(2,128)(2,1)} %copy.17), calls=%async_computation.1 | async-start | bytes 16384 | tf_op jit(solution)/shard_map/all_to_all | solution.py:59
Sparse Core Ops, SparseCore 0:
  57.0 30.3 all-reduce.2
where the time goes:
time: 161 us; the launch traced here: 160 us
  blocking collectives  63.1 us (39%)
  waiting for transfers between devices  48 us (30%)
  starting transfers between devices  18.1 us (11%)
  between operations  14.2 us (9%)
  matrix products  12 us (7%)
  local copies, waits for them, and re-layouts  2.61 us (2%)
  other arithmetic  2.07 us (1%)
    psum x1, blocking collectives, local(): grad_params = lax.psum(params_part, 'expert')  34 us
    psum x1, waiting for transfers between devices, local(): lax.psum(jnp.einsum('kf,sirk->fsir', down_slice, hidden, preferred_elemen...  30.5 us
    psum x1, blocking collectives, local(): logits = lax.psum(partial_logits, 'half')  12.7 us
    all_to_all x1, waiting for transfers between devices, local(): lax.all_to_all(slot_out.astype(jnp.bfloat16), 'expert', split_axis=3, con...  6.24 us
    psum x1, blocking collectives, local(): grad_logits = lax.psum(local_grad.astype(jnp.bfloat16), 'half')  6.11 us
    all_to_all x1, starting transfers between devices, local(): lax.all_to_all(slot_in, 'expert', split_axis=3, concat_axis=3, tiled=True)  5.83 us
    all_to_all x1, starting transfers between devices, local(): lax.all_to_all(grad_slot_in.astype(jnp.bfloat16), 'expert', split_axis=3,...  5.52 us
    all_to_all x1, waiting for transfers between devices, local(): lax.all_to_all(grad_slot_in.astype(jnp.bfloat16), 'expert', split_axis=3,...  5.21 us
  transfers between devices with their start and end apart: 5, of which 5 were waited for; matrix products, arithmetic and copies ran while one was open for 2% of the time, Pallas kernels for 0%

commit v1 on v0

v1 whole, which is shorter than its diff:
```python
import jax
import jax.numpy as jnp
from jax import lax
from jax.sharding import Mesh, PartitionSpec as P

F32 = jnp.float32
BF16 = jnp.bfloat16


def swap(array, axis):
    return lax.ppermute(array, axis, [(0, 1), (1, 0)])


def dot(left, right, over):
    return lax.dot_general(left, right, ((over[:1], over[1:]), ((), ())), preferred_element_type=F32)


def softmax(logits, axis):
    shifted = jnp.exp(logits - jnp.max(logits, axis=axis, keepdims=True))
    return shifted / jnp.sum(shifted, axis=axis, keepdims=True)


def softmax_back(probabilities, upstream, axis):
    inner = jnp.sum(probabilities * upstream, axis=axis, keepdims=True)
    return probabilities * (upstream - inner)


def gelu_grad(preact, upstream):
    pullback = jax.vjp(jax.nn.gelu, preact)[1]
    return pullback(upstream)[0]


def local(experts, halves, tokens, slot_params, w_up, w_down, cotangent):
    seq, quarter = tokens.shape
    columns = slot_params.shape[1]
    slots = columns // experts
    x_size = halves // 2
    half = lax.axis_index("x") * 2 + lax.axis_index("core")
    up_matrix, down_matrix = w_up[0], w_down[0]

    logits = dot(slot_params, tokens, (0, 1))
    logits = logits + swap(logits, "core")
    logits = logits + swap(logits, "x")
    both = jnp.stack([tokens, cotangent])
    across = swap(both, "x")
    beside = swap(jnp.stack([both, across]), "core")
    dispatch = softmax(logits, 1)
    combine = softmax(logits, 0)
    dispatch_bf = dispatch.astype(BF16)
    combine_bf = combine.astype(BF16)
    slot_in = dot(dispatch_bf, tokens, (1, 0)).astype(BF16).reshape(experts, 1, slots, quarter)
    grad_out = dot(combine_bf, cotangent, (1, 0)).astype(BF16).reshape(experts, 1, slots, quarter)
    rows = jnp.concatenate([slot_in, grad_out], axis=1).reshape(1, experts, 2 * slots, quarter)
    rows = jnp.broadcast_to(rows, (halves, experts, 2 * slots, quarter)).reshape(halves * experts, 2 * slots, quarter)

    got = lax.all_to_all(rows, ("x", "core", "expert"), 0, 0, tiled=True)
    got = got.reshape(halves, experts, 2, slots, quarter)
    forward = got[:, :, 0].reshape(halves, experts * slots, quarter)
    backward = got[:, :, 1].reshape(halves, experts * slots, quarter)
    forward = jnp.transpose(forward, (1, 0, 2)).reshape(experts * slots, halves * quarter)
    backward = jnp.transpose(backward, (1, 0, 2)).reshape(experts * slots, halves * quarter)
    preact = dot(forward, up_matrix, (1, 0))
    hidden = jax.nn.gelu(preact).astype(BF16)
    out_part = dot(hidden, down_matrix, (1, 0)).astype(BF16)
    grad_hidden = dot(backward, down_matrix, (1, 1))
    grad_preact = gelu_grad(preact, grad_hidden).astype(BF16)
    in_part = dot(grad_preact, up_matrix, (1, 1)).astype(BF16)
    part = jnp.stack([out_part.reshape(experts, slots, -1), in_part.reshape(experts, slots, -1)], axis=1)
    part = part.reshape(experts, 2 * slots, halves * quarter)

    pair = (part.astype(F32) + swap(part, "core").astype(F32)).astype(BF16)
    pair = jnp.broadcast_to(pair[None], (x_size,) + pair.shape).reshape(x_size * experts, 2 * slots, halves * quarter)
    back = lax.all_to_all(pair, ("x", "expert"), 0, 0, tiled=True)
    back = back.reshape(x_size, experts, 2, slots, halves, quarter).astype(F32).sum(0).astype(BF16)
    slot_out = back[:, 0].reshape(columns, halves, quarter)
    grad_in = back[:, 1].reshape(columns, halves, quarter)

    grad_combine = grad_dispatch = 0.0
    parts = (both, beside[0], across, beside[1])
    for offset, (token_part, cotangent_part) in enumerate(parts):
        which = jnp.bitwise_xor(half, offset)
        grad_combine += dot(lax.dynamic_index_in_dim(slot_out, which, 1, False), cotangent_part, (1, 1))
        grad_dispatch += dot(lax.dynamic_index_in_dim(grad_in, which, 1, False), token_part, (1, 1))
    grad_logits = softmax_back(combine, grad_combine, 0) + softmax_back(dispatch, grad_dispatch, 1)
    grad_logit_bf = grad_logits.astype(BF16)

    params_part = dot(grad_logit_bf, tokens, (1, 0)).astype(BF16)
    params_part = jnp.broadcast_to(params_part[None], (experts,) + params_part.shape)
    params_parts = lax.all_to_all(params_part, "expert", 0, 0, tiled=True)
    grad_params = params_parts.astype(F32).sum(0).T

    own_out = lax.dynamic_index_in_dim(slot_out, half, 1, False)
    own_in = lax.dynamic_index_in_dim(grad_in, half, 1, False)
    mixed = dot(combine_bf, own_out, (0, 0)).astype(BF16)
    grad_tokens = (dot(dispatch_bf, own_in, (0, 0)) + dot(grad_logit_bf, slot_params, (0, 1))).astype(BF16)
    return mixed, grad_tokens, grad_params


def solution(mesh):
    experts, halves = mesh.shape["expert"], mesh.shape["half"]
    split = Mesh(mesh.devices.reshape(experts, halves // 2, 2), ("expert", "x", "core"))
    half = ("x", "core")
    in_specs = (
        P("expert", half),
        P(half, None),
        P("expert", None, half),
        P("expert", half, None),
        P("expert", half),
    )
    out_specs = (P("expert", half), P("expert", half), P(half, None))

    def program(*args):
        return jax.shard_map(
            lambda *blocks: local(experts, halves, *blocks),
            mesh=split,
            in_specs=in_specs,
            out_specs=out_specs,
            check_vma=False,
        )(*args)

    return program
```

time: 161 us -> 59.9 us (0.37)
  blocking collectives: 63.1 us -> 13.5 us
  waiting for transfers between devices: 48 us -> 16.8 us
  between operations: 14.2 us -> 0.92 us
  starting transfers between devices: 18.1 us -> 11.1 us
  matrix products: 12 us -> 14 us
    psum x3 -> x0, blocking collectives: 52.7 us -> none  [the longest x1 34 us: local(): grad_params = lax.psum(params_part, 'expert')]
    psum x1 -> x0, waiting for transfers between devices: 30.5 us -> none  [local(): lax.psum(jnp.einsum('kf,sirk->fsir', down_slice, hidden, preferred_elemen...]
    all_to_all x0 -> x1, blocking collectives: none -> 13.5 us  [local(): got = lax.all_to_all(rows, ('x', 'core', 'expert'), 0, 0, tiled=True)]
    all_to_all x4 -> x2, starting transfers between devices: 18 us -> 6.86 us  [the longest x1 3.51 us: local(): back = lax.all_to_all(pair, ('x', 'expert'), 0, 0, tiled=True)]
    all_gather x2 -> x0, blocking collectives: 10.4 us -> none  [the longest x1 5.19 us: local(): lax.all_gather(received, 'half', axis=2, tiled=True)]
    all_to_all x4 -> x2, waiting for transfers between devices: 17.5 us -> 11.8 us  [the longest x1 5.97 us: local(): params_parts = lax.all_to_all(params_part, 'expert', 0, 0, tiled=True)]
    ppermute x0 -> x5, waiting for transfers between devices: none -> 5 us  [swap(): return lax.ppermute(array, axis, [(0, 1), (1, 0)])]
    ppermute x0 -> x5, starting transfers between devices: none -> 4.25 us  [swap(): return lax.ppermute(array, axis, [(0, 1), (1, 0)])]
  transfers between devices with their start and end apart: 5 -> 7, of which waited for: 5 -> 6; matrix products, arithmetic and copies ran while one was open for 2% -> 6% of each run, Pallas kernels for 0% -> 0%
where the time goes in v1:
time: 59.9 us; the launch traced here: 59.4 us
  waiting for transfers between devices  16.8 us (28%)
  matrix products  14 us (23%)
  blocking collectives  13.5 us (23%)
  starting transfers between devices  11.1 us (19%)
  local copies, waits for them, and re-layouts  1.83 us (3%)
  other arithmetic  1.21 us (2%)
  between operations  0.92 us (2%)
    dot_general x18, matrix products, dot(): lax.dot_general(left, right, ((over[:1], over[1:]), ((), ())), preferred_...  14 us
    all_to_all x1, blocking collectives, local(): got = lax.all_to_all(rows, ('x', 'core', 'expert'), 0, 0, tiled=True)  13.5 us
    all_to_all x1, waiting for transfers between devices, local(): params_parts = lax.all_to_all(params_part, 'expert', 0, 0, tiled=True)  5.97 us
    all_to_all x1, waiting for transfers between devices, local(): back = lax.all_to_all(pair, ('x', 'expert'), 0, 0, tiled=True)  5.84 us
    ppermute x5, waiting for transfers between devices, swap(): return lax.ppermute(array, axis, [(0, 1), (1, 0)])  5 us
    ppermute x5, starting transfers between devices, swap(): return lax.ppermute(array, axis, [(0, 1), (1, 0)])  4.25 us
    all_to_all x1, starting transfers between devices, local(): back = lax.all_to_all(pair, ('x', 'expert'), 0, 0, tiled=True)  3.51 us
    all_to_all x1, starting transfers between devices, local(): params_parts = lax.all_to_all(params_part, 'expert', 0, 0, tiled=True)  3.35 us
  transfers between devices with their start and end apart: 7, of which 6 were waited for; matrix products, arithmetic and copies ran while one was open for 6% of the time, Pallas kernels for 0%

profile of v1, /device:TPU:0, one launch (start us, length us, event | category | flops | bytes accessed | tf_op | source)
XLA Modules:
  0.0 59.4 jit_solution(15439332153733445316)
XLA Ops:
  0.6 1.2 %fusion.92 = f32[16,196]{1,0:T(8,128)S(1)} fusion(bf16[256,16]{0,1:T(8,128)(2,1)} %param.6, bf16[196,256]{1,0:T(8,128)(2,1)} %param.5), kind=kOutput, calls=%fused_computation.116 | convolution fusion | flops 1605632 | bytes 121088 | tf_op jit(solution)/shard_map/dot_general | solution.py:15
  1.8 0.5 collective-permute-start
  2.3 0.8 %collective-permute-done = f32[16,196]{1,0:T(8,128)S(1)} collective-permute-done((f32[16,196]{1,0:T(8,128)S(1)}, f32[16,196]{1,0:T(8,128)S(1)}, u32[]{:S(2)}, u32[]{:S(2)}) %collective-permute-start) | collective-permute-done | bytes 12576 | tf_op jit(solution)/shard_map/ppermute | solution.py:11
  3.2 2.8 %collective-permute-start.1 = (f32[16,196]{1,0:T(8,128)S(1)}, f32[16,196]{1,0:T(8,128)S(1)}, u32[]{:S(2)}, u32[]{:S(2)}) collective-permute-start(f32[16,196]{1,0:T(8,128)S(1)} %add.64), channel_id=1, source_target_pairs={{0,2},{2,0},{1,3},{3,1},{4,6},{6,4},{5,7},{7,5},{8,10},{10,8},{9,1... | collective-permute-start | bytes 37640 | tf_op jit(solution)/shard_map/ppermute | solution.py:11
  6.0 1.7 %collective-permute-done.1 = f32[16,196]{1,0:T(8,128)S(1)} collective-permute-done((f32[16,196]{1,0:T(8,128)S(1)}, f32[16,196]{1,0:T(8,128)S(1)}, u32[]{:S(2)}, u32[]{:S(2)}) %collective-permute-start.1) | collective-permute-done | bytes 12576 | tf_op jit(solution)/shard_map/ppermute | solution.py:11
  7.8 0.2 fusion.46
  8.0 1.1 %convolution_convert_fusion.3 = bf16[16,256]{1,0:T(8,128)(2,1)S(1)} fusion(bf16[196,256]{1,0:T(8,128)(2,1)} %param.5, f32[16,196]{1,0:T(8,128)S(1)} %get-tuple-element.9, f32[16]{0:T(128)S(1)} %get-tuple-element.5, f32[16]{0:T(128)S(1)} %get-tuple-element.7), kind=kOutput, calls=%fused_computation.21 | convolution fusion | flops 1619136 | bytes 121216 | tf_op jit(solution)/shard_map/dot_general | solution.py:15
  9.1 1.0 %convolution_convert_fusion.2 = bf16[16,256]{1,0:T(8,128)(2,1)S(1)} fusion(bf16[196,256]{1,0:T(8,128)(2,1)} %param.9, f32[16,196]{1,0:T(8,128)S(1)} %get-tuple-element.9, f32[196]{0:T(256)S(1)} %get-tuple-element.6, f32[196]{0:T(256)S(1)} %get-tuple-element.8), kind=kOutput, calls=%fused_computation.20 | convolution fusion | flops 1619136 | bytes 122656 | tf_op jit(solution)/shard_map/dot_general | solution.py:15
  10.3 13.5 %all_to_all.15 = bf16[32,4,256]{2,1,0:T(4,128)(2,1)S(1)} all-to-all(bf16[32,4,256]{2,1,0:T(4,128)(2,1)S(1)} %bitcast.114), channel_id=1, replica_groups=mesh['expert'=8,'x'=2,'core'=2] {'x','core','expert'}, dimensions={0} | all-to-all | bytes 131072 | tf_op jit(solution)/shard_map/all_to_all | solution.py:56
  23.9 0.4 fusion.6
  24.2 0.4 fusion.12
  24.6 2.8 %fusion.9 = bf16[16,1024]{1,0:T(8,128)(2,1)S(1)} fusion(bf16[1,1024,1024]{2,1,0:T(8,128)(2,1)S(1)} %copy-done, f32[16,1024]{1,0:T(8,128)S(1)} %fusion.6, bf16[16,1024]{1,0:T(8,128)(2,1)S(1)} %bitcast.117, bf16[1,1024,1024]{2,1,0:T(8,128)(2,1)} %param.8), kind=kOutput, calls=%fused_computation.11 | convolution fusion | flops 67452928 | bytes 4325376 | tf_op jit(solution)/shard_map/dot_general | solution.py:15
  27.6 0.2 collective-permute-start.2
  27.8 0.7 %collective-permute-start.3 = (bf16[2,196,256]{2,1,0:T(8,128)(2,1)S(1)}, bf16[2,196,256]{2,1,0:T(8,128)(2,1)S(1)}, u32[]{:S(2)}, u32[]{:S(2)}) collective-permute-start(bf16[2,196,256]{2,1,0:T(8,128)(2,1)S(1)} %get-tuple-element.11), channel_id=1, source_target_pairs={{0,2},{2,0},{1,3},{3,1},{4,6},{6,4},{5,7},{7,5},{8,10},{10,8},{9,1... | collective-permute-start | bytes 602120 | tf_op jit(solution)/shard_map/ppermute | solution.py:11
  28.5 0.4 collective-permute-done.2
  29.0 0.7 %broadcast_in_dim.10 = bf16[2,8,4,1024]{3,2,1,0:T(4,128)(2,1)} broadcast(bf16[8,4,1024]{2,1,0:T(4,128)(2,1)S(1)} %copy.63), dimensions={1,2,3} | broadcast | bytes 196608 | tf_op jit(solution)/shard_map/broadcast_in_dim | solution.py:72
  29.7 3.5 %all-to-all-start.1 = ((bf16[16,4,1024]{2,1,0:T(4,128)(2,1)}), bf16[16,4,1024]{2,1,0:T(4,128)(2,1)S(1)}, u32[]{:S(2)}, u32[]{:S(2)}) async-start(bf16[16,4,1024]{2,1,0:T(4,128)(2,1)} %bitcast.10), calls=%async_computation.1 | async-start | bytes 262144 | tf_op jit(solution)/shard_map/all_to_all | solution.py:73
  33.2 2.0 %collective-permute-done.3 = bf16[2,196,256]{2,1,0:T(8,128)(2,1)S(1)} collective-permute-done((bf16[2,196,256]{2,1,0:T(8,128)(2,1)S(1)}, bf16[2,196,256]{2,1,0:T(8,128)(2,1)S(1)}, u32[]{:S(2)}, u32[]{:S(2)}) %collective-permute-start.3) | collective-permute-done | bytes 200736 | tf_op jit(solution)/shard_map/ppermute | solution.py:11
  35.4 5.8 %all-to-all-done.1 = bf16[16,4,1024]{2,1,0:T(4,128)(2,1)S(1)} async-done(((bf16[16,4,1024]{2,1,0:T(4,128)(2,1)}), bf16[16,4,1024]{2,1,0:T(4,128)(2,1)S(1)}, u32[]{:S(2)}, u32[]{:S(2)}) %all-to-all-start.1) | async-done | bytes 131104 | tf_op jit(solution)/shard_map/all_to_all | solution.py:73
  41.7 0.9 %convolution_convert_fusion = bf16[196,256]{1,0:T(8,128)(2,1)} fusion(bf16[16,1,256]{2,1,0:T(2,128)(2,1)S(1)} %get-tuple-element.25, f32[16,196]{1,0:T(8,128)S(1)} %get-tuple-element.9, f32[196]{0:T(256)S(1)} %get-tuple-element.6, f32[196]{0:T(256)S(1)} %get-tuple-element.8), kind=kOutput, calls=%fused_computation.9 | convolution fusion | flops 1665216 | bytes 122656 | tf_op jit(solution)/shard_map/dot_general | solution.py:15
  42.7 0.3 fusion.61
  43.1 1.0 %fusion.18 = f32[16,196]{1,0:T(8,128)S(1)} fusion(bf16[2,2,196,256]{3,2,1,0:T(8,128)(2,1)} %collective-permute-done.4, bf16[16,1,256]{2,1,0:T(2,128)(2,1)S(1)} %get-tuple-element.27), kind=kOutput, calls=%fused_computation.31 | convolution fusion | flops 1605632 | bytes 123136 | tf_op jit(solution)/shard_map/dot_general | solution.py:15
  44.1 1.1 %fusion.17 = f32[16,196]{1,0:T(8,128)S(1)} fusion(bf16[2,2,196,256]{3,2,1,0:T(8,128)(2,1)} %collective-permute-done.4, bf16[16,1,256]{2,1,0:T(2,128)(2,1)S(1)} %get-tuple-element.21), kind=kOutput, calls=%fused_computation.27 | convolution fusion | flops 1605632 | bytes 123136 | tf_op jit(solution)/shard_map/dot_general | solution.py:15
  45.2 1.1 %convolution_add_fusion.4 = f32[16,196]{1,0:T(8,128)S(1)} fusion(f32[16,196]{1,0:T(8,128)S(1)} %fusion.63, bf16[2,2,196,256]{3,2,1,0:T(8,128)(2,1)} %collective-permute-done.4, bf16[16,1,256]{2,1,0:T(2,128)(2,1)S(1)} %get-tuple-element.26), kind=kOutput, calls=%fused_computation.18 | convolution fusion | flops 1608768 | bytes 135680 | tf_op jit(solution)/shard_map/dot_general | solution.py:15
  46.2 1.1 %convolution_add_fusion.2 = f32[16,196]{1,0:T(8,128)S(1)} fusion(f32[16,196]{1,0:T(8,128)S(1)} %fusion.59, bf16[2,2,196,256]{3,2,1,0:T(8,128)(2,1)} %collective-permute-done.4, bf16[16,1,256]{2,1,0:T(2,128)(2,1)S(1)} %get-tuple-element.22), kind=kOutput, calls=%fused_computation.15 | convolution fusion | flops 1608768 | bytes 135680 | tf_op jit(solution)/shard_map/dot_general | solution.py:15
  47.3 0.2 fusion.15
  47.5 0.2 multiply_reduce_fusion.1
  47.9 0.6 %broadcast_in_dim.11 = bf16[8,16,256]{2,1,0:T(8,128)(2,1)} broadcast(bf16[16,256]{1,0:T(8,128)(2,1)S(1)} %convolution_convert_fusion.1), dimensions={1,2} | broadcast | bytes 73728 | tf_op jit(solution)/shard_map/broadcast_in_dim | solution.py:88
  48.6 3.3 %all-to-all-start.2 = ((bf16[8,16,256]{2,1,0:T(8,128)(2,1)}), bf16[8,16,256]{2,1,0:T(8,128)(2,1)S(1)}, u32[]{:S(2)}, u32[]{:S(2)}) async-start(bf16[8,16,256]{2,1,0:T(8,128)(2,1)} %broadcast_in_dim.11), calls=%async_computation.2 | async-start | bytes 131072 | tf_op jit(solution)/shard_map/all_to_all | solution.py:89
  51.9 0.9 %fusion.8 = bf16[196,256]{1,0:T(8,128)(2,1)} fusion(f32[196,256]{1,0:T(8,128)S(1)} %fusion.61, bf16[16,196]{1,0:T(8,128)(2,1)S(1)} %add_convert_fusion.1, bf16[256,16]{0,1:T(8,128)(2,1)S(1)} %copy-done.4), kind=kOutput, calls=%fused_computation.10 | convolution fusion | flops 1705984 | bytes 315520 | tf_op jit(solution)/shard_map/dot_general | solution.py:15
  52.8 6.0 %all-to-all-done.2 = bf16[8,16,256]{2,1,0:T(8,128)(2,1)S(1)} async-done(((bf16[8,16,256]{2,1,0:T(8,128)(2,1)}), bf16[8,16,256]{2,1,0:T(8,128)(2,1)S(1)}, u32[]{:S(2)}, u32[]{:S(2)}) %all-to-all-start.2) | async-done | bytes 65568 | tf_op jit(solution)/shard_map/all_to_all | solution.py:89
  58.8 0.6 %convert_reduce_fusion = f32[16,256]{1,0:T(8,128)} fusion(bf16[8,16,256]{2,1,0:T(8,128)(2,1)S(1)} %all-to-all-done.2), kind=kLoop, calls=%fused_computation.24 | loop fusion | flops 61440 | bytes 81920 | tf_op jit(solution)/shard_map/reduce_sum | solution.py:90
  (44 shorter events, 1.4 us)
Async XLA Ops:
  0.6 23.2 %copy-start = (bf16[1,1024,1024]{2,1,0:T(8,128)(2,1)S(1)}, bf16[1,1024,1024]{2,1,0:T(8,128)(2,1)}, u32[]{:S(2)}) copy-start(bf16[1,1024,1024]{2,1,0:T(8,128)(2,1)} %param.7) | copy-start | bytes 6291460
  1.8 1.3 %collective-permute-start = (f32[16,196]{1,0:T(8,128)S(1)}, f32[16,196]{1,0:T(8,128)S(1)}, u32[]{:S(2)}, u32[]{:S(2)}) collective-permute-start(f32[16,196]{1,0:T(8,128)S(1)} %fusion.92), channel_id=1, source_target_pairs={{0,1},{1,0},{2,3},{3,2},{4,5},{5,4},{6,7},{7,6},{8,9},{9,8},{10,11... | collective-permute-start | bytes 37640 | tf_op jit(solution)/shard_map/ppermute | solution.py:11
  3.2 4.5 %collective-permute-start.1 = (f32[16,196]{1,0:T(8,128)S(1)}, f32[16,196]{1,0:T(8,128)S(1)}, u32[]{:S(2)}, u32[]{:S(2)}) collective-permute-start(f32[16,196]{1,0:T(8,128)S(1)} %add.64), channel_id=1, source_target_pairs={{0,2},{2,0},{1,3},{3,1},{4,6},{6,4},{5,7},{7,5},{8,10},{10,8},{9,1... | collective-permute-start | bytes 37640 | tf_op jit(solution)/shard_map/ppermute | solution.py:11
  10.2 14.1 %copy-start.1 = (bf16[1,1024,1024]{2,1,0:T(8,128)(2,1)S(1)}, bf16[1,1024,1024]{2,1,0:T(8,128)(2,1)}, u32[]{:S(2)}) copy-start(bf16[1,1024,1024]{2,1,0:T(8,128)(2,1)} %param.8) | copy-start | bytes 6291460
  24.6 3.1 %copy-start.2 = (bf16[196,256]{1,0:T(8,128)(2,1)S(1)}, bf16[196,256]{1,0:T(8,128)(2,1)}, u32[]{:S(2)}) copy-start(bf16[196,256]{1,0:T(8,128)(2,1)} %param.5) | copy-start | bytes 301060
  24.6 3.1 %copy-start.3 = (bf16[196,256]{1,0:T(8,128)(2,1)S(1)}, bf16[196,256]{1,0:T(8,128)(2,1)}, u32[]{:S(2)}) copy-start(bf16[196,256]{1,0:T(8,128)(2,1)} %param.9) | copy-start | bytes 301060
  27.6 1.3 %collective-permute-start.2 = (bf16[8,4,1024]{2,0,1:T(8,128)(2,1)S(1)}, bf16[8,4,1024]{2,0,1:T(8,128)(2,1)S(1)}, u32[]{:S(2)}, u32[]{:S(2)}) collective-permute-start(bf16[8,4,1024]{2,0,1:T(8,128)(2,1)S(1)} %bitcast.113), channel_id=1, source_target_pairs={{0,1},{1,0},{2,3},{3,2},{4,5},{5,4},{6,7},{7,6},{8,9},{9,8},{10,11... | collective-permute-start | bytes 196616 | tf_op jit(solution)/shard_map/ppermute | solution.py:11
  27.8 7.4 %collective-permute-start.3 = (bf16[2,196,256]{2,1,0:T(8,128)(2,1)S(1)}, bf16[2,196,256]{2,1,0:T(8,128)(2,1)S(1)}, u32[]{:S(2)}, u32[]{:S(2)}) collective-permute-start(bf16[2,196,256]{2,1,0:T(8,128)(2,1)S(1)} %get-tuple-element.11), channel_id=1, source_target_pairs={{0,2},{2,0},{1,3},{3,1},{4,6},{6,4},{5,7},{7,5},{8,10},{10,8},{9,1... | collective-permute-start | bytes 602120 | tf_op jit(solution)/shard_map/ppermute | solution.py:11
  29.0 22.9 %copy-start.4 = (bf16[256,16]{0,1:T(8,128)(2,1)S(1)}, bf16[256,16]{0,1:T(8,128)(2,1)}, u32[]{:S(2)}) copy-start(bf16[256,16]{0,1:T(8,128)(2,1)} %param.6) | copy-start | bytes 24580
  29.7 11.5 %all-to-all-start.1 = ((bf16[16,4,1024]{2,1,0:T(4,128)(2,1)}), bf16[16,4,1024]{2,1,0:T(4,128)(2,1)S(1)}, u32[]{:S(2)}, u32[]{:S(2)}) async-start(bf16[16,4,1024]{2,1,0:T(4,128)(2,1)} %bitcast.10), calls=%async_computation.1 | async-start | bytes 262144 | tf_op jit(solution)/shard_map/all_to_all | solution.py:73
  35.3 7.8 %collective-permute-start.4 = (bf16[2,2,196,256]{3,2,1,0:T(8,128)(2,1)S(1)}, bf16[2,2,196,256]{3,2,1,0:T(8,128)(2,1)}, u32[]{:S(2)}, u32[]{:S(2)}) collective-permute-start(bf16[2,2,196,256]{3,2,1,0:T(8,128)(2,1)S(1)} %pad_maximum_fusion), channel_id=1, source_target_pairs={{0,1},{1,0},{2,3},{3,2},{4,5},{5,4},{6,7},{7,6},{8,9},{9,8},{10,11... | collective-permute-start | bytes 1204232 | tf_op jit(solution)/shard_map/ppermute | solution.py:11
  48.6 10.2 %all-to-all-start.2 = ((bf16[8,16,256]{2,1,0:T(8,128)(2,1)}), bf16[8,16,256]{2,1,0:T(8,128)(2,1)S(1)}, u32[]{:S(2)}, u32[]{:S(2)}) async-start(bf16[8,16,256]{2,1,0:T(8,128)(2,1)} %broadcast_in_dim.11), calls=%async_computation.2 | async-start | bytes 131072 | tf_op jit(solution)/shard_map/all_to_all | solution.py:89

commit v2 on v1

v2 whole, which is shorter than its diff:
```python
import functools

import jax
import jax.numpy as jnp
from jax import lax
from jax.experimental import pallas as pl
from jax.experimental.pallas import tpu as pltpu
from jax.sharding import Mesh, PartitionSpec as P

F32 = jnp.float32
BF16 = jnp.bfloat16
MIB = 2**20


def swap(array, axis):
    return lax.ppermute(array, axis, [(0, 1), (1, 0)])


def dot(left, right, over):
    return lax.dot_general(left, right, ((over[:1], over[1:]), ((), ())), preferred_element_type=F32)


def softmax(logits, axis):
    shifted = jnp.exp(logits - jnp.max(logits, axis=axis, keepdims=True))
    return shifted / jnp.sum(shifted, axis=axis, keepdims=True)


def softmax_back(probabilities, upstream, axis):
    inner = jnp.sum(probabilities * upstream, axis=axis, keepdims=True)
    return probabilities * (upstream - inner)


def gelu_parts(value):
    scale, cubic = 0.7978845608028654, 0.044715
    square = value * value
    curve = jnp.tanh(scale * (value + cubic * value * square))
    slope = 0.5 * (1.0 + curve) + 0.5 * value * (1.0 - curve * curve) * scale * (1.0 + 3.0 * cubic * square)
    return 0.5 * value * (1.0 + curve), slope


def inward(table, slots, lead):
    table = table.reshape(-1, slots, table.shape[1]).swapaxes(0, 1)
    table = jnp.concatenate([table[:, lead:], table[:, :lead]], axis=1)
    return table.reshape(-1, table.shape[2])


def outward(table, slots, lead):
    table = table.reshape(slots, -1, table.shape[1])
    lead = table.shape[1] - lead
    table = jnp.concatenate([table[:, lead:], table[:, :lead]], axis=1)
    return table.swapaxes(0, 1).reshape(-1, table.shape[2])


def to_blocks(forward, backward, slots, copies):
    rows = [part for table in (forward, backward) for part in jnp.split(table.astype(F32), slots)]
    blocks = jnp.stack(rows, axis=1).astype(BF16)
    return jnp.concatenate([blocks] * copies, axis=0)


def from_blocks(blocks, slots):
    rows = [blocks[:, i] for i in range(2 * slots)]
    return jnp.concatenate(rows[:slots], axis=0), jnp.concatenate(rows[slots:], axis=0)


def start_kernel(slots, lead, tokens, cotangent, params, own, params_in, logits, params_here, sems):
    copies = [
        pltpu.make_async_copy(source, target, sems.at[i])
        for i, (source, target) in enumerate(((params, params_here), (tokens, own.at[0]), (cotangent, own.at[1])))
    ]
    for copy in copies:
        copy.start()
    copies[0].wait()
    params_in[...] = inward(params_here[...].astype(F32), slots, lead).astype(BF16)
    copies[1].wait()
    logits[...] = dot(params_in[...], own[0], (1, 1))
    copies[2].wait()


def weight_kernel(after, up_matrix, down_matrix, up_here, down_here, sems):
    copies = [
        pltpu.make_async_copy(source, target, sems.at[i])
        for i, (source, target) in enumerate(((up_matrix, up_here), (down_matrix, down_here)))
    ]
    for copy in copies:
        copy.start()
    for copy in copies:
        copy.wait()


def slot_kernel(slots, x_size, first, second, own, beside, blocks, dispatch, combine):
    logits = first[...] + second[...]
    over_tokens, over_columns = softmax(logits, 1), softmax(logits, 0)
    dispatch[...] = over_tokens
    combine[...] = over_columns
    quarter = own.shape[2]
    for part, core in ((own, lax.axis_index("core")), (beside, 1 - lax.axis_index("core"))):
        here = pl.ds(pl.multiple_of(core * quarter, quarter), quarter)
        slot_in = dot(over_tokens.astype(BF16), part[0], (1, 0))
        grad_out = dot(over_columns.astype(BF16), part[1], (1, 0))
        blocks[:, :, here] = to_blocks(slot_in, grad_out, slots, x_size)


def expert_kernel(slots, x_size, blocks, up_matrix, down_matrix, sums):
    got = blocks[...].astype(F32)
    sides = [from_blocks(part, slots) for part in jnp.split(got, x_size)]
    forward, backward = (jnp.concatenate(side, axis=1).astype(BF16) for side in zip(*sides))
    preact = dot(forward, up_matrix[0], (1, 0))
    grad_hidden = dot(backward, down_matrix[0], (1, 1))
    hidden, slope = gelu_parts(preact)
    sums[0] = dot(hidden.astype(BF16), down_matrix[0], (1, 0)).astype(BF16)
    sums[1] = dot((grad_hidden * slope).astype(BF16), up_matrix[0], (1, 1)).astype(BF16)


def pair_kernel(slots, x_size, first, second, blocks):
    total = first[...].astype(F32) + second[...].astype(F32)
    blocks[...] = to_blocks(total[0], total[1], slots, x_size)


def image_kernel(
    slots, x_size, lead, blocks, own, beside, across, corner, dispatch, combine, params, params_part, mixed, grad_tokens, rows
):
    half = lax.axis_index("x") * 2 + lax.axis_index("core")
    quarter = own.shape[2]
    slot_out, grad_in = from_blocks(sum(jnp.split(blocks[...].astype(F32), x_size)), slots)
    rows[0] = slot_out.astype(BF16)
    rows[1] = grad_in.astype(BF16)
    grad_combine = grad_dispatch = 0.0
    for offset, part in enumerate((own, beside, across, corner)):
        start = pl.multiple_of(jnp.bitwise_xor(half, offset) * quarter, quarter)
        grad_combine += dot(rows[0, :, pl.ds(start, quarter)], part[1], (1, 1))
        grad_dispatch += dot(rows[1, :, pl.ds(start, quarter)], part[0], (1, 1))
    grad_logits = softmax_back(combine[...], grad_combine, 0) + softmax_back(dispatch[...], grad_dispatch, 1)
    partial = dot(grad_logits.astype(BF16), own[0], (1, 0))
    partial = outward(partial, slots, lead).astype(BF16)
    params_part[...] = jnp.broadcast_to(partial[None], params_part.shape)
    here = pl.ds(pl.multiple_of(half * quarter, quarter), quarter)
    mixed[...] = dot(combine[...].astype(BF16), rows[0, :, here], (0, 0)).astype(BF16)
    token_term = dot(dispatch[...].astype(BF16), rows[1, :, here], (0, 0))
    grad_tokens[...] = (token_term + dot(grad_logits.astype(BF16), params[...], (0, 0))).astype(BF16)


def end_kernel(parts, mixed_here, grad_tokens_here, mixed, grad_tokens, grad_params):
    mixed[...] = mixed_here[...]
    grad_tokens[...] = grad_tokens_here[...]
    grad_params[...] = jnp.sum(parts[...].astype(F32), axis=0)


def call(kernel, outs, *args, scratch=(), in_hbm=(), limit=16):
    whole = pl.BlockSpec(memory_space=pltpu.VMEM)
    elsewhere = pl.BlockSpec(memory_space=pltpu.HBM)
    run = pl.pallas_call(
        kernel,
        out_shape=[jax.ShapeDtypeStruct(*out) if isinstance(out, tuple) else out for out in outs],
        in_specs=[elsewhere if i in in_hbm else whole for i in range(len(args))],
        out_specs=[whole] * len(outs),
        scratch_shapes=list(scratch),
        compiler_params=pltpu.CompilerParams(vmem_limit_bytes=limit * MIB),
    )
    return run(*(pltpu.with_memory_space_constraint(arg, pltpu.HBM) if i in in_hbm else arg for i, arg in enumerate(args)))


def local(experts, halves, tokens, slot_params, w_up, w_down, cotangent):
    seq, quarter = tokens.shape
    columns = slot_params.shape[1]
    slots = columns // experts
    x_size = halves // 2
    width = halves * quarter
    table = (columns, seq)
    lead = experts * 5 // 8
    order = [(lead + i) % experts for i in range(experts)]
    wide_order = [expert * x_size + x for x in range(x_size) for expert in order]

    own, params, logits = call(
        functools.partial(start_kernel, slots, lead),
        [((2, seq, quarter), BF16), ((columns, quarter), BF16), (table, F32)],
        tokens,
        cotangent,
        slot_params.T,
        scratch=[pltpu.VMEM((columns, quarter), BF16), pltpu.SemaphoreType.DMA((3,))],
        in_hbm=(0, 1, 2),
    )
    logits = logits + swap(logits, "core")
    other = swap(logits, "x")
    across = swap(own, "x")
    beside = swap(own, "core")
    up_here, down_here = call(
        weight_kernel,
        [pltpu.VMEM(w_up.shape, BF16), pltpu.VMEM(w_down.shape, BF16)],
        logits,
        w_up,
        w_down,
        scratch=[pltpu.SemaphoreType.DMA((2,))],
        in_hbm=(1, 2),
    )
    logits, up_here, down_here = lax.optimization_barrier((logits, up_here, down_here))
    blocks, dispatch, combine = call(
        functools.partial(slot_kernel, slots, x_size),
        [((x_size * experts, 2 * slots, 2 * quarter), BF16), (table, F32), (table, F32)],
        logits,
        other,
        own,
        beside,
    )

    blocks = lax.all_to_all(blocks, ("expert", "x"), 0, 0, tiled=True, axis_index_groups=[wide_order])
    (sums,) = call(
        functools.partial(expert_kernel, slots, x_size), [((2, columns, width), BF16)], blocks, up_here, down_here
    )

    sums, across = lax.optimization_barrier((sums, across))
    other_sums = swap(sums, "core")
    corner = swap(across, "core")
    (blocks,) = call(
        functools.partial(pair_kernel, slots, x_size),
        [((x_size * experts, 2 * slots, width), BF16)],
        sums,
        other_sums,
    )
    blocks, corner = lax.optimization_barrier((blocks, corner))
    blocks = lax.all_to_all(blocks, ("expert", "x"), 0, 0, tiled=True, axis_index_groups=[wide_order])
    params_part, mixed, grad_tokens = call(
        functools.partial(image_kernel, slots, x_size, lead),
        [((experts, columns, quarter), BF16), pltpu.VMEM((seq, quarter), BF16), pltpu.VMEM((seq, quarter), BF16)],
        blocks,
        own,
        beside,
        across,
        corner,
        dispatch,
        combine,
        params,
        scratch=[pltpu.VMEM((2, columns, width), BF16)],
        limit=16 if experts * columns <= 1024 else 48,
    )

    params_parts = lax.all_to_all(params_part, "expert", 0, 0, tiled=True, axis_index_groups=[order])
    mixed, grad_tokens, grad_params = call(
        end_kernel,
        [((seq, quarter), BF16), ((seq, quarter), BF16), ((columns, quarter), F32)],
        params_parts,
        mixed,
        grad_tokens,
        limit=16 if experts * columns <= 1024 else 48,
    )
    return mixed, grad_tokens, grad_params.T


def solution(mesh):
    experts, halves = mesh.shape["expert"], mesh.shape["half"]
    split = Mesh(mesh.devices.reshape(experts, halves // 2, 2), ("expert", "x", "core"))
    half = ("x", "core")
    in_specs = (
        P("expert", half),
        P(half, None),
        P("expert", None, half),
        P("expert", half, None),
        P("expert", half),
    )
    out_specs = (P("expert", half), P("expert", half), P(half, None))

    def program(*args):
        return jax.shard_map(
            lambda *blocks: local(experts, halves, *blocks),
            mesh=split,
            in_specs=in_specs,
            out_specs=out_specs,
            check_vma=False,
        )(*args)

    return program
```

time: 59.9 us -> 46.9 us (0.78)
  blocking collectives: 13.5 us -> 30.5 us
  matrix products: 14 us -> 0 us
  waiting for transfers between devices: 16.8 us -> 4.43 us
  starting transfers between devices: 11.1 us -> 3.98 us
  Pallas kernels: 0 us -> 6.93 us
  local copies, waits for them, and re-layouts: 1.83 us -> 0 us
  other arithmetic: 1.21 us -> 0.01 us
    all_to_all x1 -> x3, blocking collectives: 13.5 us -> 30.5 us  [the longest x2 22 us: local(): lax.all_to_all(blocks, ('expert', 'x'), 0, 0, tiled=True, axis_index_grou...]
    dot_general x18 -> x0, matrix products: 14 us -> none  [dot(): lax.dot_general(left, right, ((over[:1], over[1:]), ((), ())), preferred_...]
    all_to_all x2 -> x0, waiting for transfers between devices: 11.8 us -> none  [the longest x1 5.97 us: local(): params_parts = lax.all_to_all(params_part, 'expert', 0, 0, tiled=True)]
    pallas_call x0 -> x7, Pallas kernels: none -> 6.93 us  [call(): run(*(pltpu.with_memory_space_constraint(arg, pltpu.HBM) if i in in_hbm e...]
    all_to_all x2 -> x0, starting transfers between devices: 6.86 us -> none  [the longest x1 3.51 us: local(): back = lax.all_to_all(pair, ('x', 'expert'), 0, 0, tiled=True)]
    broadcast_in_dim x4 -> x0, local copies, waits for them, and re-layouts: 1.34 us -> none  [the longest x1 0.68 us: local(): jnp.broadcast_to(pair[None], (x_size,) + pair.shape)]
    reduce_sum x3 -> x0, other arithmetic: 0.89 us -> none  [the longest x1 0.62 us: local(): grad_params = params_parts.astype(F32).sum(0).T]
    ppermute x5 -> x6, waiting for transfers between devices: 5 us -> 4.43 us  [swap(): return lax.ppermute(array, axis, [(0, 1), (1, 0)])]
  transfers between devices with their start and end apart: 7 -> 6, of which waited for: 6 -> 3; matrix products, arithmetic and copies ran while one was open for 6% -> 0% of each run, Pallas kernels for 0% -> 10%
where the time goes in v2:
time: 46.9 us; the launch traced here: 46.6 us
  blocking collectives  30.5 us (65%)
  Pallas kernels  6.93 us (15%)
  waiting for transfers between devices  4.43 us (9%)
  starting transfers between devices  3.98 us (8%)
  between operations  0.69 us (1%)
    all_to_all x2, blocking collectives, local(): lax.all_to_all(blocks, ('expert', 'x'), 0, 0, tiled=True, axis_index_grou...  22 us
    all_to_all x1, blocking collectives, local(): lax.all_to_all(params_part, 'expert', 0, 0, tiled=True, axis_index_groups...  8.54 us
    pallas_call x7, Pallas kernels, call(): run(*(pltpu.with_memory_space_constraint(arg, pltpu.HBM) if i in in_hbm e...  6.93 us
    ppermute x6, waiting for transfers between devices, swap(): return lax.ppermute(array, axis, [(0, 1), (1, 0)])  4.43 us
    ppermute x6, starting transfers between devices, swap(): return lax.ppermute(array, axis, [(0, 1), (1, 0)])  3.98 us
  transfers between devices with their start and end apart: 6, of which 3 were waited for; matrix products, arithmetic and copies ran while one was open for 0% of the time, Pallas kernels for 10%

profile of v2, /device:TPU:0, one launch (start us, length us, event | category | flops | bytes accessed | tf_op | source)
XLA Modules:
  0.0 46.6 jit_solution(4424610433782749111)
XLA Ops:
  0.6 1.1 %shard_map.76 = (bf16[2,196,256]{2,1,0:T(8,128)(2,1)S(1)}, bf16[16,256]{1,0:T(8,128)(2,1)S(1)}, f32[16,196]{1,0:T(8,128)S(1)}) custom-call(bf16[196,256]{1,0:T(8,128)(2,1)} %tokens.1, bf16[196,256]{1,0:T(8,128)(2,1)} %cotangent.1, bf16[16,256]{1,0:T(8,128)(2,1)} %bitcast.2), custom_call_target="tpu_custom_call" | custom-call | tf_op jit(solution)/shard_map/pallas_call | solution.py:159
  1.7 0.5 %collective-permute-start.2 = (bf16[2,196,256]{2,1,0:T(8,128)(2,1)S(1)}, bf16[2,196,256]{2,1,0:T(8,128)(2,1)S(1)}, u32[]{:S(2)}, u32[]{:S(2)}) collective-permute-start(bf16[2,196,256]{2,1,0:T(8,128)(2,1)S(1)} %get-tuple-element.28.own), channel_id=1, source_target_pairs={{0,1},{1,0},{2,3},{3,2},{4,5},{5,4},{6,7},{7,6},{8,9},{9,8},{10,11... | collective-permute-start | bytes 602120 | tf_op jit(solution)/shard_map/ppermute | solution.py:16
  2.3 2.6 %collective-permute-start.3 = (bf16[2,196,256]{2,1,0:T(8,128)(2,1)S(1)}, bf16[2,196,256]{2,1,0:T(8,128)(2,1)S(1)}, u32[]{:S(2)}, u32[]{:S(2)}) collective-permute-start(bf16[2,196,256]{2,1,0:T(8,128)(2,1)S(1)} %get-tuple-element.28.own), channel_id=1, source_target_pairs={{0,2},{2,0},{1,3},{3,1},{4,6},{6,4},{5,7},{7,5},{8,10},{10,8},{9,1... | collective-permute-start | bytes 602120 | tf_op jit(solution)/shard_map/ppermute | solution.py:16
  4.8 0.2 collective-permute-start
  5.0 1.0 %collective-permute-done = f32[16,196]{1,0:T(8,128)S(1)} collective-permute-done((f32[16,196]{1,0:T(8,128)S(1)}, f32[16,196]{1,0:T(8,128)S(1)}, u32[]{:S(2)}, u32[]{:S(2)}) %collective-permute-start) | collective-permute-done | bytes 12576 | tf_op jit(solution)/shard_map/ppermute | solution.py:16
  6.0 0.2 collective-permute-start.1
  6.2 2.2 %shard_map.77 = (bf16[1,1024,1024]{2,1,0:T(8,128)(2,1)S(1)}, bf16[1,1024,1024]{2,1,0:T(8,128)(2,1)S(1)}) custom-call(f32[16,196]{1,0:T(8,128)S(1)} %add.3.after.first, bf16[1,1024,1024]{2,1,0:T(8,128)(2,1)} %up_matrix.1, bf16[1,1024,1024]{2,1,0:T(8,128)(2,1)} %down_matrix.1), custom_call_target="tpu_custom_call" | custom-call | tf_op jit(solution)/shard_map/pallas_call | solution.py:159
  8.5 2.4 %collective-permute-done.1.second = f32[16,196]{1,0:T(8,128)S(1)} collective-permute-done((f32[16,196]{1,0:T(8,128)S(1)}, f32[16,196]{1,0:T(8,128)S(1)}, u32[]{:S(2)}, u32[]{:S(2)}) %collective-permute-start.1) | collective-permute-done | bytes 12576 | tf_op jit(solution)/shard_map/ppermute | solution.py:16
  10.9 0.0 collective-permute-done.2.beside
  10.9 0.3 shard_map.78
  11.2 11.9 %all_to_all.15.blocks = bf16[16,4,512]{2,1,0:T(4,128)(2,1)S(1)} all-to-all(bf16[16,4,512]{2,1,0:T(4,128)(2,1)S(1)} %get-tuple-element.29), channel_id=1, replica_groups={{20,24,28,0,4,8,12,16,22,26,30,2,6,10,14,18},{21,25,29,1,5,9,13,17,23,2..., dimensions={0} | all-to-all | bytes 131072 | tf_op jit(solution)/shard_map/all_to_all | solution.py:205
  23.1 1.7 %shard_map.79.first = bf16[2,16,1024]{2,1,0:T(8,128)(2,1)S(1)} custom-call(bf16[16,4,512]{2,1,0:T(4,128)(2,1)S(1)} %all_to_all.15.blocks, bf16[1,1024,1024]{2,1,0:T(8,128)(2,1)S(1)} %get-tuple-element.30.up_matrix, bf16[1,1024,1024]{2,1,0:T(8,128)(2,1)S(1)} %get-tuple-element.31.down_matrix), custom_call_target="tpu_custom_call" | custom-call | tf_op jit(solution)/shard_map/pallas_call | solution.py:159
  24.8 0.0 collective-permute-done.3.across
  24.8 0.0 collective-permute-start.5
  24.9 0.5 %collective-permute-start.4 = (bf16[2,16,1024]{2,1,0:T(8,128)(2,1)S(1)}, bf16[2,16,1024]{2,1,0:T(8,128)(2,1)S(1)}, u32[]{:S(2)}, u32[]{:S(2)}) collective-permute-start(bf16[2,16,1024]{2,1,0:T(8,128)(2,1)S(1)} %shard_map.79.first), channel_id=1, source_target_pairs={{0,1},{1,0},{2,3},{3,2},{4,5},{5,4},{6,7},{7,6},{8,9},{9,8},{10,11... | collective-permute-start | bytes 196616 | tf_op jit(solution)/shard_map/ppermute | solution.py:16
  25.4 1.0 %collective-permute-done.4.second = bf16[2,16,1024]{2,1,0:T(8,128)(2,1)S(1)} collective-permute-done((bf16[2,16,1024]{2,1,0:T(8,128)(2,1)S(1)}, bf16[2,16,1024]{2,1,0:T(8,128)(2,1)S(1)}, u32[]{:S(2)}, u32[]{:S(2)}) %collective-permute-start.4) | collective-permute-done | bytes 65568 | tf_op jit(solution)/shard_map/ppermute | solution.py:16
  26.4 0.1 shard_map.80
  26.5 0.0 collective-permute-done.5.corner
  26.5 10.1 %all_to_all.16.blocks = bf16[16,4,1024]{2,1,0:T(4,128)(2,1)S(1)} all-to-all(bf16[16,4,1024]{2,1,0:T(4,128)(2,1)S(1)} %shard_map.80), channel_id=1, replica_groups={{20,24,28,0,4,8,12,16,22,26,30,2,6,10,14,18},{21,25,29,1,5,9,13,17,23,2..., dimensions={0} | all-to-all | bytes 262144 | tf_op jit(solution)/shard_map/all_to_all | solution.py:220
  36.6 0.7 %shard_map.81 = (bf16[8,16,256]{2,1,0:T(8,128)(2,1)S(1)}, bf16[196,256]{1,0:T(8,128)(2,1)S(1)}, bf16[196,256]{1,0:T(8,128)(2,1)S(1)}) custom-call(bf16[16,4,1024]{2,1,0:T(4,128)(2,1)S(1)} %all_to_all.16.blocks, bf16[2,196,256]{2,1,0:T(8,128)(2,1)S(1)} %get-tuple-element.28.own, bf16[2,196,256]{2,1,0:T(8,128)(2,1)S(1)} %collective-permute-done.2.beside, ...), custom_call_target="tpu_custom_call" | custom-call | tf_op jit(solution)/shard_map/pallas_call | solution.py:159
  37.3 8.5 %all_to_all.17.parts = bf16[8,16,256]{2,1,0:T(8,128)(2,1)S(1)} all-to-all(bf16[8,16,256]{2,1,0:T(8,128)(2,1)S(1)} %get-tuple-element.39), channel_id=1, replica_groups={{20,24,28,0,4,8,12,16},{21,25,29,1,5,9,13,17},{22,26,30,2,6,10,14,18},{..., dimensions={0} | all-to-all | bytes 131072 | tf_op jit(solution)/shard_map/all_to_all | solution.py:236
  45.9 0.7 %shard_map.82 = (bf16[196,256]{1,0:T(8,128)(2,1)}, bf16[196,256]{1,0:T(8,128)(2,1)}, f32[16,256]{1,0:T(8,128)}) custom-call(bf16[8,16,256]{2,1,0:T(8,128)(2,1)S(1)} %all_to_all.17.parts, bf16[196,256]{1,0:T(8,128)(2,1)S(1)} %get-tuple-element.40.mixed_here, bf16[196,256]{1,0:T(8,128)(2,1)S(1)} %get-tuple-element.41.grad_tokens_here), custom_call_target="tpu_custom_call" | custom-call | tf_op jit(solution)/shard_map/pallas_call | solution.py:159
  (1 shorter events, 0.0 us)
Async XLA Ops:
  1.7 9.1 %collective-permute-start.2 = (bf16[2,196,256]{2,1,0:T(8,128)(2,1)S(1)}, bf16[2,196,256]{2,1,0:T(8,128)(2,1)S(1)}, u32[]{:S(2)}, u32[]{:S(2)}) collective-permute-start(bf16[2,196,256]{2,1,0:T(8,128)(2,1)S(1)} %get-tuple-element.28.own), channel_id=1, source_target_pairs={{0,1},{1,0},{2,3},{3,2},{4,5},{5,4},{6,7},{7,6},{8,9},{9,8},{10,11... | collective-permute-start | bytes 602120 | tf_op jit(solution)/shard_map/ppermute | solution.py:16
  2.3 22.6 %collective-permute-start.3 = (bf16[2,196,256]{2,1,0:T(8,128)(2,1)S(1)}, bf16[2,196,256]{2,1,0:T(8,128)(2,1)S(1)}, u32[]{:S(2)}, u32[]{:S(2)}) collective-permute-start(bf16[2,196,256]{2,1,0:T(8,128)(2,1)S(1)} %get-tuple-element.28.own), channel_id=1, source_target_pairs={{0,2},{2,0},{1,3},{3,1},{4,6},{6,4},{5,7},{7,5},{8,10},{10,8},{9,1... | collective-permute-start | bytes 602120 | tf_op jit(solution)/shard_map/ppermute | solution.py:16
  4.8 1.2 %collective-permute-start = (f32[16,196]{1,0:T(8,128)S(1)}, f32[16,196]{1,0:T(8,128)S(1)}, u32[]{:S(2)}, u32[]{:S(2)}) collective-permute-start(f32[16,196]{1,0:T(8,128)S(1)} %get-tuple-element.24), channel_id=1, source_target_pairs={{0,1},{1,0},{2,3},{3,2},{4,5},{5,4},{6,7},{7,6},{8,9},{9,8},{10,11... | collective-permute-start | bytes 37640 | tf_op jit(solution)/shard_map/ppermute | solution.py:16
  6.0 4.8 %collective-permute-start.1 = (f32[16,196]{1,0:T(8,128)S(1)}, f32[16,196]{1,0:T(8,128)S(1)}, u32[]{:S(2)}, u32[]{:S(2)}) collective-permute-start(f32[16,196]{1,0:T(8,128)S(1)} %add.3.after.first), channel_id=1, source_target_pairs={{0,2},{2,0},{1,3},{3,1},{4,6},{6,4},{5,7},{7,5},{8,10},{10,8},{9,1... | collective-permute-start | bytes 37640 | tf_op jit(solution)/shard_map/ppermute | solution.py:16
  24.8 1.7 %collective-permute-start.5 = (bf16[2,196,256]{2,1,0:T(8,128)(2,1)S(1)}, bf16[2,196,256]{2,1,0:T(8,128)(2,1)S(1)}, u32[]{:S(2)}, u32[]{:S(2)}) collective-permute-start(bf16[2,196,256]{2,1,0:T(8,128)(2,1)S(1)} %collective-permute-done.3.across), channel_id=1, source_target_pairs={{0,1},{1,0},{2,3},{3,2},{4,5},{5,4},{6,7},{7,6},{8,9},{9,8},{10,11... | collective-permute-start | bytes 602120 | tf_op jit(solution)/shard_map/ppermute | solution.py:16
  24.9 1.5 %collective-permute-start.4 = (bf16[2,16,1024]{2,1,0:T(8,128)(2,1)S(1)}, bf16[2,16,1024]{2,1,0:T(8,128)(2,1)S(1)}, u32[]{:S(2)}, u32[]{:S(2)}) collective-permute-start(bf16[2,16,1024]{2,1,0:T(8,128)(2,1)S(1)} %shard_map.79.first), channel_id=1, source_target_pairs={{0,1},{1,0},{2,3},{3,2},{4,5},{5,4},{6,7},{7,6},{8,9},{9,8},{10,11... | collective-permute-start | bytes 196616 | tf_op jit(solution)/shard_map/ppermute | solution.py:16

commit v3 on v2

--- a/solution.py
+++ b/solution.py
@@ -179,9 +179,7 @@
         scratch=[pltpu.VMEM((columns, quarter), BF16), pltpu.SemaphoreType.DMA((3,))],
         in_hbm=(0, 1, 2),
     )
-    logits = logits + swap(logits, "core")
     other = swap(logits, "x")
-    across = swap(own, "x")
     beside = swap(own, "core")
     up_here, down_here = call(
         weight_kernel,
@@ -192,7 +190,10 @@
         scratch=[pltpu.SemaphoreType.DMA((2,))],
         in_hbm=(1, 2),
     )
-    logits, up_here, down_here = lax.optimization_barrier((logits, up_here, down_here))
+    logits, up_here, down_here = lax.optimization_barrier((logits + other, up_here, down_here))
+    logits, own_later = lax.optimization_barrier((logits, own))
+    across = swap(own_later, "x")
+    other = swap(logits, "core")
     blocks, dispatch, combine = call(
         functools.partial(slot_kernel, slots, x_size),
         [((x_size * experts, 2 * slots, 2 * quarter), BF16), (table, F32), (table, F32)],

time: 46.9 us -> 44.6 us (0.951)
  waiting for transfers between devices: 4.43 us -> 2.23 us
  blocking collectives: 30.5 us -> 29.4 us
  starting transfers between devices: 3.98 us -> 5.08 us
    ppermute x6, waiting for transfers between devices: 4.43 us -> 2.23 us  [swap(): return lax.ppermute(array, axis, [(0, 1), (1, 0)])]
    all_to_all x2, blocking collectives: 22 us -> 20.8 us  [local(): lax.all_to_all(blocks, ('expert', 'x'), 0, 0, tiled=True, axis_index_grou...]
    ppermute x6, starting transfers between devices: 3.98 us -> 5.08 us  [swap(): return lax.ppermute(array, axis, [(0, 1), (1, 0)])]
  transfers between devices with their start and end apart: 6 -> 6, of which waited for: 3 -> 2; matrix products, arithmetic and copies ran while one was open for 0% -> 0% of each run, Pallas kernels for 10% -> 10%
where the time goes in v3:
time: 44.6 us; the launch traced here: 44.3 us
  blocking collectives  29.4 us (66%)
  Pallas kernels  6.93 us (16%)
  starting transfers between devices  5.08 us (11%)
  waiting for transfers between devices  2.23 us (5%)
  between operations  0.7 us (2%)
    all_to_all x2, blocking collectives, local(): lax.all_to_all(blocks, ('expert', 'x'), 0, 0, tiled=True, axis_index_grou...  20.8 us
    all_to_all x1, blocking collectives, local(): lax.all_to_all(params_part, 'expert', 0, 0, tiled=True, axis_index_groups...  8.54 us
    pallas_call x7, Pallas kernels, call(): run(*(pltpu.with_memory_space_constraint(arg, pltpu.HBM) if i in in_hbm e...  6.93 us
    ppermute x6, starting transfers between devices, swap(): return lax.ppermute(array, axis, [(0, 1), (1, 0)])  5.08 us
    ppermute x6, waiting for transfers between devices, swap(): return lax.ppermute(array, axis, [(0, 1), (1, 0)])  2.23 us
  transfers between devices with their start and end apart: 6, of which 2 were waited for; matrix products, arithmetic and copies ran while one was open for 0% of the time, Pallas kernels for 10%

profile of v3, /device:TPU:0, one launch (start us, length us, event | category | flops | bytes accessed | tf_op | source)
XLA Modules:
  0.0 44.3 jit_solution(1872383397719512301)
XLA Ops:
  0.6 1.1 %shard_map.76 = (bf16[2,196,256]{2,1,0:T(8,128)(2,1)S(1)}, bf16[16,256]{1,0:T(8,128)(2,1)S(1)}, f32[16,196]{1,0:T(8,128)S(1)}) custom-call(bf16[196,256]{1,0:T(8,128)(2,1)} %tokens.1, bf16[196,256]{1,0:T(8,128)(2,1)} %cotangent.1, bf16[16,256]{1,0:T(8,128)(2,1)} %bitcast.2), custom_call_target="tpu_custom_call" | custom-call | tf_op jit(solution)/shard_map/pallas_call | solution.py:159
  1.7 0.5 %collective-permute-start.2 = (bf16[2,196,256]{2,1,0:T(8,128)(2,1)S(1)}, bf16[2,196,256]{2,1,0:T(8,128)(2,1)S(1)}, u32[]{:S(2)}, u32[]{:S(2)}) collective-permute-start(bf16[2,196,256]{2,1,0:T(8,128)(2,1)S(1)} %get-tuple-element.35.own), channel_id=1, source_target_pairs={{0,1},{1,0},{2,3},{3,2},{4,5},{5,4},{6,7},{7,6},{8,9},{9,8},{10,11... | collective-permute-start | bytes 602120 | tf_op jit(solution)/shard_map/ppermute | solution.py:16
  2.3 2.6 %collective-permute-start = (f32[16,196]{1,0:T(8,128)S(1)}, f32[16,196]{1,0:T(8,128)S(1)}, u32[]{:S(2)}, u32[]{:S(2)}) collective-permute-start(f32[16,196]{1,0:T(8,128)S(1)} %get-tuple-element.26.after), channel_id=1, source_target_pairs={{0,2},{2,0},{1,3},{3,1},{4,6},{6,4},{5,7},{7,5},{8,10},{10,8},{9,1... | collective-permute-start | bytes 37640 | tf_op jit(solution)/shard_map/ppermute | solution.py:16
  4.8 2.2 %shard_map.77 = (bf16[1,1024,1024]{2,1,0:T(8,128)(2,1)S(1)}, bf16[1,1024,1024]{2,1,0:T(8,128)(2,1)S(1)}) custom-call(f32[16,196]{1,0:T(8,128)S(1)} %get-tuple-element.26.after, bf16[1,1024,1024]{2,1,0:T(8,128)(2,1)} %up_matrix.1, bf16[1,1024,1024]{2,1,0:T(8,128)(2,1)} %down_matrix.1), custom_call_target="tpu_custom_call" | custom-call | tf_op jit(solution)/shard_map/pallas_call | solution.py:159
  7.1 0.0 collective-permute-done
  7.1 1.5 %collective-permute-start.3 = (bf16[2,196,256]{2,1,0:T(8,128)(2,1)S(1)}, bf16[2,196,256]{2,1,0:T(8,128)(2,1)S(1)}, u32[]{:S(2)}, u32[]{:S(2)}) collective-permute-start(bf16[2,196,256]{2,1,0:T(8,128)(2,1)S(1)} %get-tuple-element.35.own), channel_id=1, source_target_pairs={{0,2},{2,0},{1,3},{3,1},{4,6},{6,4},{5,7},{7,5},{8,10},{10,8},{9,1... | collective-permute-start | bytes 602120 | tf_op jit(solution)/shard_map/ppermute | solution.py:16
  8.6 0.0 collective-permute-start.1
  8.6 1.2 %collective-permute-done.1.second = f32[16,196]{1,0:T(8,128)S(1)} collective-permute-done((f32[16,196]{1,0:T(8,128)S(1)}, f32[16,196]{1,0:T(8,128)S(1)}, u32[]{:S(2)}, u32[]{:S(2)}) %collective-permute-start.1) | collective-permute-done | bytes 12576 | tf_op jit(solution)/shard_map/ppermute | solution.py:16
  9.8 0.0 collective-permute-done.2.beside
  9.8 0.3 shard_map.78
  10.1 10.8 %all_to_all.15.blocks = bf16[16,4,512]{2,1,0:T(4,128)(2,1)S(1)} all-to-all(bf16[16,4,512]{2,1,0:T(4,128)(2,1)S(1)} %get-tuple-element.32), channel_id=1, replica_groups={{20,24,28,0,4,8,12,16,22,26,30,2,6,10,14,18},{21,25,29,1,5,9,13,17,23,2..., dimensions={0} | all-to-all | bytes 131072 | tf_op jit(solution)/shard_map/all_to_all | solution.py:206
  20.9 1.7 %shard_map.79.first = bf16[2,16,1024]{2,1,0:T(8,128)(2,1)S(1)} custom-call(bf16[16,4,512]{2,1,0:T(4,128)(2,1)S(1)} %all_to_all.15.blocks, bf16[1,1024,1024]{2,1,0:T(8,128)(2,1)S(1)} %get-tuple-element.33.up_matrix, bf16[1,1024,1024]{2,1,0:T(8,128)(2,1)S(1)} %get-tuple-element.34.down_matrix), custom_call_target="tpu_custom_call" | custom-call | tf_op jit(solution)/shard_map/pallas_call | solution.py:159
  22.6 0.0 collective-permute-done.3.across
  22.6 0.0 collective-permute-start.5
  22.6 0.5 %collective-permute-start.4 = (bf16[2,16,1024]{2,1,0:T(8,128)(2,1)S(1)}, bf16[2,16,1024]{2,1,0:T(8,128)(2,1)S(1)}, u32[]{:S(2)}, u32[]{:S(2)}) collective-permute-start(bf16[2,16,1024]{2,1,0:T(8,128)(2,1)S(1)} %shard_map.79.first), channel_id=1, source_target_pairs={{0,1},{1,0},{2,3},{3,2},{4,5},{5,4},{6,7},{7,6},{8,9},{9,8},{10,11... | collective-permute-start | bytes 196616 | tf_op jit(solution)/shard_map/ppermute | solution.py:16
  23.1 1.0 %collective-permute-done.4.second = bf16[2,16,1024]{2,1,0:T(8,128)(2,1)S(1)} collective-permute-done((bf16[2,16,1024]{2,1,0:T(8,128)(2,1)S(1)}, bf16[2,16,1024]{2,1,0:T(8,128)(2,1)S(1)}, u32[]{:S(2)}, u32[]{:S(2)}) %collective-permute-start.4) | collective-permute-done | bytes 65568 | tf_op jit(solution)/shard_map/ppermute | solution.py:16
  24.2 0.1 shard_map.80
  24.3 0.0 collective-permute-done.5.corner
  24.3 10.1 %all_to_all.16.blocks = bf16[16,4,1024]{2,1,0:T(4,128)(2,1)S(1)} all-to-all(bf16[16,4,1024]{2,1,0:T(4,128)(2,1)S(1)} %shard_map.80), channel_id=1, replica_groups={{20,24,28,0,4,8,12,16,22,26,30,2,6,10,14,18},{21,25,29,1,5,9,13,17,23,2..., dimensions={0} | all-to-all | bytes 262144 | tf_op jit(solution)/shard_map/all_to_all | solution.py:221
  34.4 0.7 %shard_map.81 = (bf16[8,16,256]{2,1,0:T(8,128)(2,1)S(1)}, bf16[196,256]{1,0:T(8,128)(2,1)S(1)}, bf16[196,256]{1,0:T(8,128)(2,1)S(1)}) custom-call(bf16[16,4,1024]{2,1,0:T(4,128)(2,1)S(1)} %all_to_all.16.blocks, bf16[2,196,256]{2,1,0:T(8,128)(2,1)S(1)} %get-tuple-element.35.own, bf16[2,196,256]{2,1,0:T(8,128)(2,1)S(1)} %collective-permute-done.2.beside, ...), custom_call_target="tpu_custom_call" | custom-call | tf_op jit(solution)/shard_map/pallas_call | solution.py:159
  35.1 8.5 %all_to_all.17.parts = bf16[8,16,256]{2,1,0:T(8,128)(2,1)S(1)} all-to-all(bf16[8,16,256]{2,1,0:T(8,128)(2,1)S(1)} %get-tuple-element.43), channel_id=1, replica_groups={{20,24,28,0,4,8,12,16},{21,25,29,1,5,9,13,17},{22,26,30,2,6,10,14,18},{..., dimensions={0} | all-to-all | bytes 131072 | tf_op jit(solution)/shard_map/all_to_all | solution.py:237
  43.6 0.7 %shard_map.82 = (bf16[196,256]{1,0:T(8,128)(2,1)}, bf16[196,256]{1,0:T(8,128)(2,1)}, f32[16,256]{1,0:T(8,128)}) custom-call(bf16[8,16,256]{2,1,0:T(8,128)(2,1)S(1)} %all_to_all.17.parts, bf16[196,256]{1,0:T(8,128)(2,1)S(1)} %get-tuple-element.44.mixed_here, bf16[196,256]{1,0:T(8,128)(2,1)S(1)} %get-tuple-element.45.grad_tokens_here), custom_call_target="tpu_custom_call" | custom-call | tf_op jit(solution)/shard_map/pallas_call | solution.py:159
  (1 shorter events, 0.0 us)
Async XLA Ops:
  1.7 8.0 %collective-permute-start.2 = (bf16[2,196,256]{2,1,0:T(8,128)(2,1)S(1)}, bf16[2,196,256]{2,1,0:T(8,128)(2,1)S(1)}, u32[]{:S(2)}, u32[]{:S(2)}) collective-permute-start(bf16[2,196,256]{2,1,0:T(8,128)(2,1)S(1)} %get-tuple-element.35.own), channel_id=1, source_target_pairs={{0,1},{1,0},{2,3},{3,2},{4,5},{5,4},{6,7},{7,6},{8,9},{9,8},{10,11... | collective-permute-start | bytes 602120 | tf_op jit(solution)/shard_map/ppermute | solution.py:16
  2.3 4.8 %collective-permute-start = (f32[16,196]{1,0:T(8,128)S(1)}, f32[16,196]{1,0:T(8,128)S(1)}, u32[]{:S(2)}, u32[]{:S(2)}) collective-permute-start(f32[16,196]{1,0:T(8,128)S(1)} %get-tuple-element.26.after), channel_id=1, source_target_pairs={{0,2},{2,0},{1,3},{3,1},{4,6},{6,4},{5,7},{7,5},{8,10},{10,8},{9,1... | collective-permute-start | bytes 37640 | tf_op jit(solution)/shard_map/ppermute | solution.py:16
  7.1 15.5 %collective-permute-start.3 = (bf16[2,196,256]{2,1,0:T(8,128)(2,1)S(1)}, bf16[2,196,256]{2,1,0:T(8,128)(2,1)S(1)}, u32[]{:S(2)}, u32[]{:S(2)}) collective-permute-start(bf16[2,196,256]{2,1,0:T(8,128)(2,1)S(1)} %get-tuple-element.35.own), channel_id=1, source_target_pairs={{0,2},{2,0},{1,3},{3,1},{4,6},{6,4},{5,7},{7,5},{8,10},{10,8},{9,1... | collective-permute-start | bytes 602120 | tf_op jit(solution)/shard_map/ppermute | solution.py:16
  8.6 1.2 %collective-permute-start.1 = (f32[16,196]{1,0:T(8,128)S(1)}, f32[16,196]{1,0:T(8,128)S(1)}, u32[]{:S(2)}, u32[]{:S(2)}) collective-permute-start(f32[16,196]{1,0:T(8,128)S(1)} %add.3.first), channel_id=1, source_target_pairs={{0,1},{1,0},{2,3},{3,2},{4,5},{5,4},{6,7},{7,6},{8,9},{9,8},{10,11... | collective-permute-start | bytes 37640 | tf_op jit(solution)/shard_map/ppermute | solution.py:16
  22.6 1.7 %collective-permute-start.5 = (bf16[2,196,256]{2,1,0:T(8,128)(2,1)S(1)}, bf16[2,196,256]{2,1,0:T(8,128)(2,1)S(1)}, u32[]{:S(2)}, u32[]{:S(2)}) collective-permute-start(bf16[2,196,256]{2,1,0:T(8,128)(2,1)S(1)} %collective-permute-done.3.across), channel_id=1, source_target_pairs={{0,1},{1,0},{2,3},{3,2},{4,5},{5,4},{6,7},{7,6},{8,9},{9,8},{10,11... | collective-permute-start | bytes 602120 | tf_op jit(solution)/shard_map/ppermute | solution.py:16
  22.6 1.5 %collective-permute-start.4 = (bf16[2,16,1024]{2,1,0:T(8,128)(2,1)S(1)}, bf16[2,16,1024]{2,1,0:T(8,128)(2,1)S(1)}, u32[]{:S(2)}, u32[]{:S(2)}) collective-permute-start(bf16[2,16,1024]{2,1,0:T(8,128)(2,1)S(1)} %shard_map.79.first), channel_id=1, source_target_pairs={{0,1},{1,0},{2,3},{3,2},{4,5},{5,4},{6,7},{7,6},{8,9},{9,8},{10,11... | collective-permute-start | bytes 196616 | tf_op jit(solution)/shard_map/ppermute | solution.py:16

commit v4 on v3

--- a/solution.py
+++ b/solution.py
@@ -76,15 +76,20 @@
     copies[2].wait()
 
 
-def weight_kernel(after, up_matrix, down_matrix, up_here, down_here, sems):
-    copies = [
-        pltpu.make_async_copy(source, target, sems.at[i])
-        for i, (source, target) in enumerate(((up_matrix, up_here), (down_matrix, down_here)))
-    ]
-    for copy in copies:
-        copy.start()
-    for copy in copies:
-        copy.wait()
+def weight_kernel(chunks, after, up_matrix, down_matrix, up_here, down_here, up_turned, down_turned, sems):
+    sides = ((up_matrix, up_here, up_turned), (down_matrix, down_here, down_turned))
+    copies = []
+    for i, (source, target, _) in enumerate(sides):
+        step = source.shape[1] // chunks
+        for j in range(chunks):
+            part = pl.ds(j * step, step)
+            copies.append(pltpu.make_async_copy(source.at[0, part], target.at[part], sems.at[i * chunks + j]))
+            copies[-1].start()
+    for i, (_, target, turned) in enumerate(sides):
+        step = target.shape[0] // chunks
+        for j in range(chunks):
+            copies[i * chunks + j].wait()
+            turned[:, j * step : (j + 1) * step] = target[j * step : (j + 1) * step].T
 
 
 def slot_kernel(slots, x_size, first, second, own, beside, blocks, dispatch, combine):
@@ -100,15 +105,18 @@
         blocks[:, :, here] = to_blocks(slot_in, grad_out, slots, x_size)
 
 
-def expert_kernel(slots, x_size, blocks, up_matrix, down_matrix, sums):
+def expert_kernel(slots, x_size, blocks, up_matrix, down_matrix, up_turned, down_turned, sums):
     got = blocks[...].astype(F32)
-    sides = [from_blocks(part, slots) for part in jnp.split(got, x_size)]
+    first, second = jnp.split(got, x_size)
+    in_order = lax.axis_index("x") != lax.axis_index("core")
+    parts = (jnp.where(in_order, first, second), jnp.where(in_order, second, first))
+    sides = [from_blocks(part, slots) for part in parts]
     forward, backward = (jnp.concatenate(side, axis=1).astype(BF16) for side in zip(*sides))
-    preact = dot(forward, up_matrix[0], (1, 0))
-    grad_hidden = dot(backward, down_matrix[0], (1, 1))
+    preact = dot(forward, up_matrix[...], (1, 0))
+    grad_hidden = dot(backward, down_turned[...], (1, 0))
     hidden, slope = gelu_parts(preact)
-    sums[0] = dot(hidden.astype(BF16), down_matrix[0], (1, 0)).astype(BF16)
-    sums[1] = dot((grad_hidden * slope).astype(BF16), up_matrix[0], (1, 1)).astype(BF16)
+    sums[0] = dot(hidden.astype(BF16), down_matrix[...], (1, 0)).astype(BF16)
+    sums[1] = dot((grad_hidden * slope).astype(BF16), up_turned[...], (1, 0)).astype(BF16)
 
 
 def pair_kernel(slots, x_size, first, second, blocks):
@@ -130,9 +138,12 @@
         grad_combine += dot(rows[0, :, pl.ds(start, quarter)], part[1], (1, 1))
         grad_dispatch += dot(rows[1, :, pl.ds(start, quarter)], part[0], (1, 1))
     grad_logits = softmax_back(combine[...], grad_combine, 0) + softmax_back(dispatch[...], grad_dispatch, 1)
-    partial = dot(grad_logits.astype(BF16), own[0], (1, 0))
-    partial = outward(partial, slots, lead).astype(BF16)
-    params_part[...] = jnp.broadcast_to(partial[None], params_part.shape)
+    partial = [dot(grad_logits.astype(BF16), part[0], (1, 0)) for part in (own, beside)]
+    upper = lax.axis_index("core") == 1
+    for i, part in enumerate((jnp.where(upper, *partial), jnp.where(upper, *partial[::-1]))):
+        count = params_part.shape[0] // 2
+        part = outward(part, slots, lead).astype(BF16)
+        params_part[i * count : (i + 1) * count] = jnp.broadcast_to(part[None], (count, *part.shape))
     here = pl.ds(pl.multiple_of(half * quarter, quarter), quarter)
     mixed[...] = dot(combine[...].astype(BF16), rows[0, :, here], (0, 0)).astype(BF16)
     token_term = dot(dispatch[...].astype(BF16), rows[1, :, here], (0, 0))
@@ -166,9 +177,19 @@
     x_size = halves // 2
     width = halves * quarter
     table = (columns, seq)
-    lead = experts * 5 // 8
+    lead, middle = experts * 5 // 8, experts // 2
     order = [(lead + i) % experts for i in range(experts)]
-    wide_order = [expert * x_size + x for x in range(x_size) for expert in order]
+    near = [list(range(middle))[::-1], list(range(middle, experts))]
+    wide = [
+        [(expert * x_size + (x if core else 1 - x)) * 2 + core for core in (1, 0) for expert in order]
+        for x in range(x_size)
+    ]
+    narrow = [
+        [(image * x_size + x) * 2 + core for core in (1, 0) for image in near[side if core else 1 - side]]
+        for x in range(x_size)
+        for side in (0, 1)
+    ]
+    axes = ("expert", "x", "core")
 
     own, params, logits = call(
         functools.partial(start_kernel, slots, lead),
@@ -181,16 +202,18 @@
     )
     other = swap(logits, "x")
     beside = swap(own, "core")
-    up_here, down_here = call(
-        weight_kernel,
-        [pltpu.VMEM(w_up.shape, BF16), pltpu.VMEM(w_down.shape, BF16)],
+    chunks = 2
+    shapes = [w_up.shape[1:], w_down.shape[1:], w_up.shape[:0:-1], w_down.shape[:0:-1]]
+    weights = call(
+        functools.partial(weight_kernel, chunks),
+        [pltpu.VMEM(shape, BF16) for shape in shapes],
         logits,
         w_up,
         w_down,
-        scratch=[pltpu.SemaphoreType.DMA((2,))],
+        scratch=[pltpu.SemaphoreType.DMA((2 * chunks,))],
         in_hbm=(1, 2),
     )
-    logits, up_here, down_here = lax.optimization_barrier((logits + other, up_here, down_here))
+    logits, *weights = lax.optimization_barrier((logits + other, *weights))
     logits, own_later = lax.optimization_barrier((logits, own))
     across = swap(own_later, "x")
     other = swap(logits, "core")
@@ -203,9 +226,9 @@
         beside,
     )
 
-    blocks = lax.all_to_all(blocks, ("expert", "x"), 0, 0, tiled=True, axis_index_groups=[wide_order])
+    blocks = lax.all_to_all(blocks, axes, 0, 0, tiled=True, axis_index_groups=wide)
     (sums,) = call(
-        functools.partial(expert_kernel, slots, x_size), [((2, columns, width), BF16)], blocks, up_here, down_here
+        functools.partial(expert_kernel, slots, x_size), [((2, columns, width), BF16)], blocks, *weights
     )
 
     sums, across = lax.optimization_barrier((sums, across))
@@ -218,7 +241,7 @@
         other_sums,
     )
     blocks, corner = lax.optimization_barrier((blocks, corner))
-    blocks = lax.all_to_all(blocks, ("expert", "x"), 0, 0, tiled=True, axis_index_groups=[wide_order])
+    blocks = lax.all_to_all(blocks, axes, 0, 0, tiled=True, axis_index_groups=wide)
     params_part, mixed, grad_tokens = call(
         functools.partial(image_kernel, slots, x_size, lead),
         [((experts, columns, quarter), BF16), pltpu.VMEM((seq, quarter), BF16), pltpu.VMEM((seq, quarter), BF16)],
@@ -234,7 +257,7 @@
         limit=16 if experts * columns <= 1024 else 48,
     )
 
-    params_parts = lax.all_to_all(params_part, "expert", 0, 0, tiled=True, axis_index_groups=[order])
+    params_parts = lax.all_to_all(params_part, axes, 0, 0, tiled=True, axis_index_groups=narrow)
     mixed, grad_tokens, grad_params = call(
         end_kernel,
         [((seq, quarter), BF16), ((seq, quarter), BF16), ((columns, quarter), F32)],

time: 44.6 us -> 43.7 us (0.980)
  blocking collectives: 29.4 us -> 28.9 us
    all_to_all x3, blocking collectives: 29.4 us -> 28.9 us  [the longest x2 20.4 us: local(): lax.all_to_all(blocks, axes, 0, 0, tiled=True, axis_index_groups=wide)]
where the time goes in v4:
time: 43.7 us; the launch traced here: 43.3 us
  blocking collectives  28.9 us (66%)
  Pallas kernels  6.85 us (16%)
  starting transfers between devices  4.66 us (11%)
  waiting for transfers between devices  2.23 us (5%)
  between operations  0.69 us (2%)
    all_to_all x2, blocking collectives, local(): lax.all_to_all(blocks, axes, 0, 0, tiled=True, axis_index_groups=wide)  20.4 us
    all_to_all x1, blocking collectives, local(): lax.all_to_all(params_part, axes, 0, 0, tiled=True, axis_index_groups=nar...  8.51 us
    pallas_call x7, Pallas kernels, call(): run(*(pltpu.with_memory_space_constraint(arg, pltpu.HBM) if i in in_hbm e...  6.85 us
    ppermute x6, starting transfers between devices, swap(): return lax.ppermute(array, axis, [(0, 1), (1, 0)])  4.66 us
    ppermute x6, waiting for transfers between devices, swap(): return lax.ppermute(array, axis, [(0, 1), (1, 0)])  2.23 us
  transfers between devices with their start and end apart: 6, of which 2 were waited for; matrix products, arithmetic and copies ran while one was open for 0% of the time, Pallas kernels for 10%

profile of v4, /device:TPU:0, one launch (start us, length us, event | category | flops | bytes accessed | tf_op | source)
XLA Modules:
  0.0 43.3 jit_solution(14163488490991933054)
XLA Ops:
  0.6 1.1 %shard_map.76 = (bf16[2,196,256]{2,1,0:T(8,128)(2,1)S(1)}, bf16[16,256]{1,0:T(8,128)(2,1)S(1)}, f32[16,196]{1,0:T(8,128)S(1)}) custom-call(bf16[196,256]{1,0:T(8,128)(2,1)} %tokens.1, bf16[196,256]{1,0:T(8,128)(2,1)} %cotangent.1, bf16[16,256]{1,0:T(8,128)(2,1)} %bitcast.2), custom_call_target="tpu_custom_call" | custom-call | tf_op jit(solution)/shard_map/pallas_call | solution.py:170
  1.7 0.5 %collective-permute-start.2 = (bf16[2,196,256]{2,1,0:T(8,128)(2,1)S(1)}, bf16[2,196,256]{2,1,0:T(8,128)(2,1)S(1)}, u32[]{:S(2)}, u32[]{:S(2)}) collective-permute-start(bf16[2,196,256]{2,1,0:T(8,128)(2,1)S(1)} %get-tuple-element.43.own), channel_id=1, source_target_pairs={{0,1},{1,0},{2,3},{3,2},{4,5},{5,4},{6,7},{7,6},{8,9},{9,8},{10,11... | collective-permute-start | bytes 602120 | tf_op jit(solution)/shard_map/ppermute | solution.py:16
  2.3 2.6 %collective-permute-start = (f32[16,196]{1,0:T(8,128)S(1)}, f32[16,196]{1,0:T(8,128)S(1)}, u32[]{:S(2)}, u32[]{:S(2)}) collective-permute-start(f32[16,196]{1,0:T(8,128)S(1)} %get-tuple-element.30.after), channel_id=1, source_target_pairs={{0,2},{2,0},{1,3},{3,1},{4,6},{6,4},{5,7},{7,5},{8,10},{10,8},{9,1... | collective-permute-start | bytes 37640 | tf_op jit(solution)/shard_map/ppermute | solution.py:16
  4.8 2.7 %shard_map.77 = (bf16[1024,1024]{1,0:T(8,128)(2,1)S(1)}, bf16[1024,1024]{1,0:T(8,128)(2,1)S(1)}, bf16[1024,1024]{1,0:T(8,128)(2,1)S(1)}, bf16[1024,1024]{1,0:T(8,128)(2,1)S(1)}) custom-call(f32[16,196]{1,0:T(8,128)S(1)} %get-tuple-element.30.after, bf16[1,1024,1024]{2,1,0:T(8,128)(2,1)} %up_matrix.1, bf16[1,1024,1024]{2,1,0:T(8,128)(2,1)} %down_matrix.1), custom_call_target="tpu_custom_call" | custom-call | tf_op jit(solution)/shard_map/pallas_call | solution.py:170
  7.5 0.0 collective-permute-done
  7.5 1.1 %collective-permute-start.3 = (bf16[2,196,256]{2,1,0:T(8,128)(2,1)S(1)}, bf16[2,196,256]{2,1,0:T(8,128)(2,1)S(1)}, u32[]{:S(2)}, u32[]{:S(2)}) collective-permute-start(bf16[2,196,256]{2,1,0:T(8,128)(2,1)S(1)} %get-tuple-element.43.own), channel_id=1, source_target_pairs={{0,2},{2,0},{1,3},{3,1},{4,6},{6,4},{5,7},{7,5},{8,10},{10,8},{9,1... | collective-permute-start | bytes 602120 | tf_op jit(solution)/shard_map/ppermute | solution.py:16
  8.6 0.0 collective-permute-start.1
  8.6 1.2 %collective-permute-done.1.second = f32[16,196]{1,0:T(8,128)S(1)} collective-permute-done((f32[16,196]{1,0:T(8,128)S(1)}, f32[16,196]{1,0:T(8,128)S(1)}, u32[]{:S(2)}, u32[]{:S(2)}) %collective-permute-start.1) | collective-permute-done | bytes 12576 | tf_op jit(solution)/shard_map/ppermute | solution.py:16
  9.8 0.0 collective-permute-done.2.beside
  9.8 0.3 shard_map.78
  10.1 10.6 %all_to_all.15.blocks = bf16[16,4,512]{2,1,0:T(4,128)(2,1)S(1)} all-to-all(bf16[16,4,512]{2,1,0:T(4,128)(2,1)S(1)} %get-tuple-element.38), channel_id=1, replica_groups={{21,25,29,1,5,9,13,17,22,26,30,2,6,10,14,18},{23,27,31,3,7,11,15,19,20,..., dimensions={0} | all-to-all | bytes 131072 | tf_op jit(solution)/shard_map/all_to_all | solution.py:229
  20.7 1.2 %shard_map.79.first = bf16[2,16,1024]{2,1,0:T(8,128)(2,1)S(1)} custom-call(bf16[16,4,512]{2,1,0:T(4,128)(2,1)S(1)} %all_to_all.15.blocks, bf16[1024,1024]{1,0:T(8,128)(2,1)S(1)} %get-tuple-element.39.up_matrix, bf16[1024,1024]{1,0:T(8,128)(2,1)S(1)} %get-tuple-element.40.down_matrix, bf16[1024,1024]{1,0:T(8,128)(2,1)S(1)} %get-tuple-element.41.up_turned, ...), custom_call_target="tpu_custom_call" | custom-call | tf_op jit(solution)/shard_map/pallas_call | solution.py:170
  21.9 0.0 collective-permute-done.3.across
  21.9 0.2 collective-permute-start.5
  22.0 0.3 collective-permute-start.4
  22.4 1.0 %collective-permute-done.4.second = bf16[2,16,1024]{2,1,0:T(8,128)(2,1)S(1)} collective-permute-done((bf16[2,16,1024]{2,1,0:T(8,128)(2,1)S(1)}, bf16[2,16,1024]{2,1,0:T(8,128)(2,1)S(1)}, u32[]{:S(2)}, u32[]{:S(2)}) %collective-permute-start.4) | collective-permute-done | bytes 65568 | tf_op jit(solution)/shard_map/ppermute | solution.py:16
  23.4 0.1 shard_map.80
  23.5 0.0 collective-permute-done.5.corner
  23.6 9.8 %all_to_all.16.blocks = bf16[16,4,1024]{2,1,0:T(4,128)(2,1)S(1)} all-to-all(bf16[16,4,1024]{2,1,0:T(4,128)(2,1)S(1)} %shard_map.80), channel_id=1, replica_groups={{21,25,29,1,5,9,13,17,22,26,30,2,6,10,14,18},{23,27,31,3,7,11,15,19,20,..., dimensions={0} | all-to-all | bytes 262144 | tf_op jit(solution)/shard_map/all_to_all | solution.py:244
  33.4 0.7 %shard_map.81 = (bf16[8,16,256]{2,1,0:T(8,128)(2,1)S(1)}, bf16[196,256]{1,0:T(8,128)(2,1)S(1)}, bf16[196,256]{1,0:T(8,128)(2,1)S(1)}) custom-call(bf16[16,4,1024]{2,1,0:T(4,128)(2,1)S(1)} %all_to_all.16.blocks, bf16[2,196,256]{2,1,0:T(8,128)(2,1)S(1)} %get-tuple-element.43.own, bf16[2,196,256]{2,1,0:T(8,128)(2,1)S(1)} %collective-permute-done.2.beside, ...), custom_call_target="tpu_custom_call" | custom-call | tf_op jit(solution)/shard_map/pallas_call | solution.py:170
  34.1 8.5 %all_to_all.17.parts = bf16[8,16,256]{2,1,0:T(8,128)(2,1)S(1)} all-to-all(bf16[8,16,256]{2,1,0:T(8,128)(2,1)S(1)} %get-tuple-element.51), channel_id=1, replica_groups={{13,9,5,1,16,20,24,28},{17,21,25,29,12,8,4,0},{15,11,7,3,18,22,26,30},{..., dimensions={0} | all-to-all | bytes 131072 | tf_op jit(solution)/shard_map/all_to_all | solution.py:260
  42.6 0.7 %shard_map.82 = (bf16[196,256]{1,0:T(8,128)(2,1)}, bf16[196,256]{1,0:T(8,128)(2,1)}, f32[16,256]{1,0:T(8,128)}) custom-call(bf16[8,16,256]{2,1,0:T(8,128)(2,1)S(1)} %all_to_all.17.parts, bf16[196,256]{1,0:T(8,128)(2,1)S(1)} %get-tuple-element.52.mixed_here, bf16[196,256]{1,0:T(8,128)(2,1)S(1)} %get-tuple-element.53.grad_tokens_here), custom_call_target="tpu_custom_call" | custom-call | tf_op jit(solution)/shard_map/pallas_call | solution.py:170
  (1 shorter events, 0.0 us)
Async XLA Ops:
  1.7 8.0 %collective-permute-start.2 = (bf16[2,196,256]{2,1,0:T(8,128)(2,1)S(1)}, bf16[2,196,256]{2,1,0:T(8,128)(2,1)S(1)}, u32[]{:S(2)}, u32[]{:S(2)}) collective-permute-start(bf16[2,196,256]{2,1,0:T(8,128)(2,1)S(1)} %get-tuple-element.43.own), channel_id=1, source_target_pairs={{0,1},{1,0},{2,3},{3,2},{4,5},{5,4},{6,7},{7,6},{8,9},{9,8},{10,11... | collective-permute-start | bytes 602120 | tf_op jit(solution)/shard_map/ppermute | solution.py:16
  2.3 5.2 %collective-permute-start = (f32[16,196]{1,0:T(8,128)S(1)}, f32[16,196]{1,0:T(8,128)S(1)}, u32[]{:S(2)}, u32[]{:S(2)}) collective-permute-start(f32[16,196]{1,0:T(8,128)S(1)} %get-tuple-element.30.after), channel_id=1, source_target_pairs={{0,2},{2,0},{1,3},{3,1},{4,6},{6,4},{5,7},{7,5},{8,10},{10,8},{9,1... | collective-permute-start | bytes 37640 | tf_op jit(solution)/shard_map/ppermute | solution.py:16
  7.5 14.4 %collective-permute-start.3 = (bf16[2,196,256]{2,1,0:T(8,128)(2,1)S(1)}, bf16[2,196,256]{2,1,0:T(8,128)(2,1)S(1)}, u32[]{:S(2)}, u32[]{:S(2)}) collective-permute-start(bf16[2,196,256]{2,1,0:T(8,128)(2,1)S(1)} %get-tuple-element.43.own), channel_id=1, source_target_pairs={{0,2},{2,0},{1,3},{3,1},{4,6},{6,4},{5,7},{7,5},{8,10},{10,8},{9,1... | collective-permute-start | bytes 602120 | tf_op jit(solution)/shard_map/ppermute | solution.py:16
  8.6 1.2 %collective-permute-start.1 = (f32[16,196]{1,0:T(8,128)S(1)}, f32[16,196]{1,0:T(8,128)S(1)}, u32[]{:S(2)}, u32[]{:S(2)}) collective-permute-start(f32[16,196]{1,0:T(8,128)S(1)} %add.3.first), channel_id=1, source_target_pairs={{0,1},{1,0},{2,3},{3,2},{4,5},{5,4},{6,7},{7,6},{8,9},{9,8},{10,11... | collective-permute-start | bytes 37640 | tf_op jit(solution)/shard_map/ppermute | solution.py:16
  21.9 1.7 %collective-permute-start.5 = (bf16[2,196,256]{2,1,0:T(8,128)(2,1)S(1)}, bf16[2,196,256]{2,1,0:T(8,128)(2,1)S(1)}, u32[]{:S(2)}, u32[]{:S(2)}) collective-permute-start(bf16[2,196,256]{2,1,0:T(8,128)(2,1)S(1)} %collective-permute-done.3.across), channel_id=1, source_target_pairs={{0,1},{1,0},{2,3},{3,2},{4,5},{5,4},{6,7},{7,6},{8,9},{9,8},{10,11... | collective-permute-start | bytes 602120 | tf_op jit(solution)/shard_map/ppermute | solution.py:16
  22.0 1.4 %collective-permute-start.4 = (bf16[2,16,1024]{2,1,0:T(8,128)(2,1)S(1)}, bf16[2,16,1024]{2,1,0:T(8,128)(2,1)S(1)}, u32[]{:S(2)}, u32[]{:S(2)}) collective-permute-start(bf16[2,16,1024]{2,1,0:T(8,128)(2,1)S(1)} %shard_map.79.first), channel_id=1, source_target_pairs={{0,1},{1,0},{2,3},{3,2},{4,5},{5,4},{6,7},{7,6},{8,9},{9,8},{10,11... | collective-permute-start | bytes 196616 | tf_op jit(solution)/shard_map/ppermute | solution.py:16

commit v5 on v4

--- a/solution.py
+++ b/solution.py
@@ -74,6 +74,11 @@
     copies[1].wait()
     logits[...] = dot(params_in[...], own[0], (1, 1))
     copies[2].wait()
+
+
+def add_kernel(slots, lead, logits, tokens, params, total):
+    params_in = inward(params[...].astype(F32), slots, lead).astype(BF16)
+    total[...] = logits[...] + dot(params_in, tokens[...], (1, 1))
 
 
 def weight_kernel(chunks, after, up_matrix, down_matrix, up_here, down_here, up_turned, down_turned, sems):
@@ -92,13 +97,14 @@
             turned[:, j * step : (j + 1) * step] = target[j * step : (j + 1) * step].T
 
 
-def slot_kernel(slots, x_size, first, second, own, beside, blocks, dispatch, combine):
+def slot_kernel(slots, x_size, first, second, own, tokens, cotangent, blocks, dispatch, combine):
     logits = first[...] + second[...]
     over_tokens, over_columns = softmax(logits, 1), softmax(logits, 0)
     dispatch[...] = over_tokens
     combine[...] = over_columns
     quarter = own.shape[2]
-    for part, core in ((own, lax.axis_index("core")), (beside, 1 - lax.axis_index("core"))):
+    core = lax.axis_index("core")
+    for part, core in (((own[0], own[1]), core), ((tokens[...], cotangent[...]), 1 - core)):
         here = pl.ds(pl.multiple_of(core * quarter, quarter), quarter)
         slot_in = dot(over_tokens.astype(BF16), part[0], (1, 0))
         grad_out = dot(over_columns.astype(BF16), part[1], (1, 0))
@@ -125,7 +131,7 @@
 
 
 def image_kernel(
-    slots, x_size, lead, blocks, own, beside, across, corner, dispatch, combine, params, params_part, mixed, grad_tokens, rows
+    slots, x_size, lead, blocks, own, tokens, cotangent, across, corner, dispatch, combine, params, params_part, mixed, grad_tokens, rows
 ):
     half = lax.axis_index("x") * 2 + lax.axis_index("core")
     quarter = own.shape[2]
@@ -133,12 +139,12 @@
     rows[0] = slot_out.astype(BF16)
     rows[1] = grad_in.astype(BF16)
     grad_combine = grad_dispatch = 0.0
-    for offset, part in enumerate((own, beside, across, corner)):
+    for offset, part in enumerate((own, (tokens, cotangent), across, corner)):
         start = pl.multiple_of(jnp.bitwise_xor(half, offset) * quarter, quarter)
-        grad_combine += dot(rows[0, :, pl.ds(start, quarter)], part[1], (1, 1))
-        grad_dispatch += dot(rows[1, :, pl.ds(start, quarter)], part[0], (1, 1))
+        grad_combine += dot(rows[0, :, pl.ds(start, quarter)], part[1][...], (1, 1))
+        grad_dispatch += dot(rows[1, :, pl.ds(start, quarter)], part[0][...], (1, 1))
     grad_logits = softmax_back(combine[...], grad_combine, 0) + softmax_back(dispatch[...], grad_dispatch, 1)
-    partial = [dot(grad_logits.astype(BF16), part[0], (1, 0)) for part in (own, beside)]
+    partial = [dot(grad_logits.astype(BF16), part[0], (1, 0)) for part in (own, (tokens[...],))]
     upper = lax.axis_index("core") == 1
     for i, part in enumerate((jnp.where(upper, *partial), jnp.where(upper, *partial[::-1]))):
         count = params_part.shape[0] // 2
@@ -191,6 +197,7 @@
     ]
     axes = ("expert", "x", "core")
 
+    beside = [swap(tokens, "core"), swap(cotangent, "core")]
     own, params, logits = call(
         functools.partial(start_kernel, slots, lead),
         [((2, seq, quarter), BF16), ((columns, quarter), BF16), (table, F32)],
@@ -200,8 +207,10 @@
         scratch=[pltpu.VMEM((columns, quarter), BF16), pltpu.SemaphoreType.DMA((3,))],
         in_hbm=(0, 1, 2),
     )
+    (logits,) = call(
+        functools.partial(add_kernel, slots, lead), [(table, F32)], logits, beside[0], swap(slot_params.T, "core")
+    )
     other = swap(logits, "x")
-    beside = swap(own, "core")
     chunks = 2
     shapes = [w_up.shape[1:], w_down.shape[1:], w_up.shape[:0:-1], w_down.shape[:0:-1]]
     weights = call(
@@ -213,17 +222,15 @@
         scratch=[pltpu.SemaphoreType.DMA((2 * chunks,))],
         in_hbm=(1, 2),
     )
-    logits, *weights = lax.optimization_barrier((logits + other, *weights))
-    logits, own_later = lax.optimization_barrier((logits, own))
+    other, own_later, *weights = lax.optimization_barrier((other, own, *weights))
     across = swap(own_later, "x")
-    other = swap(logits, "core")
     blocks, dispatch, combine = call(
         functools.partial(slot_kernel, slots, x_size),
         [((x_size * experts, 2 * slots, 2 * quarter), BF16), (table, F32), (table, F32)],
         logits,
         other,
         own,
-        beside,
+        *beside,
     )
 
     blocks = lax.all_to_all(blocks, axes, 0, 0, tiled=True, axis_index_groups=wide)
@@ -247,7 +254,7 @@
         [((experts, columns, quarter), BF16), pltpu.VMEM((seq, quarter), BF16), pltpu.VMEM((seq, quarter), BF16)],
         blocks,
         own,
-        beside,
+        *beside,
         across,
         corner,
         dispatch,

time: 43.7 us -> 43.3 us (level)
  waiting for transfers between devices: 2.23 us -> 1.05 us
  starting transfers between devices: 4.66 us -> 5.38 us
    ppermute x6 -> x7, waiting for transfers between devices: 2.23 us -> 1.05 us  [swap(): return lax.ppermute(array, axis, [(0, 1), (1, 0)])]
    ppermute x6 -> x7, starting transfers between devices: 4.66 us -> 5.38 us  [swap(): return lax.ppermute(array, axis, [(0, 1), (1, 0)])]
    pallas_call x7 -> x8, Pallas kernels: 6.85 us -> 6.99 us  [call(): run(*(pltpu.with_memory_space_constraint(arg, pltpu.HBM) if i in in_hbm e...]
  transfers between devices with their start and end apart: 6 -> 7, of which waited for: 2 -> 1; matrix products, arithmetic and copies ran while one was open for 0% -> 0% of each run, Pallas kernels for 10% -> 13%
where the time goes in v5:
time: 43.3 us; the launch traced here: 43 us
  blocking collectives  28.9 us (67%)
  Pallas kernels  6.99 us (16%)
  starting transfers between devices  5.38 us (12%)
  waiting for transfers between devices  1.05 us (2%)
  between operations  0.7 us (2%)
    all_to_all x2, blocking collectives, local(): lax.all_to_all(blocks, axes, 0, 0, tiled=True, axis_index_groups=wide)  20.4 us
    all_to_all x1, blocking collectives, local(): lax.all_to_all(params_part, axes, 0, 0, tiled=True, axis_index_groups=nar...  8.52 us
    pallas_call x8, Pallas kernels, call(): run(*(pltpu.with_memory_space_constraint(arg, pltpu.HBM) if i in in_hbm e...  6.99 us
    ppermute x7, starting transfers between devices, swap(): return lax.ppermute(array, axis, [(0, 1), (1, 0)])  5.38 us
    ppermute x7, waiting for transfers between devices, swap(): return lax.ppermute(array, axis, [(0, 1), (1, 0)])  1.05 us
  transfers between devices with their start and end apart: 7, of which 1 were waited for; matrix products, arithmetic and copies ran while one was open for 0% of the time, Pallas kernels for 13%

profile of v5, /device:TPU:0, one launch (start us, length us, event | category | flops | bytes accessed | tf_op | source)
XLA Modules:
  0.0 43.0 jit_solution(7294861621099366052)
XLA Ops:
  0.6 0.5 %collective-permute-start = (bf16[196,256]{1,0:T(8,128)(2,1)}, bf16[196,256]{1,0:T(8,128)(2,1)S(1)}, u32[]{:S(2)}, u32[]{:S(2)}) collective-permute-start(bf16[196,256]{1,0:T(8,128)(2,1)} %tokens.1), channel_id=1, source_target_pairs={{0,1},{1,0},{2,3},{3,2},{4,5},{5,4},{6,7},{7,6},{8,9},{9,8},{10,11... | collective-permute-start | bytes 301064 | tf_op jit(solution)/shard_map/ppermute | solution.py:16
  1.1 0.1 collective-permute-start.3
  1.2 0.4 %collective-permute-start.1 = (bf16[16,256]{1,0:T(8,128)(2,1)}, bf16[16,256]{1,0:T(8,128)(2,1)S(1)}, u32[]{:S(2)}, u32[]{:S(2)}) collective-permute-start(bf16[16,256]{1,0:T(8,128)(2,1)} %bitcast.2), channel_id=1, source_target_pairs={{0,1},{1,0},{2,3},{3,2},{4,5},{5,4},{6,7},{7,6},{8,9},{9,8},{10,11... | collective-permute-start | bytes 24584 | tf_op jit(solution)/shard_map/ppermute | solution.py:16
  1.7 1.1 %shard_map.76 = (bf16[2,196,256]{2,1,0:T(8,128)(2,1)S(1)}, bf16[16,256]{1,0:T(8,128)(2,1)S(1)}, f32[16,196]{1,0:T(8,128)S(1)}) custom-call(bf16[196,256]{1,0:T(8,128)(2,1)} %tokens.1, bf16[196,256]{1,0:T(8,128)(2,1)} %cotangent.1, bf16[16,256]{1,0:T(8,128)(2,1)} %bitcast.3), custom_call_target="tpu_custom_call" | custom-call | tf_op jit(solution)/shard_map/pallas_call | solution.py:176
  2.8 0.0 collective-permute-done.1.params
  2.8 0.0 collective-permute-done.tokens
  2.8 0.1 shard_map.77.after.first
  2.9 2.8 %collective-permute-start.2 = (f32[16,196]{1,0:T(8,128)S(1)}, f32[16,196]{1,0:T(8,128)S(1)}, u32[]{:S(2)}, u32[]{:S(2)}) collective-permute-start(f32[16,196]{1,0:T(8,128)S(1)} %shard_map.77.after.first), channel_id=1, source_target_pairs={{0,2},{2,0},{1,3},{3,1},{4,6},{6,4},{5,7},{7,5},{8,10},{10,8},{9,1... | collective-permute-start | bytes 37640 | tf_op jit(solution)/shard_map/ppermute | solution.py:16
  5.7 2.7 %shard_map.78 = (bf16[1024,1024]{1,0:T(8,128)(2,1)S(1)}, bf16[1024,1024]{1,0:T(8,128)(2,1)S(1)}, bf16[1024,1024]{1,0:T(8,128)(2,1)S(1)}, bf16[1024,1024]{1,0:T(8,128)(2,1)S(1)}) custom-call(f32[16,196]{1,0:T(8,128)S(1)} %shard_map.77.after.first, bf16[1,1024,1024]{2,1,0:T(8,128)(2,1)} %up_matrix.1, bf16[1,1024,1024]{2,1,0:T(8,128)(2,1)} %down_matrix.1), custom_call_target="tpu_custom_call" | custom-call | tf_op jit(solution)/shard_map/pallas_call | solution.py:176
  8.4 0.0 collective-permute-done.2.second
  8.4 1.1 %collective-permute-start.4 = (bf16[2,196,256]{2,1,0:T(8,128)(2,1)S(1)}, bf16[2,196,256]{2,1,0:T(8,128)(2,1)S(1)}, u32[]{:S(2)}, u32[]{:S(2)}) collective-permute-start(bf16[2,196,256]{2,1,0:T(8,128)(2,1)S(1)} %get-tuple-element.41.own), channel_id=1, source_target_pairs={{0,2},{2,0},{1,3},{3,1},{4,6},{6,4},{5,7},{7,5},{8,10},{10,8},{9,1... | collective-permute-start | bytes 602120 | tf_op jit(solution)/shard_map/ppermute | solution.py:16
  9.4 0.0 collective-permute-done.3.cotangent
  9.4 0.3 shard_map.79
  9.8 10.6 %all_to_all.15.blocks = bf16[16,4,512]{2,1,0:T(4,128)(2,1)S(1)} all-to-all(bf16[16,4,512]{2,1,0:T(4,128)(2,1)S(1)} %get-tuple-element.36), channel_id=1, replica_groups={{21,25,29,1,5,9,13,17,22,26,30,2,6,10,14,18},{23,27,31,3,7,11,15,19,20,..., dimensions={0} | all-to-all | bytes 131072 | tf_op jit(solution)/shard_map/all_to_all | solution.py:236
  20.4 1.2 %shard_map.80.first = bf16[2,16,1024]{2,1,0:T(8,128)(2,1)S(1)} custom-call(bf16[16,4,512]{2,1,0:T(4,128)(2,1)S(1)} %all_to_all.15.blocks, bf16[1024,1024]{1,0:T(8,128)(2,1)S(1)} %get-tuple-element.37.up_matrix, bf16[1024,1024]{1,0:T(8,128)(2,1)S(1)} %get-tuple-element.38.down_matrix, bf16[1024,1024]{1,0:T(8,128)(2,1)S(1)} %get-tuple-element.39.up_turned, ...), custom_call_target="tpu_custom_call" | custom-call | tf_op jit(solution)/shard_map/pallas_call | solution.py:176
  21.6 0.0 collective-permute-done.4.across
  21.6 0.2 collective-permute-start.6
  21.7 0.4 collective-permute-start.5
  22.1 1.0 %collective-permute-done.5.second = bf16[2,16,1024]{2,1,0:T(8,128)(2,1)S(1)} collective-permute-done((bf16[2,16,1024]{2,1,0:T(8,128)(2,1)S(1)}, bf16[2,16,1024]{2,1,0:T(8,128)(2,1)S(1)}, u32[]{:S(2)}, u32[]{:S(2)}) %collective-permute-start.5) | collective-permute-done | bytes 65568 | tf_op jit(solution)/shard_map/ppermute | solution.py:16
  23.1 0.1 shard_map.81
  23.2 0.0 collective-permute-done.6.corner
  23.2 9.8 %all_to_all.16.blocks = bf16[16,4,1024]{2,1,0:T(4,128)(2,1)S(1)} all-to-all(bf16[16,4,1024]{2,1,0:T(4,128)(2,1)S(1)} %shard_map.81), channel_id=1, replica_groups={{21,25,29,1,5,9,13,17,22,26,30,2,6,10,14,18},{23,27,31,3,7,11,15,19,20,..., dimensions={0} | all-to-all | bytes 262144 | tf_op jit(solution)/shard_map/all_to_all | solution.py:251
  33.1 0.7 %shard_map.82 = (bf16[8,16,256]{2,1,0:T(8,128)(2,1)S(1)}, bf16[196,256]{1,0:T(8,128)(2,1)S(1)}, bf16[196,256]{1,0:T(8,128)(2,1)S(1)}) custom-call(bf16[16,4,1024]{2,1,0:T(4,128)(2,1)S(1)} %all_to_all.16.blocks, bf16[2,196,256]{2,1,0:T(8,128)(2,1)S(1)} %get-tuple-element.41.own, bf16[196,256]{1,0:T(8,128)(2,1)S(1)} %collective-permute-done.tokens, ...), custom_call_target="tpu_custom_call" | custom-call | tf_op jit(solution)/shard_map/pallas_call | solution.py:176
  33.8 8.5 %all_to_all.17.parts = bf16[8,16,256]{2,1,0:T(8,128)(2,1)S(1)} all-to-all(bf16[8,16,256]{2,1,0:T(8,128)(2,1)S(1)} %get-tuple-element.49), channel_id=1, replica_groups={{13,9,5,1,16,20,24,28},{17,21,25,29,12,8,4,0},{15,11,7,3,18,22,26,30},{..., dimensions={0} | all-to-all | bytes 131072 | tf_op jit(solution)/shard_map/all_to_all | solution.py:267
  42.3 0.7 %shard_map.83 = (bf16[196,256]{1,0:T(8,128)(2,1)}, bf16[196,256]{1,0:T(8,128)(2,1)}, f32[16,256]{1,0:T(8,128)}) custom-call(bf16[8,16,256]{2,1,0:T(8,128)(2,1)S(1)} %all_to_all.17.parts, bf16[196,256]{1,0:T(8,128)(2,1)S(1)} %get-tuple-element.50.mixed_here, bf16[196,256]{1,0:T(8,128)(2,1)S(1)} %get-tuple-element.51.grad_tokens_here), custom_call_target="tpu_custom_call" | custom-call | tf_op jit(solution)/shard_map/pallas_call | solution.py:176
Async XLA Ops:
  0.6 2.2 %collective-permute-start = (bf16[196,256]{1,0:T(8,128)(2,1)}, bf16[196,256]{1,0:T(8,128)(2,1)S(1)}, u32[]{:S(2)}, u32[]{:S(2)}) collective-permute-start(bf16[196,256]{1,0:T(8,128)(2,1)} %tokens.1), channel_id=1, source_target_pairs={{0,1},{1,0},{2,3},{3,2},{4,5},{5,4},{6,7},{7,6},{8,9},{9,8},{10,11... | collective-permute-start | bytes 301064 | tf_op jit(solution)/shard_map/ppermute | solution.py:16
  1.1 8.3 %collective-permute-start.3 = (bf16[196,256]{1,0:T(8,128)(2,1)}, bf16[196,256]{1,0:T(8,128)(2,1)S(1)}, u32[]{:S(2)}, u32[]{:S(2)}) collective-permute-start(bf16[196,256]{1,0:T(8,128)(2,1)} %cotangent.1), channel_id=1, source_target_pairs={{0,1},{1,0},{2,3},{3,2},{4,5},{5,4},{6,7},{7,6},{8,9},{9,8},{10,11... | collective-permute-start | bytes 301064 | tf_op jit(solution)/shard_map/ppermute | solution.py:16
  1.2 1.6 %collective-permute-start.1 = (bf16[16,256]{1,0:T(8,128)(2,1)}, bf16[16,256]{1,0:T(8,128)(2,1)S(1)}, u32[]{:S(2)}, u32[]{:S(2)}) collective-permute-start(bf16[16,256]{1,0:T(8,128)(2,1)} %bitcast.2), channel_id=1, source_target_pairs={{0,1},{1,0},{2,3},{3,2},{4,5},{5,4},{6,7},{7,6},{8,9},{9,8},{10,11... | collective-permute-start | bytes 24584 | tf_op jit(solution)/shard_map/ppermute | solution.py:16
  2.9 5.4 %collective-permute-start.2 = (f32[16,196]{1,0:T(8,128)S(1)}, f32[16,196]{1,0:T(8,128)S(1)}, u32[]{:S(2)}, u32[]{:S(2)}) collective-permute-start(f32[16,196]{1,0:T(8,128)S(1)} %shard_map.77.after.first), channel_id=1, source_target_pairs={{0,2},{2,0},{1,3},{3,1},{4,6},{6,4},{5,7},{7,5},{8,10},{10,8},{9,1... | collective-permute-start | bytes 37640 | tf_op jit(solution)/shard_map/ppermute | solution.py:16
  8.4 13.2 %collective-permute-start.4 = (bf16[2,196,256]{2,1,0:T(8,128)(2,1)S(1)}, bf16[2,196,256]{2,1,0:T(8,128)(2,1)S(1)}, u32[]{:S(2)}, u32[]{:S(2)}) collective-permute-start(bf16[2,196,256]{2,1,0:T(8,128)(2,1)S(1)} %get-tuple-element.41.own), channel_id=1, source_target_pairs={{0,2},{2,0},{1,3},{3,1},{4,6},{6,4},{5,7},{7,5},{8,10},{10,8},{9,1... | collective-permute-start | bytes 602120 | tf_op jit(solution)/shard_map/ppermute | solution.py:16
  21.6 1.7 %collective-permute-start.6 = (bf16[2,196,256]{2,1,0:T(8,128)(2,1)S(1)}, bf16[2,196,256]{2,1,0:T(8,128)(2,1)S(1)}, u32[]{:S(2)}, u32[]{:S(2)}) collective-permute-start(bf16[2,196,256]{2,1,0:T(8,128)(2,1)S(1)} %collective-permute-done.4.across), channel_id=1, source_target_pairs={{0,1},{1,0},{2,3},{3,2},{4,5},{5,4},{6,7},{7,6},{8,9},{9,8},{10,11... | collective-permute-start | bytes 602120 | tf_op jit(solution)/shard_map/ppermute | solution.py:16
  21.7 1.4 %collective-permute-start.5 = (bf16[2,16,1024]{2,1,0:T(8,128)(2,1)S(1)}, bf16[2,16,1024]{2,1,0:T(8,128)(2,1)S(1)}, u32[]{:S(2)}, u32[]{:S(2)}) collective-permute-start(bf16[2,16,1024]{2,1,0:T(8,128)(2,1)S(1)} %shard_map.80.first), channel_id=1, source_target_pairs={{0,1},{1,0},{2,3},{3,2},{4,5},{5,4},{6,7},{7,6},{8,9},{9,8},{10,11... | collective-permute-start | bytes 196616 | tf_op jit(solution)/shard_map/ppermute | solution.py:16

commit v6 on v5

--- a/solution.py
+++ b/solution.py
@@ -131,7 +131,7 @@
 
 
 def image_kernel(
-    slots, x_size, lead, blocks, own, tokens, cotangent, across, corner, dispatch, combine, params, params_part, mixed, grad_tokens, rows
+    slots, x_size, lead, middle, order, blocks, own, tokens, cotangent, across, corner, dispatch, combine, params, params_part, mixed, grad_tokens, rows
 ):
     half = lax.axis_index("x") * 2 + lax.axis_index("core")
     quarter = own.shape[2]
@@ -145,11 +145,11 @@
         grad_dispatch += dot(rows[1, :, pl.ds(start, quarter)], part[0][...], (1, 1))
     grad_logits = softmax_back(combine[...], grad_combine, 0) + softmax_back(dispatch[...], grad_dispatch, 1)
     partial = [dot(grad_logits.astype(BF16), part[0], (1, 0)) for part in (own, (tokens[...],))]
-    upper = lax.axis_index("core") == 1
-    for i, part in enumerate((jnp.where(upper, *partial), jnp.where(upper, *partial[::-1]))):
-        count = params_part.shape[0] // 2
-        part = outward(part, slots, lead).astype(BF16)
-        params_part[i * count : (i + 1) * count] = jnp.broadcast_to(part[None], (count, *part.shape))
+    partial = [outward(part, slots, lead).astype(BF16) for part in partial]
+    early = lax.axis_index("expert") < middle
+    sides = jnp.where(early, *partial), jnp.where(early, *partial[::-1])
+    for i, image in enumerate(order):
+        params_part[i] = sides[0 if image < middle else 1]
     here = pl.ds(pl.multiple_of(half * quarter, quarter), quarter)
     mixed[...] = dot(combine[...].astype(BF16), rows[0, :, here], (0, 0)).astype(BF16)
     token_term = dot(dispatch[...].astype(BF16), rows[1, :, here], (0, 0))
@@ -185,13 +185,12 @@
     table = (columns, seq)
     lead, middle = experts * 5 // 8, experts // 2
     order = [(lead + i) % experts for i in range(experts)]
-    near = [list(range(middle))[::-1], list(range(middle, experts))]
     wide = [
         [(expert * x_size + (x if core else 1 - x)) * 2 + core for core in (1, 0) for expert in order]
         for x in range(x_size)
     ]
     narrow = [
-        [(image * x_size + x) * 2 + core for core in (1, 0) for image in near[side if core else 1 - side]]
+        [(image * x_size + x) * 2 + (side if image < middle else 1 - side) for image in order]
         for x in range(x_size)
         for side in (0, 1)
     ]
@@ -250,7 +249,7 @@
     blocks, corner = lax.optimization_barrier((blocks, corner))
     blocks = lax.all_to_all(blocks, axes, 0, 0, tiled=True, axis_index_groups=wide)
     params_part, mixed, grad_tokens = call(
-        functools.partial(image_kernel, slots, x_size, lead),
+        functools.partial(image_kernel, slots, x_size, lead, middle, order),
         [((experts, columns, quarter), BF16), pltpu.VMEM((seq, quarter), BF16), pltpu.VMEM((seq, quarter), BF16)],
         blocks,
         own,

time: 43.3 us -> 42.6 us (0.984)
  blocking collectives: 28.9 us -> 28.1 us
    all_to_all x1, blocking collectives: 8.52 us -> 7.68 us  [local(): lax.all_to_all(params_part, axes, 0, 0, tiled=True, axis_index_groups=nar...]
where the time goes in v6:
time: 42.6 us; the launch traced here: 42.2 us
  blocking collectives  28.1 us (66%)
  Pallas kernels  6.99 us (16%)
  starting transfers between devices  5.38 us (13%)
  waiting for transfers between devices  1.05 us (2%)
  between operations  0.7 us (2%)
    all_to_all x2, blocking collectives, local(): lax.all_to_all(blocks, axes, 0, 0, tiled=True, axis_index_groups=wide)  20.4 us
    all_to_all x1, blocking collectives, local(): lax.all_to_all(params_part, axes, 0, 0, tiled=True, axis_index_groups=nar...  7.68 us
    pallas_call x8, Pallas kernels, call(): run(*(pltpu.with_memory_space_constraint(arg, pltpu.HBM) if i in in_hbm e...  6.99 us
    ppermute x7, starting transfers between devices, swap(): return lax.ppermute(array, axis, [(0, 1), (1, 0)])  5.38 us
    ppermute x7, waiting for transfers between devices, swap(): return lax.ppermute(array, axis, [(0, 1), (1, 0)])  1.05 us
  transfers between devices with their start and end apart: 7, of which 1 were waited for; matrix products, arithmetic and copies ran while one was open for 0% of the time, Pallas kernels for 13%

profile of v6, /device:TPU:0, one launch (start us, length us, event | category | flops | bytes accessed | tf_op | source)
XLA Modules:
  0.0 42.2 jit_solution(7717479173766509777)
XLA Ops:
  0.6 0.5 %collective-permute-start = (bf16[196,256]{1,0:T(8,128)(2,1)}, bf16[196,256]{1,0:T(8,128)(2,1)S(1)}, u32[]{:S(2)}, u32[]{:S(2)}) collective-permute-start(bf16[196,256]{1,0:T(8,128)(2,1)} %tokens.1), channel_id=1, source_target_pairs={{0,1},{1,0},{2,3},{3,2},{4,5},{5,4},{6,7},{7,6},{8,9},{9,8},{10,11... | collective-permute-start | bytes 301064 | tf_op jit(solution)/shard_map/ppermute | solution.py:16
  1.1 0.1 collective-permute-start.3
  1.2 0.4 %collective-permute-start.1 = (bf16[16,256]{1,0:T(8,128)(2,1)}, bf16[16,256]{1,0:T(8,128)(2,1)S(1)}, u32[]{:S(2)}, u32[]{:S(2)}) collective-permute-start(bf16[16,256]{1,0:T(8,128)(2,1)} %bitcast.2), channel_id=1, source_target_pairs={{0,1},{1,0},{2,3},{3,2},{4,5},{5,4},{6,7},{7,6},{8,9},{9,8},{10,11... | collective-permute-start | bytes 24584 | tf_op jit(solution)/shard_map/ppermute | solution.py:16
  1.7 1.1 %shard_map.76 = (bf16[2,196,256]{2,1,0:T(8,128)(2,1)S(1)}, bf16[16,256]{1,0:T(8,128)(2,1)S(1)}, f32[16,196]{1,0:T(8,128)S(1)}) custom-call(bf16[196,256]{1,0:T(8,128)(2,1)} %tokens.1, bf16[196,256]{1,0:T(8,128)(2,1)} %cotangent.1, bf16[16,256]{1,0:T(8,128)(2,1)} %bitcast.3), custom_call_target="tpu_custom_call" | custom-call | tf_op jit(solution)/shard_map/pallas_call | solution.py:176
  2.8 0.0 collective-permute-done.1.params
  2.8 0.0 collective-permute-done.tokens
  2.8 0.1 shard_map.77.after.first
  2.9 2.8 %collective-permute-start.2 = (f32[16,196]{1,0:T(8,128)S(1)}, f32[16,196]{1,0:T(8,128)S(1)}, u32[]{:S(2)}, u32[]{:S(2)}) collective-permute-start(f32[16,196]{1,0:T(8,128)S(1)} %shard_map.77.after.first), channel_id=1, source_target_pairs={{0,2},{2,0},{1,3},{3,1},{4,6},{6,4},{5,7},{7,5},{8,10},{10,8},{9,1... | collective-permute-start | bytes 37640 | tf_op jit(solution)/shard_map/ppermute | solution.py:16
  5.7 2.7 %shard_map.78 = (bf16[1024,1024]{1,0:T(8,128)(2,1)S(1)}, bf16[1024,1024]{1,0:T(8,128)(2,1)S(1)}, bf16[1024,1024]{1,0:T(8,128)(2,1)S(1)}, bf16[1024,1024]{1,0:T(8,128)(2,1)S(1)}) custom-call(f32[16,196]{1,0:T(8,128)S(1)} %shard_map.77.after.first, bf16[1,1024,1024]{2,1,0:T(8,128)(2,1)} %up_matrix.1, bf16[1,1024,1024]{2,1,0:T(8,128)(2,1)} %down_matrix.1), custom_call_target="tpu_custom_call" | custom-call | tf_op jit(solution)/shard_map/pallas_call | solution.py:176
  8.4 0.0 collective-permute-done.2.second
  8.4 1.1 %collective-permute-start.4 = (bf16[2,196,256]{2,1,0:T(8,128)(2,1)S(1)}, bf16[2,196,256]{2,1,0:T(8,128)(2,1)S(1)}, u32[]{:S(2)}, u32[]{:S(2)}) collective-permute-start(bf16[2,196,256]{2,1,0:T(8,128)(2,1)S(1)} %get-tuple-element.41.own), channel_id=1, source_target_pairs={{0,2},{2,0},{1,3},{3,1},{4,6},{6,4},{5,7},{7,5},{8,10},{10,8},{9,1... | collective-permute-start | bytes 602120 | tf_op jit(solution)/shard_map/ppermute | solution.py:16
  9.4 0.0 collective-permute-done.3.cotangent
  9.4 0.3 shard_map.79
  9.8 10.6 %all_to_all.15.blocks = bf16[16,4,512]{2,1,0:T(4,128)(2,1)S(1)} all-to-all(bf16[16,4,512]{2,1,0:T(4,128)(2,1)S(1)} %get-tuple-element.36), channel_id=1, replica_groups={{21,25,29,1,5,9,13,17,22,26,30,2,6,10,14,18},{23,27,31,3,7,11,15,19,20,..., dimensions={0} | all-to-all | bytes 131072 | tf_op jit(solution)/shard_map/all_to_all | solution.py:235
  20.4 1.2 %shard_map.80.first = bf16[2,16,1024]{2,1,0:T(8,128)(2,1)S(1)} custom-call(bf16[16,4,512]{2,1,0:T(4,128)(2,1)S(1)} %all_to_all.15.blocks, bf16[1024,1024]{1,0:T(8,128)(2,1)S(1)} %get-tuple-element.37.up_matrix, bf16[1024,1024]{1,0:T(8,128)(2,1)S(1)} %get-tuple-element.38.down_matrix, bf16[1024,1024]{1,0:T(8,128)(2,1)S(1)} %get-tuple-element.39.up_turned, ...), custom_call_target="tpu_custom_call" | custom-call | tf_op jit(solution)/shard_map/pallas_call | solution.py:176
  21.6 0.0 collective-permute-done.4.across
  21.6 0.2 collective-permute-start.6
  21.7 0.4 collective-permute-start.5
  22.1 1.0 %collective-permute-done.5.second = bf16[2,16,1024]{2,1,0:T(8,128)(2,1)S(1)} collective-permute-done((bf16[2,16,1024]{2,1,0:T(8,128)(2,1)S(1)}, bf16[2,16,1024]{2,1,0:T(8,128)(2,1)S(1)}, u32[]{:S(2)}, u32[]{:S(2)}) %collective-permute-start.5) | collective-permute-done | bytes 65568 | tf_op jit(solution)/shard_map/ppermute | solution.py:16
  23.1 0.1 shard_map.81
  23.2 0.0 collective-permute-done.6.corner
  23.2 9.8 %all_to_all.16.blocks = bf16[16,4,1024]{2,1,0:T(4,128)(2,1)S(1)} all-to-all(bf16[16,4,1024]{2,1,0:T(4,128)(2,1)S(1)} %shard_map.81), channel_id=1, replica_groups={{21,25,29,1,5,9,13,17,22,26,30,2,6,10,14,18},{23,27,31,3,7,11,15,19,20,..., dimensions={0} | all-to-all | bytes 262144 | tf_op jit(solution)/shard_map/all_to_all | solution.py:250
  33.1 0.7 %shard_map.82 = (bf16[8,16,256]{2,1,0:T(8,128)(2,1)S(1)}, bf16[196,256]{1,0:T(8,128)(2,1)S(1)}, bf16[196,256]{1,0:T(8,128)(2,1)S(1)}) custom-call(bf16[16,4,1024]{2,1,0:T(4,128)(2,1)S(1)} %all_to_all.16.blocks, bf16[2,196,256]{2,1,0:T(8,128)(2,1)S(1)} %get-tuple-element.41.own, bf16[196,256]{1,0:T(8,128)(2,1)S(1)} %collective-permute-done.tokens, ...), custom_call_target="tpu_custom_call" | custom-call | tf_op jit(solution)/shard_map/pallas_call | solution.py:176
  33.8 7.7 %all_to_all.17.parts = bf16[8,16,256]{2,1,0:T(8,128)(2,1)S(1)} all-to-all(bf16[8,16,256]{2,1,0:T(8,128)(2,1)S(1)} %get-tuple-element.49), channel_id=1, replica_groups={{21,25,29,0,4,8,12,17},{20,24,28,1,5,9,13,16},{23,27,31,2,6,10,14,19},{..., dimensions={0} | all-to-all | bytes 131072 | tf_op jit(solution)/shard_map/all_to_all | solution.py:266
  41.5 0.7 %shard_map.83 = (bf16[196,256]{1,0:T(8,128)(2,1)}, bf16[196,256]{1,0:T(8,128)(2,1)}, f32[16,256]{1,0:T(8,128)}) custom-call(bf16[8,16,256]{2,1,0:T(8,128)(2,1)S(1)} %all_to_all.17.parts, bf16[196,256]{1,0:T(8,128)(2,1)S(1)} %get-tuple-element.50.mixed_here, bf16[196,256]{1,0:T(8,128)(2,1)S(1)} %get-tuple-element.51.grad_tokens_here), custom_call_target="tpu_custom_call" | custom-call | tf_op jit(solution)/shard_map/pallas_call | solution.py:176
Async XLA Ops:
  0.6 2.2 %collective-permute-start = (bf16[196,256]{1,0:T(8,128)(2,1)}, bf16[196,256]{1,0:T(8,128)(2,1)S(1)}, u32[]{:S(2)}, u32[]{:S(2)}) collective-permute-start(bf16[196,256]{1,0:T(8,128)(2,1)} %tokens.1), channel_id=1, source_target_pairs={{0,1},{1,0},{2,3},{3,2},{4,5},{5,4},{6,7},{7,6},{8,9},{9,8},{10,11... | collective-permute-start | bytes 301064 | tf_op jit(solution)/shard_map/ppermute | solution.py:16
  1.1 8.3 %collective-permute-start.3 = (bf16[196,256]{1,0:T(8,128)(2,1)}, bf16[196,256]{1,0:T(8,128)(2,1)S(1)}, u32[]{:S(2)}, u32[]{:S(2)}) collective-permute-start(bf16[196,256]{1,0:T(8,128)(2,1)} %cotangent.1), channel_id=1, source_target_pairs={{0,1},{1,0},{2,3},{3,2},{4,5},{5,4},{6,7},{7,6},{8,9},{9,8},{10,11... | collective-permute-start | bytes 301064 | tf_op jit(solution)/shard_map/ppermute | solution.py:16
  1.2 1.6 %collective-permute-start.1 = (bf16[16,256]{1,0:T(8,128)(2,1)}, bf16[16,256]{1,0:T(8,128)(2,1)S(1)}, u32[]{:S(2)}, u32[]{:S(2)}) collective-permute-start(bf16[16,256]{1,0:T(8,128)(2,1)} %bitcast.2), channel_id=1, source_target_pairs={{0,1},{1,0},{2,3},{3,2},{4,5},{5,4},{6,7},{7,6},{8,9},{9,8},{10,11... | collective-permute-start | bytes 24584 | tf_op jit(solution)/shard_map/ppermute | solution.py:16
  2.9 5.4 %collective-permute-start.2 = (f32[16,196]{1,0:T(8,128)S(1)}, f32[16,196]{1,0:T(8,128)S(1)}, u32[]{:S(2)}, u32[]{:S(2)}) collective-permute-start(f32[16,196]{1,0:T(8,128)S(1)} %shard_map.77.after.first), channel_id=1, source_target_pairs={{0,2},{2,0},{1,3},{3,1},{4,6},{6,4},{5,7},{7,5},{8,10},{10,8},{9,1... | collective-permute-start | bytes 37640 | tf_op jit(solution)/shard_map/ppermute | solution.py:16
  8.4 13.2 %collective-permute-start.4 = (bf16[2,196,256]{2,1,0:T(8,128)(2,1)S(1)}, bf16[2,196,256]{2,1,0:T(8,128)(2,1)S(1)}, u32[]{:S(2)}, u32[]{:S(2)}) collective-permute-start(bf16[2,196,256]{2,1,0:T(8,128)(2,1)S(1)} %get-tuple-element.41.own), channel_id=1, source_target_pairs={{0,2},{2,0},{1,3},{3,1},{4,6},{6,4},{5,7},{7,5},{8,10},{10,8},{9,1... | collective-permute-start | bytes 602120 | tf_op jit(solution)/shard_map/ppermute | solution.py:16
  21.6 1.7 %collective-permute-start.6 = (bf16[2,196,256]{2,1,0:T(8,128)(2,1)S(1)}, bf16[2,196,256]{2,1,0:T(8,128)(2,1)S(1)}, u32[]{:S(2)}, u32[]{:S(2)}) collective-permute-start(bf16[2,196,256]{2,1,0:T(8,128)(2,1)S(1)} %collective-permute-done.4.across), channel_id=1, source_target_pairs={{0,1},{1,0},{2,3},{3,2},{4,5},{5,4},{6,7},{7,6},{8,9},{9,8},{10,11... | collective-permute-start | bytes 602120 | tf_op jit(solution)/shard_map/ppermute | solution.py:16
  21.7 1.4 %collective-permute-start.5 = (bf16[2,16,1024]{2,1,0:T(8,128)(2,1)S(1)}, bf16[2,16,1024]{2,1,0:T(8,128)(2,1)S(1)}, u32[]{:S(2)}, u32[]{:S(2)}) collective-permute-start(bf16[2,16,1024]{2,1,0:T(8,128)(2,1)S(1)} %shard_map.80.first), channel_id=1, source_target_pairs={{0,1},{1,0},{2,3},{3,2},{4,5},{5,4},{6,7},{7,6},{8,9},{9,8},{10,11... | collective-permute-start | bytes 196616 | tf_op jit(solution)/shard_map/ppermute | solution.py:16

commit v7 on v6

--- a/solution.py
+++ b/solution.py
@@ -14,6 +14,10 @@
 
 def swap(array, axis):
     return lax.ppermute(array, axis, [(0, 1), (1, 0)])
+
+
+def cross(array):
+    return lax.ppermute(array, ("x", "core"), [(0, 3), (1, 2), (2, 1), (3, 0)])
 
 
 def dot(left, right, over):
@@ -139,7 +143,7 @@
     rows[0] = slot_out.astype(BF16)
     rows[1] = grad_in.astype(BF16)
     grad_combine = grad_dispatch = 0.0
-    for offset, part in enumerate((own, (tokens, cotangent), across, corner)):
+    for offset, part in enumerate((own, (tokens, cotangent), corner, across)):
         start = pl.multiple_of(jnp.bitwise_xor(half, offset) * quarter, quarter)
         grad_combine += dot(rows[0, :, pl.ds(start, quarter)], part[1][...], (1, 1))
         grad_dispatch += dot(rows[1, :, pl.ds(start, quarter)], part[0][...], (1, 1))
@@ -209,7 +213,7 @@
     (logits,) = call(
         functools.partial(add_kernel, slots, lead), [(table, F32)], logits, beside[0], swap(slot_params.T, "core")
     )
-    other = swap(logits, "x")
+    other = cross(logits)
     chunks = 2
     shapes = [w_up.shape[1:], w_down.shape[1:], w_up.shape[:0:-1], w_down.shape[:0:-1]]
     weights = call(
@@ -222,7 +226,7 @@
         in_hbm=(1, 2),
     )
     other, own_later, *weights = lax.optimization_barrier((other, own, *weights))
-    across = swap(own_later, "x")
+    across = cross(own_later)
     blocks, dispatch, combine = call(
         functools.partial(slot_kernel, slots, x_size),
         [((x_size * experts, 2 * slots, 2 * quarter), BF16), (table, F32), (table, F32)],

time: 42.6 us -> 42.4 us (level)
  starting transfers between devices: 5.38 us -> 4.81 us
    ppermute x7 -> x5, starting transfers between devices: 5.38 us -> 1.69 us  [swap(): return lax.ppermute(array, axis, [(0, 1), (1, 0)])]
    ppermute x0 -> x2, starting transfers between devices: none -> 3.12 us  [cross(): return lax.ppermute(array, ('x', 'core'), [(0, 3), (1, 2), (2, 1), (3, 0)])]
    ppermute x7 -> x5, waiting for transfers between devices: 1.05 us -> 1.2 us  [swap(): return lax.ppermute(array, axis, [(0, 1), (1, 0)])]
where the time goes in v7:
time: 42.4 us; the launch traced here: 41.9 us
  blocking collectives  28.2 us (67%)
  Pallas kernels  7 us (17%)
  starting transfers between devices  4.81 us (11%)
  waiting for transfers between devices  1.2 us (3%)
  between operations  0.7 us (2%)
    all_to_all x2, blocking collectives, local(): lax.all_to_all(blocks, axes, 0, 0, tiled=True, axis_index_groups=wide)  20.5 us
    all_to_all x1, blocking collectives, local(): lax.all_to_all(params_part, axes, 0, 0, tiled=True, axis_index_groups=nar...  7.68 us
    pallas_call x8, Pallas kernels, call(): run(*(pltpu.with_memory_space_constraint(arg, pltpu.HBM) if i in in_hbm e...  7 us
    ppermute x2, starting transfers between devices, cross(): return lax.ppermute(array, ('x', 'core'), [(0, 3), (1, 2), (2, 1), (3, 0)])  3.12 us
    ppermute x5, starting transfers between devices, swap(): return lax.ppermute(array, axis, [(0, 1), (1, 0)])  1.69 us
    ppermute x5, waiting for transfers between devices, swap(): return lax.ppermute(array, axis, [(0, 1), (1, 0)])  1.2 us
  transfers between devices with their start and end apart: 7, of which 1 were waited for; matrix products, arithmetic and copies ran while one was open for 0% of the time, Pallas kernels for 13%

profile of v7, /device:TPU:0, one launch (start us, length us, event | category | flops | bytes accessed | tf_op | source)
XLA Modules:
  0.0 41.9 jit_solution(10898779867465310959)
XLA Ops:
  0.6 0.5 %collective-permute-start = (bf16[196,256]{1,0:T(8,128)(2,1)}, bf16[196,256]{1,0:T(8,128)(2,1)S(1)}, u32[]{:S(2)}, u32[]{:S(2)}) collective-permute-start(bf16[196,256]{1,0:T(8,128)(2,1)} %tokens.1), channel_id=1, source_target_pairs={{0,1},{1,0},{2,3},{3,2},{4,5},{5,4},{6,7},{7,6},{8,9},{9,8},{10,11... | collective-permute-start | bytes 301064 | tf_op jit(solution)/shard_map/ppermute | solution.py:16
  1.1 0.1 collective-permute-start.3
  1.2 0.4 %collective-permute-start.1 = (bf16[16,256]{1,0:T(8,128)(2,1)}, bf16[16,256]{1,0:T(8,128)(2,1)S(1)}, u32[]{:S(2)}, u32[]{:S(2)}) collective-permute-start(bf16[16,256]{1,0:T(8,128)(2,1)} %bitcast.2), channel_id=1, source_target_pairs={{0,1},{1,0},{2,3},{3,2},{4,5},{5,4},{6,7},{7,6},{8,9},{9,8},{10,11... | collective-permute-start | bytes 24584 | tf_op jit(solution)/shard_map/ppermute | solution.py:16
  1.7 1.1 %shard_map.76 = (bf16[2,196,256]{2,1,0:T(8,128)(2,1)S(1)}, bf16[16,256]{1,0:T(8,128)(2,1)S(1)}, f32[16,196]{1,0:T(8,128)S(1)}) custom-call(bf16[196,256]{1,0:T(8,128)(2,1)} %tokens.1, bf16[196,256]{1,0:T(8,128)(2,1)} %cotangent.1, bf16[16,256]{1,0:T(8,128)(2,1)} %bitcast.3), custom_call_target="tpu_custom_call" | custom-call | tf_op jit(solution)/shard_map/pallas_call | solution.py:180
  2.8 0.0 collective-permute-done.1.params
  2.8 0.0 collective-permute-done.tokens
  2.8 0.1 shard_map.77.after.first
  2.9 2.6 %collective-permute-start.2 = (f32[16,196]{1,0:T(8,128)S(1)}, f32[16,196]{1,0:T(8,128)S(1)}, u32[]{:S(2)}, u32[]{:S(2)}) collective-permute-start(f32[16,196]{1,0:T(8,128)S(1)} %shard_map.77.after.first), channel_id=1, source_target_pairs={{0,3},{1,2},{2,1},{3,0},{4,7},{5,6},{6,5},{7,4},{8,11},{9,10},{10,... | collective-permute-start | bytes 37640 | tf_op jit(solution)/shard_map/ppermute | solution.py:20
  5.6 2.7 %shard_map.78 = (bf16[1024,1024]{1,0:T(8,128)(2,1)S(1)}, bf16[1024,1024]{1,0:T(8,128)(2,1)S(1)}, bf16[1024,1024]{1,0:T(8,128)(2,1)S(1)}, bf16[1024,1024]{1,0:T(8,128)(2,1)S(1)}) custom-call(f32[16,196]{1,0:T(8,128)S(1)} %shard_map.77.after.first, bf16[1,1024,1024]{2,1,0:T(8,128)(2,1)} %up_matrix.1, bf16[1,1024,1024]{2,1,0:T(8,128)(2,1)} %down_matrix.1), custom_call_target="tpu_custom_call" | custom-call | tf_op jit(solution)/shard_map/pallas_call | solution.py:180
  8.2 0.0 collective-permute-done.2.second
  8.2 0.5 %collective-permute-start.4 = (bf16[2,196,256]{2,1,0:T(8,128)(2,1)S(1)}, bf16[2,196,256]{2,1,0:T(8,128)(2,1)S(1)}, u32[]{:S(2)}, u32[]{:S(2)}) collective-permute-start(bf16[2,196,256]{2,1,0:T(8,128)(2,1)S(1)} %get-tuple-element.41.own), channel_id=1, source_target_pairs={{0,3},{1,2},{2,1},{3,0},{4,7},{5,6},{6,5},{7,4},{8,11},{9,10},{10,... | collective-permute-start | bytes 602120 | tf_op jit(solution)/shard_map/ppermute | solution.py:20
  8.7 0.0 collective-permute-done.3.cotangent
  8.7 0.3 shard_map.79
  9.1 10.6 %all_to_all.15.blocks = bf16[16,4,512]{2,1,0:T(4,128)(2,1)S(1)} all-to-all(bf16[16,4,512]{2,1,0:T(4,128)(2,1)S(1)} %get-tuple-element.36), channel_id=1, replica_groups={{21,25,29,1,5,9,13,17,22,26,30,2,6,10,14,18},{23,27,31,3,7,11,15,19,20,..., dimensions={0} | all-to-all | bytes 131072 | tf_op jit(solution)/shard_map/all_to_all | solution.py:239
  19.6 1.2 %shard_map.80.first = bf16[2,16,1024]{2,1,0:T(8,128)(2,1)S(1)} custom-call(bf16[16,4,512]{2,1,0:T(4,128)(2,1)S(1)} %all_to_all.15.blocks, bf16[1024,1024]{1,0:T(8,128)(2,1)S(1)} %get-tuple-element.37.up_matrix, bf16[1024,1024]{1,0:T(8,128)(2,1)S(1)} %get-tuple-element.38.down_matrix, bf16[1024,1024]{1,0:T(8,128)(2,1)S(1)} %get-tuple-element.39.up_turned, ...), custom_call_target="tpu_custom_call" | custom-call | tf_op jit(solution)/shard_map/pallas_call | solution.py:180
  20.8 0.0 collective-permute-done.4.across
  20.9 0.6 %collective-permute-start.6 = (bf16[2,196,256]{2,1,0:T(8,128)(2,1)S(1)}, bf16[2,196,256]{2,1,0:T(8,128)(2,1)S(1)}, u32[]{:S(2)}, u32[]{:S(2)}) collective-permute-start(bf16[2,196,256]{2,1,0:T(8,128)(2,1)S(1)} %collective-permute-done.4.across), channel_id=1, source_target_pairs={{0,1},{1,0},{2,3},{3,2},{4,5},{5,4},{6,7},{7,6},{8,9},{9,8},{10,11... | collective-permute-start | bytes 602120 | tf_op jit(solution)/shard_map/ppermute | solution.py:16
  21.4 0.1 collective-permute-start.5
  21.5 1.2 %collective-permute-done.5.second = bf16[2,16,1024]{2,1,0:T(8,128)(2,1)S(1)} collective-permute-done((bf16[2,16,1024]{2,1,0:T(8,128)(2,1)S(1)}, bf16[2,16,1024]{2,1,0:T(8,128)(2,1)S(1)}, u32[]{:S(2)}, u32[]{:S(2)}) %collective-permute-start.5) | collective-permute-done | bytes 65568 | tf_op jit(solution)/shard_map/ppermute | solution.py:16
  22.7 0.1 shard_map.81
  22.8 0.0 collective-permute-done.6.corner
  22.8 10.0 %all_to_all.16.blocks = bf16[16,4,1024]{2,1,0:T(4,128)(2,1)S(1)} all-to-all(bf16[16,4,1024]{2,1,0:T(4,128)(2,1)S(1)} %shard_map.81), channel_id=1, replica_groups={{21,25,29,1,5,9,13,17,22,26,30,2,6,10,14,18},{23,27,31,3,7,11,15,19,20,..., dimensions={0} | all-to-all | bytes 262144 | tf_op jit(solution)/shard_map/all_to_all | solution.py:254
  32.8 0.7 %shard_map.82 = (bf16[8,16,256]{2,1,0:T(8,128)(2,1)S(1)}, bf16[196,256]{1,0:T(8,128)(2,1)S(1)}, bf16[196,256]{1,0:T(8,128)(2,1)S(1)}) custom-call(bf16[16,4,1024]{2,1,0:T(4,128)(2,1)S(1)} %all_to_all.16.blocks, bf16[2,196,256]{2,1,0:T(8,128)(2,1)S(1)} %get-tuple-element.41.own, bf16[196,256]{1,0:T(8,128)(2,1)S(1)} %collective-permute-done.tokens, ...), custom_call_target="tpu_custom_call" | custom-call | tf_op jit(solution)/shard_map/pallas_call | solution.py:180
  33.5 7.7 %all_to_all.17.parts = bf16[8,16,256]{2,1,0:T(8,128)(2,1)S(1)} all-to-all(bf16[8,16,256]{2,1,0:T(8,128)(2,1)S(1)} %get-tuple-element.49), channel_id=1, replica_groups={{21,25,29,0,4,8,12,17},{20,24,28,1,5,9,13,16},{23,27,31,2,6,10,14,19},{..., dimensions={0} | all-to-all | bytes 131072 | tf_op jit(solution)/shard_map/all_to_all | solution.py:270
  41.2 0.7 %shard_map.83 = (bf16[196,256]{1,0:T(8,128)(2,1)}, bf16[196,256]{1,0:T(8,128)(2,1)}, f32[16,256]{1,0:T(8,128)}) custom-call(bf16[8,16,256]{2,1,0:T(8,128)(2,1)S(1)} %all_to_all.17.parts, bf16[196,256]{1,0:T(8,128)(2,1)S(1)} %get-tuple-element.50.mixed_here, bf16[196,256]{1,0:T(8,128)(2,1)S(1)} %get-tuple-element.51.grad_tokens_here), custom_call_target="tpu_custom_call" | custom-call | tf_op jit(solution)/shard_map/pallas_call | solution.py:180
Async XLA Ops:
  0.6 2.2 %collective-permute-start = (bf16[196,256]{1,0:T(8,128)(2,1)}, bf16[196,256]{1,0:T(8,128)(2,1)S(1)}, u32[]{:S(2)}, u32[]{:S(2)}) collective-permute-start(bf16[196,256]{1,0:T(8,128)(2,1)} %tokens.1), channel_id=1, source_target_pairs={{0,1},{1,0},{2,3},{3,2},{4,5},{5,4},{6,7},{7,6},{8,9},{9,8},{10,11... | collective-permute-start | bytes 301064 | tf_op jit(solution)/shard_map/ppermute | solution.py:16
  1.1 7.6 %collective-permute-start.3 = (bf16[196,256]{1,0:T(8,128)(2,1)}, bf16[196,256]{1,0:T(8,128)(2,1)S(1)}, u32[]{:S(2)}, u32[]{:S(2)}) collective-permute-start(bf16[196,256]{1,0:T(8,128)(2,1)} %cotangent.1), channel_id=1, source_target_pairs={{0,1},{1,0},{2,3},{3,2},{4,5},{5,4},{6,7},{7,6},{8,9},{9,8},{10,11... | collective-permute-start | bytes 301064 | tf_op jit(solution)/shard_map/ppermute | solution.py:16
  1.2 1.6 %collective-permute-start.1 = (bf16[16,256]{1,0:T(8,128)(2,1)}, bf16[16,256]{1,0:T(8,128)(2,1)S(1)}, u32[]{:S(2)}, u32[]{:S(2)}) collective-permute-start(bf16[16,256]{1,0:T(8,128)(2,1)} %bitcast.2), channel_id=1, source_target_pairs={{0,1},{1,0},{2,3},{3,2},{4,5},{5,4},{6,7},{7,6},{8,9},{9,8},{10,11... | collective-permute-start | bytes 24584 | tf_op jit(solution)/shard_map/ppermute | solution.py:16
  2.9 5.3 %collective-permute-start.2 = (f32[16,196]{1,0:T(8,128)S(1)}, f32[16,196]{1,0:T(8,128)S(1)}, u32[]{:S(2)}, u32[]{:S(2)}) collective-permute-start(f32[16,196]{1,0:T(8,128)S(1)} %shard_map.77.after.first), channel_id=1, source_target_pairs={{0,3},{1,2},{2,1},{3,0},{4,7},{5,6},{6,5},{7,4},{8,11},{9,10},{10,... | collective-permute-start | bytes 37640 | tf_op jit(solution)/shard_map/ppermute | solution.py:20
  8.2 12.6 %collective-permute-start.4 = (bf16[2,196,256]{2,1,0:T(8,128)(2,1)S(1)}, bf16[2,196,256]{2,1,0:T(8,128)(2,1)S(1)}, u32[]{:S(2)}, u32[]{:S(2)}) collective-permute-start(bf16[2,196,256]{2,1,0:T(8,128)(2,1)S(1)} %get-tuple-element.41.own), channel_id=1, source_target_pairs={{0,3},{1,2},{2,1},{3,0},{4,7},{5,6},{6,5},{7,4},{8,11},{9,10},{10,... | collective-permute-start | bytes 602120 | tf_op jit(solution)/shard_map/ppermute | solution.py:20
  20.9 2.0 %collective-permute-start.6 = (bf16[2,196,256]{2,1,0:T(8,128)(2,1)S(1)}, bf16[2,196,256]{2,1,0:T(8,128)(2,1)S(1)}, u32[]{:S(2)}, u32[]{:S(2)}) collective-permute-start(bf16[2,196,256]{2,1,0:T(8,128)(2,1)S(1)} %collective-permute-done.4.across), channel_id=1, source_target_pairs={{0,1},{1,0},{2,3},{3,2},{4,5},{5,4},{6,7},{7,6},{8,9},{9,8},{10,11... | collective-permute-start | bytes 602120 | tf_op jit(solution)/shard_map/ppermute | solution.py:16
  21.4 1.3 %collective-permute-start.5 = (bf16[2,16,1024]{2,1,0:T(8,128)(2,1)S(1)}, bf16[2,16,1024]{2,1,0:T(8,128)(2,1)S(1)}, u32[]{:S(2)}, u32[]{:S(2)}) collective-permute-start(bf16[2,16,1024]{2,1,0:T(8,128)(2,1)S(1)} %shard_map.80.first), channel_id=1, source_target_pairs={{0,1},{1,0},{2,3},{3,2},{4,5},{5,4},{6,7},{7,6},{8,9},{9,8},{10,11... | collective-permute-start | bytes 196616 | tf_op jit(solution)/shard_map/ppermute | solution.py:16

commit v8 on v7

--- a/solution.py
+++ b/solution.py
@@ -189,12 +189,13 @@
     table = (columns, seq)
     lead, middle = experts * 5 // 8, experts // 2
     order = [(lead + i) % experts for i in range(experts)]
+    near = [lead] + [i for i in range(experts) if i != lead]
     wide = [
         [(expert * x_size + (x if core else 1 - x)) * 2 + core for core in (1, 0) for expert in order]
         for x in range(x_size)
     ]
     narrow = [
-        [(image * x_size + x) * 2 + (side if image < middle else 1 - side) for image in order]
+        [(image * x_size + x) * 2 + (side if image < middle else 1 - side) for image in near]
         for x in range(x_size)
         for side in (0, 1)
     ]
@@ -253,7 +254,7 @@
     blocks, corner = lax.optimization_barrier((blocks, corner))
     blocks = lax.all_to_all(blocks, axes, 0, 0, tiled=True, axis_index_groups=wide)
     params_part, mixed, grad_tokens = call(
-        functools.partial(image_kernel, slots, x_size, lead, middle, order),
+        functools.partial(image_kernel, slots, x_size, lead, middle, near),
         [((experts, columns, quarter), BF16), pltpu.VMEM((seq, quarter), BF16), pltpu.VMEM((seq, quarter), BF16)],
         blocks,
         own,

time: 42.4 us -> 42.2 us (level)
  no operation moved by 1% of the time
where the time goes in v8:
time: 42.2 us; the launch traced here: 41.7 us
  blocking collectives  28 us (66%)
  Pallas kernels  7 us (17%)
  starting transfers between devices  4.81 us (11%)
  waiting for transfers between devices  1.2 us (3%)
  between operations  0.7 us (2%)
    all_to_all x2, blocking collectives, local(): lax.all_to_all(blocks, axes, 0, 0, tiled=True, axis_index_groups=wide)  20.5 us
    all_to_all x1, blocking collectives, local(): lax.all_to_all(params_part, axes, 0, 0, tiled=True, axis_index_groups=nar...  7.52 us
    pallas_call x8, Pallas kernels, call(): run(*(pltpu.with_memory_space_constraint(arg, pltpu.HBM) if i in in_hbm e...  7 us
    ppermute x2, starting transfers between devices, cross(): return lax.ppermute(array, ('x', 'core'), [(0, 3), (1, 2), (2, 1), (3, 0)])  3.12 us
    ppermute x5, starting transfers between devices, swap(): return lax.ppermute(array, axis, [(0, 1), (1, 0)])  1.69 us
    ppermute x5, waiting for transfers between devices, swap(): return lax.ppermute(array, axis, [(0, 1), (1, 0)])  1.2 us
  transfers between devices with their start and end apart: 7, of which 1 were waited for; matrix products, arithmetic and copies ran while one was open for 0% of the time, Pallas kernels for 13%

profile of v8, /device:TPU:0, one launch (start us, length us, event | category | flops | bytes accessed | tf_op | source)
XLA Modules:
  0.0 41.7 jit_solution(9177024616205967125)
XLA Ops:
  0.6 0.5 %collective-permute-start = (bf16[196,256]{1,0:T(8,128)(2,1)}, bf16[196,256]{1,0:T(8,128)(2,1)S(1)}, u32[]{:S(2)}, u32[]{:S(2)}) collective-permute-start(bf16[196,256]{1,0:T(8,128)(2,1)} %tokens.1), channel_id=1, source_target_pairs={{0,1},{1,0},{2,3},{3,2},{4,5},{5,4},{6,7},{7,6},{8,9},{9,8},{10,11... | collective-permute-start | bytes 301064 | tf_op jit(solution)/shard_map/ppermute | solution.py:16
  1.1 0.1 collective-permute-start.3
  1.2 0.4 %collective-permute-start.1 = (bf16[16,256]{1,0:T(8,128)(2,1)}, bf16[16,256]{1,0:T(8,128)(2,1)S(1)}, u32[]{:S(2)}, u32[]{:S(2)}) collective-permute-start(bf16[16,256]{1,0:T(8,128)(2,1)} %bitcast.2), channel_id=1, source_target_pairs={{0,1},{1,0},{2,3},{3,2},{4,5},{5,4},{6,7},{7,6},{8,9},{9,8},{10,11... | collective-permute-start | bytes 24584 | tf_op jit(solution)/shard_map/ppermute | solution.py:16
  1.7 1.1 %shard_map.76 = (bf16[2,196,256]{2,1,0:T(8,128)(2,1)S(1)}, bf16[16,256]{1,0:T(8,128)(2,1)S(1)}, f32[16,196]{1,0:T(8,128)S(1)}) custom-call(bf16[196,256]{1,0:T(8,128)(2,1)} %tokens.1, bf16[196,256]{1,0:T(8,128)(2,1)} %cotangent.1, bf16[16,256]{1,0:T(8,128)(2,1)} %bitcast.3), custom_call_target="tpu_custom_call" | custom-call | tf_op jit(solution)/shard_map/pallas_call | solution.py:180
  2.8 0.0 collective-permute-done.1.params
  2.8 0.0 collective-permute-done.tokens
  2.8 0.1 shard_map.77.after.first
  2.9 2.6 %collective-permute-start.2 = (f32[16,196]{1,0:T(8,128)S(1)}, f32[16,196]{1,0:T(8,128)S(1)}, u32[]{:S(2)}, u32[]{:S(2)}) collective-permute-start(f32[16,196]{1,0:T(8,128)S(1)} %shard_map.77.after.first), channel_id=1, source_target_pairs={{0,3},{1,2},{2,1},{3,0},{4,7},{5,6},{6,5},{7,4},{8,11},{9,10},{10,... | collective-permute-start | bytes 37640 | tf_op jit(solution)/shard_map/ppermute | solution.py:20
  5.6 2.7 %shard_map.78 = (bf16[1024,1024]{1,0:T(8,128)(2,1)S(1)}, bf16[1024,1024]{1,0:T(8,128)(2,1)S(1)}, bf16[1024,1024]{1,0:T(8,128)(2,1)S(1)}, bf16[1024,1024]{1,0:T(8,128)(2,1)S(1)}) custom-call(f32[16,196]{1,0:T(8,128)S(1)} %shard_map.77.after.first, bf16[1,1024,1024]{2,1,0:T(8,128)(2,1)} %up_matrix.1, bf16[1,1024,1024]{2,1,0:T(8,128)(2,1)} %down_matrix.1), custom_call_target="tpu_custom_call" | custom-call | tf_op jit(solution)/shard_map/pallas_call | solution.py:180
  8.2 0.0 collective-permute-done.2.second
  8.2 0.5 %collective-permute-start.4 = (bf16[2,196,256]{2,1,0:T(8,128)(2,1)S(1)}, bf16[2,196,256]{2,1,0:T(8,128)(2,1)S(1)}, u32[]{:S(2)}, u32[]{:S(2)}) collective-permute-start(bf16[2,196,256]{2,1,0:T(8,128)(2,1)S(1)} %get-tuple-element.41.own), channel_id=1, source_target_pairs={{0,3},{1,2},{2,1},{3,0},{4,7},{5,6},{6,5},{7,4},{8,11},{9,10},{10,... | collective-permute-start | bytes 602120 | tf_op jit(solution)/shard_map/ppermute | solution.py:20
  8.7 0.0 collective-permute-done.3.cotangent
  8.7 0.3 shard_map.79
  9.1 10.6 %all_to_all.15.blocks = bf16[16,4,512]{2,1,0:T(4,128)(2,1)S(1)} all-to-all(bf16[16,4,512]{2,1,0:T(4,128)(2,1)S(1)} %get-tuple-element.36), channel_id=1, replica_groups={{21,25,29,1,5,9,13,17,22,26,30,2,6,10,14,18},{23,27,31,3,7,11,15,19,20,..., dimensions={0} | all-to-all | bytes 131072 | tf_op jit(solution)/shard_map/all_to_all | solution.py:240
  19.6 1.2 %shard_map.80.first = bf16[2,16,1024]{2,1,0:T(8,128)(2,1)S(1)} custom-call(bf16[16,4,512]{2,1,0:T(4,128)(2,1)S(1)} %all_to_all.15.blocks, bf16[1024,1024]{1,0:T(8,128)(2,1)S(1)} %get-tuple-element.37.up_matrix, bf16[1024,1024]{1,0:T(8,128)(2,1)S(1)} %get-tuple-element.38.down_matrix, bf16[1024,1024]{1,0:T(8,128)(2,1)S(1)} %get-tuple-element.39.up_turned, ...), custom_call_target="tpu_custom_call" | custom-call | tf_op jit(solution)/shard_map/pallas_call | solution.py:180
  20.8 0.0 collective-permute-done.4.across
  20.9 0.6 %collective-permute-start.6 = (bf16[2,196,256]{2,1,0:T(8,128)(2,1)S(1)}, bf16[2,196,256]{2,1,0:T(8,128)(2,1)S(1)}, u32[]{:S(2)}, u32[]{:S(2)}) collective-permute-start(bf16[2,196,256]{2,1,0:T(8,128)(2,1)S(1)} %collective-permute-done.4.across), channel_id=1, source_target_pairs={{0,1},{1,0},{2,3},{3,2},{4,5},{5,4},{6,7},{7,6},{8,9},{9,8},{10,11... | collective-permute-start | bytes 602120 | tf_op jit(solution)/shard_map/ppermute | solution.py:16
  21.4 0.1 collective-permute-start.5
  21.5 1.2 %collective-permute-done.5.second = bf16[2,16,1024]{2,1,0:T(8,128)(2,1)S(1)} collective-permute-done((bf16[2,16,1024]{2,1,0:T(8,128)(2,1)S(1)}, bf16[2,16,1024]{2,1,0:T(8,128)(2,1)S(1)}, u32[]{:S(2)}, u32[]{:S(2)}) %collective-permute-start.5) | collective-permute-done | bytes 65568 | tf_op jit(solution)/shard_map/ppermute | solution.py:16
  22.7 0.1 shard_map.81
  22.8 0.0 collective-permute-done.6.corner
  22.8 10.0 %all_to_all.16.blocks = bf16[16,4,1024]{2,1,0:T(4,128)(2,1)S(1)} all-to-all(bf16[16,4,1024]{2,1,0:T(4,128)(2,1)S(1)} %shard_map.81), channel_id=1, replica_groups={{21,25,29,1,5,9,13,17,22,26,30,2,6,10,14,18},{23,27,31,3,7,11,15,19,20,..., dimensions={0} | all-to-all | bytes 262144 | tf_op jit(solution)/shard_map/all_to_all | solution.py:255
  32.8 0.7 %shard_map.82 = (bf16[8,16,256]{2,1,0:T(8,128)(2,1)S(1)}, bf16[196,256]{1,0:T(8,128)(2,1)S(1)}, bf16[196,256]{1,0:T(8,128)(2,1)S(1)}) custom-call(bf16[16,4,1024]{2,1,0:T(4,128)(2,1)S(1)} %all_to_all.16.blocks, bf16[2,196,256]{2,1,0:T(8,128)(2,1)S(1)} %get-tuple-element.41.own, bf16[196,256]{1,0:T(8,128)(2,1)S(1)} %collective-permute-done.tokens, ...), custom_call_target="tpu_custom_call" | custom-call | tf_op jit(solution)/shard_map/pallas_call | solution.py:180
  33.5 7.5 %all_to_all.17.parts = bf16[8,16,256]{2,1,0:T(8,128)(2,1)S(1)} all-to-all(bf16[8,16,256]{2,1,0:T(8,128)(2,1)S(1)} %get-tuple-element.49), channel_id=1, replica_groups={{21,0,4,8,12,17,25,29},{20,1,5,9,13,16,24,28},{23,2,6,10,14,19,27,31},{..., dimensions={0} | all-to-all | bytes 131072 | tf_op jit(solution)/shard_map/all_to_all | solution.py:271
  41.1 0.7 %shard_map.83 = (bf16[196,256]{1,0:T(8,128)(2,1)}, bf16[196,256]{1,0:T(8,128)(2,1)}, f32[16,256]{1,0:T(8,128)}) custom-call(bf16[8,16,256]{2,1,0:T(8,128)(2,1)S(1)} %all_to_all.17.parts, bf16[196,256]{1,0:T(8,128)(2,1)S(1)} %get-tuple-element.50.mixed_here, bf16[196,256]{1,0:T(8,128)(2,1)S(1)} %get-tuple-element.51.grad_tokens_here), custom_call_target="tpu_custom_call" | custom-call | tf_op jit(solution)/shard_map/pallas_call | solution.py:180
Async XLA Ops:
  0.6 2.2 %collective-permute-start = (bf16[196,256]{1,0:T(8,128)(2,1)}, bf16[196,256]{1,0:T(8,128)(2,1)S(1)}, u32[]{:S(2)}, u32[]{:S(2)}) collective-permute-start(bf16[196,256]{1,0:T(8,128)(2,1)} %tokens.1), channel_id=1, source_target_pairs={{0,1},{1,0},{2,3},{3,2},{4,5},{5,4},{6,7},{7,6},{8,9},{9,8},{10,11... | collective-permute-start | bytes 301064 | tf_op jit(solution)/shard_map/ppermute | solution.py:16
  1.1 7.6 %collective-permute-start.3 = (bf16[196,256]{1,0:T(8,128)(2,1)}, bf16[196,256]{1,0:T(8,128)(2,1)S(1)}, u32[]{:S(2)}, u32[]{:S(2)}) collective-permute-start(bf16[196,256]{1,0:T(8,128)(2,1)} %cotangent.1), channel_id=1, source_target_pairs={{0,1},{1,0},{2,3},{3,2},{4,5},{5,4},{6,7},{7,6},{8,9},{9,8},{10,11... | collective-permute-start | bytes 301064 | tf_op jit(solution)/shard_map/ppermute | solution.py:16
  1.2 1.6 %collective-permute-start.1 = (bf16[16,256]{1,0:T(8,128)(2,1)}, bf16[16,256]{1,0:T(8,128)(2,1)S(1)}, u32[]{:S(2)}, u32[]{:S(2)}) collective-permute-start(bf16[16,256]{1,0:T(8,128)(2,1)} %bitcast.2), channel_id=1, source_target_pairs={{0,1},{1,0},{2,3},{3,2},{4,5},{5,4},{6,7},{7,6},{8,9},{9,8},{10,11... | collective-permute-start | bytes 24584 | tf_op jit(solution)/shard_map/ppermute | solution.py:16
  2.9 5.3 %collective-permute-start.2 = (f32[16,196]{1,0:T(8,128)S(1)}, f32[16,196]{1,0:T(8,128)S(1)}, u32[]{:S(2)}, u32[]{:S(2)}) collective-permute-start(f32[16,196]{1,0:T(8,128)S(1)} %shard_map.77.after.first), channel_id=1, source_target_pairs={{0,3},{1,2},{2,1},{3,0},{4,7},{5,6},{6,5},{7,4},{8,11},{9,10},{10,... | collective-permute-start | bytes 37640 | tf_op jit(solution)/shard_map/ppermute | solution.py:20
  8.2 12.6 %collective-permute-start.4 = (bf16[2,196,256]{2,1,0:T(8,128)(2,1)S(1)}, bf16[2,196,256]{2,1,0:T(8,128)(2,1)S(1)}, u32[]{:S(2)}, u32[]{:S(2)}) collective-permute-start(bf16[2,196,256]{2,1,0:T(8,128)(2,1)S(1)} %get-tuple-element.41.own), channel_id=1, source_target_pairs={{0,3},{1,2},{2,1},{3,0},{4,7},{5,6},{6,5},{7,4},{8,11},{9,10},{10,... | collective-permute-start | bytes 602120 | tf_op jit(solution)/shard_map/ppermute | solution.py:20
  20.9 2.0 %collective-permute-start.6 = (bf16[2,196,256]{2,1,0:T(8,128)(2,1)S(1)}, bf16[2,196,256]{2,1,0:T(8,128)(2,1)S(1)}, u32[]{:S(2)}, u32[]{:S(2)}) collective-permute-start(bf16[2,196,256]{2,1,0:T(8,128)(2,1)S(1)} %collective-permute-done.4.across), channel_id=1, source_target_pairs={{0,1},{1,0},{2,3},{3,2},{4,5},{5,4},{6,7},{7,6},{8,9},{9,8},{10,11... | collective-permute-start | bytes 602120 | tf_op jit(solution)/shard_map/ppermute | solution.py:16
  21.4 1.3 %collective-permute-start.5 = (bf16[2,16,1024]{2,1,0:T(8,128)(2,1)S(1)}, bf16[2,16,1024]{2,1,0:T(8,128)(2,1)S(1)}, u32[]{:S(2)}, u32[]{:S(2)}) collective-permute-start(bf16[2,16,1024]{2,1,0:T(8,128)(2,1)S(1)} %shard_map.80.first), channel_id=1, source_target_pairs={{0,1},{1,0},{2,3},{3,2},{4,5},{5,4},{6,7},{7,6},{8,9},{9,8},{10,11... | collective-permute-start | bytes 196616 | tf_op jit(solution)/shard_map/ppermute | solution.py:16

commit v9 on v8

--- a/solution.py
+++ b/solution.py
@@ -16,8 +16,8 @@
     return lax.ppermute(array, axis, [(0, 1), (1, 0)])
 
 
-def cross(array):
-    return lax.ppermute(array, ("x", "core"), [(0, 3), (1, 2), (2, 1), (3, 0)])
+def cross(array, halves):
+    return lax.ppermute(array, ("x", "core"), [(i, halves - 1 - i) for i in range(halves)])
 
 
 def dot(left, right, over):
@@ -214,7 +214,7 @@
     (logits,) = call(
         functools.partial(add_kernel, slots, lead), [(table, F32)], logits, beside[0], swap(slot_params.T, "core")
     )
-    other = cross(logits)
+    other = cross(logits, halves)
     chunks = 2
     shapes = [w_up.shape[1:], w_down.shape[1:], w_up.shape[:0:-1], w_down.shape[:0:-1]]
     weights = call(
@@ -227,7 +227,7 @@
         in_hbm=(1, 2),
     )
     other, own_later, *weights = lax.optimization_barrier((other, own, *weights))
-    across = cross(own_later)
+    across = cross(own_later, halves)
     blocks, dispatch, combine = call(
         functools.partial(slot_kernel, slots, x_size),
         [((x_size * experts, 2 * slots, 2 * quarter), BF16), (table, F32), (table, F32)],

time: 42.2 us -> 42.2 us (level)
  no operation moved by 1% of the time
where the time goes in v9:
time: 42.2 us; the launch traced here: 41.7 us
  blocking collectives  28 us (66%)
  Pallas kernels  7 us (17%)
  starting transfers between devices  4.81 us (11%)
  waiting for transfers between devices  1.2 us (3%)
  between operations  0.7 us (2%)
    all_to_all x2, blocking collectives, local(): lax.all_to_all(blocks, axes, 0, 0, tiled=True, axis_index_groups=wide)  20.5 us
    all_to_all x1, blocking collectives, local(): lax.all_to_all(params_part, axes, 0, 0, tiled=True, axis_index_groups=nar...  7.52 us
    pallas_call x8, Pallas kernels, call(): run(*(pltpu.with_memory_space_constraint(arg, pltpu.HBM) if i in in_hbm e...  7 us
    ppermute x2, starting transfers between devices, cross(): lax.ppermute(array, ('x', 'core'), [(i, halves - 1 - i) for i in range(ha...  3.12 us
    ppermute x5, starting transfers between devices, swap(): return lax.ppermute(array, axis, [(0, 1), (1, 0)])  1.69 us
    ppermute x5, waiting for transfers between devices, swap(): return lax.ppermute(array, axis, [(0, 1), (1, 0)])  1.2 us
  transfers between devices with their start and end apart: 7, of which 1 were waited for; matrix products, arithmetic and copies ran while one was open for 0% of the time, Pallas kernels for 13%

profile of v9, /device:TPU:0, one launch (start us, length us, event | category | flops | bytes accessed | tf_op | source)
XLA Modules:
  0.0 41.7 jit_solution(9177024616205967125)
XLA Ops:
  0.6 0.5 %collective-permute-start = (bf16[196,256]{1,0:T(8,128)(2,1)}, bf16[196,256]{1,0:T(8,128)(2,1)S(1)}, u32[]{:S(2)}, u32[]{:S(2)}) collective-permute-start(bf16[196,256]{1,0:T(8,128)(2,1)} %tokens.1), channel_id=1, source_target_pairs={{0,1},{1,0},{2,3},{3,2},{4,5},{5,4},{6,7},{7,6},{8,9},{9,8},{10,11... | collective-permute-start | bytes 301064 | tf_op jit(solution)/shard_map/ppermute | solution.py:16
  1.1 0.1 collective-permute-start.3
  1.2 0.4 %collective-permute-start.1 = (bf16[16,256]{1,0:T(8,128)(2,1)}, bf16[16,256]{1,0:T(8,128)(2,1)S(1)}, u32[]{:S(2)}, u32[]{:S(2)}) collective-permute-start(bf16[16,256]{1,0:T(8,128)(2,1)} %bitcast.2), channel_id=1, source_target_pairs={{0,1},{1,0},{2,3},{3,2},{4,5},{5,4},{6,7},{7,6},{8,9},{9,8},{10,11... | collective-permute-start | bytes 24584 | tf_op jit(solution)/shard_map/ppermute | solution.py:16
  1.7 1.1 %shard_map.76 = (bf16[2,196,256]{2,1,0:T(8,128)(2,1)S(1)}, bf16[16,256]{1,0:T(8,128)(2,1)S(1)}, f32[16,196]{1,0:T(8,128)S(1)}) custom-call(bf16[196,256]{1,0:T(8,128)(2,1)} %tokens.1, bf16[196,256]{1,0:T(8,128)(2,1)} %cotangent.1, bf16[16,256]{1,0:T(8,128)(2,1)} %bitcast.3), custom_call_target="tpu_custom_call" | custom-call | tf_op jit(solution)/shard_map/pallas_call | solution.py:180
  2.8 0.0 collective-permute-done.1.params
  2.8 0.0 collective-permute-done.tokens
  2.8 0.1 shard_map.77.after.first
  2.9 2.6 %collective-permute-start.2 = (f32[16,196]{1,0:T(8,128)S(1)}, f32[16,196]{1,0:T(8,128)S(1)}, u32[]{:S(2)}, u32[]{:S(2)}) collective-permute-start(f32[16,196]{1,0:T(8,128)S(1)} %shard_map.77.after.first), channel_id=1, source_target_pairs={{0,3},{1,2},{2,1},{3,0},{4,7},{5,6},{6,5},{7,4},{8,11},{9,10},{10,... | collective-permute-start | bytes 37640 | tf_op jit(solution)/shard_map/ppermute | solution.py:20
  5.6 2.7 %shard_map.78 = (bf16[1024,1024]{1,0:T(8,128)(2,1)S(1)}, bf16[1024,1024]{1,0:T(8,128)(2,1)S(1)}, bf16[1024,1024]{1,0:T(8,128)(2,1)S(1)}, bf16[1024,1024]{1,0:T(8,128)(2,1)S(1)}) custom-call(f32[16,196]{1,0:T(8,128)S(1)} %shard_map.77.after.first, bf16[1,1024,1024]{2,1,0:T(8,128)(2,1)} %up_matrix.1, bf16[1,1024,1024]{2,1,0:T(8,128)(2,1)} %down_matrix.1), custom_call_target="tpu_custom_call" | custom-call | tf_op jit(solution)/shard_map/pallas_call | solution.py:180
  8.2 0.0 collective-permute-done.2.second
  8.2 0.5 %collective-permute-start.4 = (bf16[2,196,256]{2,1,0:T(8,128)(2,1)S(1)}, bf16[2,196,256]{2,1,0:T(8,128)(2,1)S(1)}, u32[]{:S(2)}, u32[]{:S(2)}) collective-permute-start(bf16[2,196,256]{2,1,0:T(8,128)(2,1)S(1)} %get-tuple-element.41.own), channel_id=1, source_target_pairs={{0,3},{1,2},{2,1},{3,0},{4,7},{5,6},{6,5},{7,4},{8,11},{9,10},{10,... | collective-permute-start | bytes 602120 | tf_op jit(solution)/shard_map/ppermute | solution.py:20
  8.7 0.0 collective-permute-done.3.cotangent
  8.7 0.3 shard_map.79
  9.1 10.6 %all_to_all.15.blocks = bf16[16,4,512]{2,1,0:T(4,128)(2,1)S(1)} all-to-all(bf16[16,4,512]{2,1,0:T(4,128)(2,1)S(1)} %get-tuple-element.36), channel_id=1, replica_groups={{21,25,29,1,5,9,13,17,22,26,30,2,6,10,14,18},{23,27,31,3,7,11,15,19,20,..., dimensions={0} | all-to-all | bytes 131072 | tf_op jit(solution)/shard_map/all_to_all | solution.py:240
  19.6 1.2 %shard_map.80.first = bf16[2,16,1024]{2,1,0:T(8,128)(2,1)S(1)} custom-call(bf16[16,4,512]{2,1,0:T(4,128)(2,1)S(1)} %all_to_all.15.blocks, bf16[1024,1024]{1,0:T(8,128)(2,1)S(1)} %get-tuple-element.37.up_matrix, bf16[1024,1024]{1,0:T(8,128)(2,1)S(1)} %get-tuple-element.38.down_matrix, bf16[1024,1024]{1,0:T(8,128)(2,1)S(1)} %get-tuple-element.39.up_turned, ...), custom_call_target="tpu_custom_call" | custom-call | tf_op jit(solution)/shard_map/pallas_call | solution.py:180
  20.8 0.0 collective-permute-done.4.across
  20.9 0.6 %collective-permute-start.6 = (bf16[2,196,256]{2,1,0:T(8,128)(2,1)S(1)}, bf16[2,196,256]{2,1,0:T(8,128)(2,1)S(1)}, u32[]{:S(2)}, u32[]{:S(2)}) collective-permute-start(bf16[2,196,256]{2,1,0:T(8,128)(2,1)S(1)} %collective-permute-done.4.across), channel_id=1, source_target_pairs={{0,1},{1,0},{2,3},{3,2},{4,5},{5,4},{6,7},{7,6},{8,9},{9,8},{10,11... | collective-permute-start | bytes 602120 | tf_op jit(solution)/shard_map/ppermute | solution.py:16
  21.4 0.1 collective-permute-start.5
  21.5 1.2 %collective-permute-done.5.second = bf16[2,16,1024]{2,1,0:T(8,128)(2,1)S(1)} collective-permute-done((bf16[2,16,1024]{2,1,0:T(8,128)(2,1)S(1)}, bf16[2,16,1024]{2,1,0:T(8,128)(2,1)S(1)}, u32[]{:S(2)}, u32[]{:S(2)}) %collective-permute-start.5) | collective-permute-done | bytes 65568 | tf_op jit(solution)/shard_map/ppermute | solution.py:16
  22.7 0.1 shard_map.81
  22.8 0.0 collective-permute-done.6.corner
  22.8 10.0 %all_to_all.16.blocks = bf16[16,4,1024]{2,1,0:T(4,128)(2,1)S(1)} all-to-all(bf16[16,4,1024]{2,1,0:T(4,128)(2,1)S(1)} %shard_map.81), channel_id=1, replica_groups={{21,25,29,1,5,9,13,17,22,26,30,2,6,10,14,18},{23,27,31,3,7,11,15,19,20,..., dimensions={0} | all-to-all | bytes 262144 | tf_op jit(solution)/shard_map/all_to_all | solution.py:255
  32.8 0.7 %shard_map.82 = (bf16[8,16,256]{2,1,0:T(8,128)(2,1)S(1)}, bf16[196,256]{1,0:T(8,128)(2,1)S(1)}, bf16[196,256]{1,0:T(8,128)(2,1)S(1)}) custom-call(bf16[16,4,1024]{2,1,0:T(4,128)(2,1)S(1)} %all_to_all.16.blocks, bf16[2,196,256]{2,1,0:T(8,128)(2,1)S(1)} %get-tuple-element.41.own, bf16[196,256]{1,0:T(8,128)(2,1)S(1)} %collective-permute-done.tokens, ...), custom_call_target="tpu_custom_call" | custom-call | tf_op jit(solution)/shard_map/pallas_call | solution.py:180
  33.5 7.5 %all_to_all.17.parts = bf16[8,16,256]{2,1,0:T(8,128)(2,1)S(1)} all-to-all(bf16[8,16,256]{2,1,0:T(8,128)(2,1)S(1)} %get-tuple-element.49), channel_id=1, replica_groups={{21,0,4,8,12,17,25,29},{20,1,5,9,13,16,24,28},{23,2,6,10,14,19,27,31},{..., dimensions={0} | all-to-all | bytes 131072 | tf_op jit(solution)/shard_map/all_to_all | solution.py:271
  41.1 0.7 %shard_map.83 = (bf16[196,256]{1,0:T(8,128)(2,1)}, bf16[196,256]{1,0:T(8,128)(2,1)}, f32[16,256]{1,0:T(8,128)}) custom-call(bf16[8,16,256]{2,1,0:T(8,128)(2,1)S(1)} %all_to_all.17.parts, bf16[196,256]{1,0:T(8,128)(2,1)S(1)} %get-tuple-element.50.mixed_here, bf16[196,256]{1,0:T(8,128)(2,1)S(1)} %get-tuple-element.51.grad_tokens_here), custom_call_target="tpu_custom_call" | custom-call | tf_op jit(solution)/shard_map/pallas_call | solution.py:180
Async XLA Ops:
  0.6 2.2 %collective-permute-start = (bf16[196,256]{1,0:T(8,128)(2,1)}, bf16[196,256]{1,0:T(8,128)(2,1)S(1)}, u32[]{:S(2)}, u32[]{:S(2)}) collective-permute-start(bf16[196,256]{1,0:T(8,128)(2,1)} %tokens.1), channel_id=1, source_target_pairs={{0,1},{1,0},{2,3},{3,2},{4,5},{5,4},{6,7},{7,6},{8,9},{9,8},{10,11... | collective-permute-start | bytes 301064 | tf_op jit(solution)/shard_map/ppermute | solution.py:16
  1.1 7.6 %collective-permute-start.3 = (bf16[196,256]{1,0:T(8,128)(2,1)}, bf16[196,256]{1,0:T(8,128)(2,1)S(1)}, u32[]{:S(2)}, u32[]{:S(2)}) collective-permute-start(bf16[196,256]{1,0:T(8,128)(2,1)} %cotangent.1), channel_id=1, source_target_pairs={{0,1},{1,0},{2,3},{3,2},{4,5},{5,4},{6,7},{7,6},{8,9},{9,8},{10,11... | collective-permute-start | bytes 301064 | tf_op jit(solution)/shard_map/ppermute | solution.py:16
  1.2 1.6 %collective-permute-start.1 = (bf16[16,256]{1,0:T(8,128)(2,1)}, bf16[16,256]{1,0:T(8,128)(2,1)S(1)}, u32[]{:S(2)}, u32[]{:S(2)}) collective-permute-start(bf16[16,256]{1,0:T(8,128)(2,1)} %bitcast.2), channel_id=1, source_target_pairs={{0,1},{1,0},{2,3},{3,2},{4,5},{5,4},{6,7},{7,6},{8,9},{9,8},{10,11... | collective-permute-start | bytes 24584 | tf_op jit(solution)/shard_map/ppermute | solution.py:16
  2.9 5.3 %collective-permute-start.2 = (f32[16,196]{1,0:T(8,128)S(1)}, f32[16,196]{1,0:T(8,128)S(1)}, u32[]{:S(2)}, u32[]{:S(2)}) collective-permute-start(f32[16,196]{1,0:T(8,128)S(1)} %shard_map.77.after.first), channel_id=1, source_target_pairs={{0,3},{1,2},{2,1},{3,0},{4,7},{5,6},{6,5},{7,4},{8,11},{9,10},{10,... | collective-permute-start | bytes 37640 | tf_op jit(solution)/shard_map/ppermute | solution.py:20
  8.2 12.6 %collective-permute-start.4 = (bf16[2,196,256]{2,1,0:T(8,128)(2,1)S(1)}, bf16[2,196,256]{2,1,0:T(8,128)(2,1)S(1)}, u32[]{:S(2)}, u32[]{:S(2)}) collective-permute-start(bf16[2,196,256]{2,1,0:T(8,128)(2,1)S(1)} %get-tuple-element.41.own), channel_id=1, source_target_pairs={{0,3},{1,2},{2,1},{3,0},{4,7},{5,6},{6,5},{7,4},{8,11},{9,10},{10,... | collective-permute-start | bytes 602120 | tf_op jit(solution)/shard_map/ppermute | solution.py:20
  20.9 2.0 %collective-permute-start.6 = (bf16[2,196,256]{2,1,0:T(8,128)(2,1)S(1)}, bf16[2,196,256]{2,1,0:T(8,128)(2,1)S(1)}, u32[]{:S(2)}, u32[]{:S(2)}) collective-permute-start(bf16[2,196,256]{2,1,0:T(8,128)(2,1)S(1)} %collective-permute-done.4.across), channel_id=1, source_target_pairs={{0,1},{1,0},{2,3},{3,2},{4,5},{5,4},{6,7},{7,6},{8,9},{9,8},{10,11... | collective-permute-start | bytes 602120 | tf_op jit(solution)/shard_map/ppermute | solution.py:16
  21.4 1.3 %collective-permute-start.5 = (bf16[2,16,1024]{2,1,0:T(8,128)(2,1)S(1)}, bf16[2,16,1024]{2,1,0:T(8,128)(2,1)S(1)}, u32[]{:S(2)}, u32[]{:S(2)}) collective-permute-start(bf16[2,16,1024]{2,1,0:T(8,128)(2,1)S(1)} %shard_map.80.first), channel_id=1, source_target_pairs={{0,1},{1,0},{2,3},{3,2},{4,5},{5,4},{6,7},{7,6},{8,9},{9,8},{10,11... | collective-permute-start | bytes 196616 | tf_op jit(solution)/shard_map/ppermute | solution.py:16

commit v10 on v9

--- a/solution.py
+++ b/solution.py
@@ -85,20 +85,20 @@
     total[...] = logits[...] + dot(params_in, tokens[...], (1, 1))
 
 
-def weight_kernel(chunks, after, up_matrix, down_matrix, up_here, down_here, up_turned, down_turned, sems):
-    sides = ((up_matrix, up_here, up_turned), (down_matrix, down_here, down_turned))
+def weight_kernel(chunks, after, up_matrix, down_matrix, up_here, down_here, up_turned, sems):
     copies = []
-    for i, (source, target, _) in enumerate(sides):
+    for i, (source, target) in enumerate(((up_matrix, up_here), (down_matrix, down_here))):
         step = source.shape[1] // chunks
         for j in range(chunks):
             part = pl.ds(j * step, step)
             copies.append(pltpu.make_async_copy(source.at[0, part], target.at[part], sems.at[i * chunks + j]))
             copies[-1].start()
-    for i, (_, target, turned) in enumerate(sides):
-        step = target.shape[0] // chunks
-        for j in range(chunks):
-            copies[i * chunks + j].wait()
-            turned[:, j * step : (j + 1) * step] = target[j * step : (j + 1) * step].T
+    step = up_here.shape[0] // chunks
+    for j in range(chunks):
+        copies[j].wait()
+        up_turned[:, j * step : (j + 1) * step] = up_here[j * step : (j + 1) * step].T
+    for copy in copies[chunks:]:
+        copy.wait()
 
 
 def slot_kernel(slots, x_size, first, second, own, tokens, cotangent, blocks, dispatch, combine):
@@ -115,7 +115,7 @@
         blocks[:, :, here] = to_blocks(slot_in, grad_out, slots, x_size)
 
 
-def expert_kernel(slots, x_size, blocks, up_matrix, down_matrix, up_turned, down_turned, sums):
+def expert_kernel(slots, x_size, blocks, up_matrix, down_matrix, up_turned, sums):
     got = blocks[...].astype(F32)
     first, second = jnp.split(got, x_size)
     in_order = lax.axis_index("x") != lax.axis_index("core")
@@ -123,7 +123,7 @@
     sides = [from_blocks(part, slots) for part in parts]
     forward, backward = (jnp.concatenate(side, axis=1).astype(BF16) for side in zip(*sides))
     preact = dot(forward, up_matrix[...], (1, 0))
-    grad_hidden = dot(backward, down_turned[...], (1, 0))
+    grad_hidden = dot(backward, down_matrix[...], (1, 1))
     hidden, slope = gelu_parts(preact)
     sums[0] = dot(hidden.astype(BF16), down_matrix[...], (1, 0)).astype(BF16)
     sums[1] = dot((grad_hidden * slope).astype(BF16), up_turned[...], (1, 0)).astype(BF16)
@@ -216,7 +216,7 @@
     )
     other = cross(logits, halves)
     chunks = 2
-    shapes = [w_up.shape[1:], w_down.shape[1:], w_up.shape[:0:-1], w_down.shape[:0:-1]]
+    shapes = [w_up.shape[1:], w_down.shape[1:], w_up.shape[:0:-1]]
     weights = call(
         functools.partial(weight_kernel, chunks),
         [pltpu.VMEM(shape, BF16) for shape in shapes],

time: 42.2 us -> 42 us (level)
    ppermute x2, starting transfers between devices: 3.12 us -> 3.57 us  [cross(): lax.ppermute(array, ('x', 'core'), [(i, halves - 1 - i) for i in range(ha...]
where the time goes in v10:
time: 42 us; the launch traced here: 41.6 us
  blocking collectives  27.9 us (66%)
  Pallas kernels  6.82 us (16%)
  starting transfers between devices  5.12 us (12%)
  waiting for transfers between devices  1.05 us (2%)
  between operations  0.7 us (2%)
    all_to_all x2, blocking collectives, local(): lax.all_to_all(blocks, axes, 0, 0, tiled=True, axis_index_groups=wide)  20.4 us
    all_to_all x1, blocking collectives, local(): lax.all_to_all(params_part, axes, 0, 0, tiled=True, axis_index_groups=nar...  7.52 us
    pallas_call x8, Pallas kernels, call(): run(*(pltpu.with_memory_space_constraint(arg, pltpu.HBM) if i in in_hbm e...  6.82 us
    ppermute x2, starting transfers between devices, cross(): lax.ppermute(array, ('x', 'core'), [(i, halves - 1 - i) for i in range(ha...  3.57 us
    ppermute x5, starting transfers between devices, swap(): return lax.ppermute(array, axis, [(0, 1), (1, 0)])  1.55 us
    ppermute x5, waiting for transfers between devices, swap(): return lax.ppermute(array, axis, [(0, 1), (1, 0)])  1.05 us
  transfers between devices with their start and end apart: 7, of which 1 were waited for; matrix products, arithmetic and copies ran while one was open for 0% of the time, Pallas kernels for 13%

profile of v10, /device:TPU:0, one launch (start us, length us, event | category | flops | bytes accessed | tf_op | source)
XLA Modules:
  0.0 41.6 jit_solution(15924396051098800309)
XLA Ops:
  0.6 0.5 %collective-permute-start = (bf16[196,256]{1,0:T(8,128)(2,1)}, bf16[196,256]{1,0:T(8,128)(2,1)S(1)}, u32[]{:S(2)}, u32[]{:S(2)}) collective-permute-start(bf16[196,256]{1,0:T(8,128)(2,1)} %tokens.1), channel_id=1, source_target_pairs={{0,1},{1,0},{2,3},{3,2},{4,5},{5,4},{6,7},{7,6},{8,9},{9,8},{10,11... | collective-permute-start | bytes 301064 | tf_op jit(solution)/shard_map/ppermute | solution.py:16
  1.1 0.1 collective-permute-start.3
  1.2 0.4 %collective-permute-start.1 = (bf16[16,256]{1,0:T(8,128)(2,1)}, bf16[16,256]{1,0:T(8,128)(2,1)S(1)}, u32[]{:S(2)}, u32[]{:S(2)}) collective-permute-start(bf16[16,256]{1,0:T(8,128)(2,1)} %bitcast.2), channel_id=1, source_target_pairs={{0,1},{1,0},{2,3},{3,2},{4,5},{5,4},{6,7},{7,6},{8,9},{9,8},{10,11... | collective-permute-start | bytes 24584 | tf_op jit(solution)/shard_map/ppermute | solution.py:16
  1.7 1.1 %shard_map.76 = (bf16[2,196,256]{2,1,0:T(8,128)(2,1)S(1)}, bf16[16,256]{1,0:T(8,128)(2,1)S(1)}, f32[16,196]{1,0:T(8,128)S(1)}) custom-call(bf16[196,256]{1,0:T(8,128)(2,1)} %tokens.1, bf16[196,256]{1,0:T(8,128)(2,1)} %cotangent.1, bf16[16,256]{1,0:T(8,128)(2,1)} %bitcast.3), custom_call_target="tpu_custom_call" | custom-call | tf_op jit(solution)/shard_map/pallas_call | solution.py:180
  2.8 0.0 collective-permute-done.1.params
  2.8 0.0 collective-permute-done.tokens
  2.8 0.1 shard_map.77.after.first
  2.9 2.6 %collective-permute-start.2 = (f32[16,196]{1,0:T(8,128)S(1)}, f32[16,196]{1,0:T(8,128)S(1)}, u32[]{:S(2)}, u32[]{:S(2)}) collective-permute-start(f32[16,196]{1,0:T(8,128)S(1)} %shard_map.77.after.first), channel_id=1, source_target_pairs={{0,3},{1,2},{2,1},{3,0},{4,7},{5,6},{6,5},{7,4},{8,11},{9,10},{10,... | collective-permute-start | bytes 37640 | tf_op jit(solution)/shard_map/ppermute | solution.py:20
  5.6 2.2 %shard_map.78 = (bf16[1024,1024]{1,0:T(8,128)(2,1)S(1)}, bf16[1024,1024]{1,0:T(8,128)(2,1)S(1)}, bf16[1024,1024]{1,0:T(8,128)(2,1)S(1)}) custom-call(f32[16,196]{1,0:T(8,128)S(1)} %shard_map.77.after.first, bf16[1,1024,1024]{2,1,0:T(8,128)(2,1)} %up_matrix.1, bf16[1,1024,1024]{2,1,0:T(8,128)(2,1)} %down_matrix.1), custom_call_target="tpu_custom_call" | custom-call | tf_op jit(solution)/shard_map/pallas_call | solution.py:180
  7.8 0.0 collective-permute-done.2.second
  7.8 0.9 %collective-permute-start.4 = (bf16[2,196,256]{2,1,0:T(8,128)(2,1)S(1)}, bf16[2,196,256]{2,1,0:T(8,128)(2,1)S(1)}, u32[]{:S(2)}, u32[]{:S(2)}) collective-permute-start(bf16[2,196,256]{2,1,0:T(8,128)(2,1)S(1)} %get-tuple-element.37.own), channel_id=1, source_target_pairs={{0,3},{1,2},{2,1},{3,0},{4,7},{5,6},{6,5},{7,4},{8,11},{9,10},{10,... | collective-permute-start | bytes 602120 | tf_op jit(solution)/shard_map/ppermute | solution.py:20
  8.7 0.0 collective-permute-done.3.cotangent
  8.7 0.3 shard_map.79
  9.1 10.6 %all_to_all.15.blocks = bf16[16,4,512]{2,1,0:T(4,128)(2,1)S(1)} all-to-all(bf16[16,4,512]{2,1,0:T(4,128)(2,1)S(1)} %get-tuple-element.33), channel_id=1, replica_groups={{21,25,29,1,5,9,13,17,22,26,30,2,6,10,14,18},{23,27,31,3,7,11,15,19,20,..., dimensions={0} | all-to-all | bytes 131072 | tf_op jit(solution)/shard_map/all_to_all | solution.py:240
  19.6 1.5 %shard_map.80.first = bf16[2,16,1024]{2,1,0:T(8,128)(2,1)S(1)} custom-call(bf16[16,4,512]{2,1,0:T(4,128)(2,1)S(1)} %all_to_all.15.blocks, bf16[1024,1024]{1,0:T(8,128)(2,1)S(1)} %get-tuple-element.34.up_matrix, bf16[1024,1024]{1,0:T(8,128)(2,1)S(1)} %get-tuple-element.35.down_matrix, bf16[1024,1024]{1,0:T(8,128)(2,1)S(1)} %get-tuple-element.36.up_turned), custom_call_target="tpu_custom_call" | custom-call | tf_op jit(solution)/shard_map/pallas_call | solution.py:180
  21.1 0.0 collective-permute-done.4.across
  21.1 0.1 collective-permute-start.6
  21.3 0.4 collective-permute-start.5
  21.6 1.0 %collective-permute-done.5.second = bf16[2,16,1024]{2,1,0:T(8,128)(2,1)S(1)} collective-permute-done((bf16[2,16,1024]{2,1,0:T(8,128)(2,1)S(1)}, bf16[2,16,1024]{2,1,0:T(8,128)(2,1)S(1)}, u32[]{:S(2)}, u32[]{:S(2)}) %collective-permute-start.5) | collective-permute-done | bytes 65568 | tf_op jit(solution)/shard_map/ppermute | solution.py:16
  22.7 0.1 shard_map.81
  22.8 0.0 collective-permute-done.6.corner
  22.8 9.8 %all_to_all.16.blocks = bf16[16,4,1024]{2,1,0:T(4,128)(2,1)S(1)} all-to-all(bf16[16,4,1024]{2,1,0:T(4,128)(2,1)S(1)} %shard_map.81), channel_id=1, replica_groups={{21,25,29,1,5,9,13,17,22,26,30,2,6,10,14,18},{23,27,31,3,7,11,15,19,20,..., dimensions={0} | all-to-all | bytes 262144 | tf_op jit(solution)/shard_map/all_to_all | solution.py:255
  32.6 0.7 %shard_map.82 = (bf16[8,16,256]{2,1,0:T(8,128)(2,1)S(1)}, bf16[196,256]{1,0:T(8,128)(2,1)S(1)}, bf16[196,256]{1,0:T(8,128)(2,1)S(1)}) custom-call(bf16[16,4,1024]{2,1,0:T(4,128)(2,1)S(1)} %all_to_all.16.blocks, bf16[2,196,256]{2,1,0:T(8,128)(2,1)S(1)} %get-tuple-element.37.own, bf16[196,256]{1,0:T(8,128)(2,1)S(1)} %collective-permute-done.tokens, ...), custom_call_target="tpu_custom_call" | custom-call | tf_op jit(solution)/shard_map/pallas_call | solution.py:180
  33.4 7.5 %all_to_all.17.parts = bf16[8,16,256]{2,1,0:T(8,128)(2,1)S(1)} all-to-all(bf16[8,16,256]{2,1,0:T(8,128)(2,1)S(1)} %get-tuple-element.45), channel_id=1, replica_groups={{21,0,4,8,12,17,25,29},{20,1,5,9,13,16,24,28},{23,2,6,10,14,19,27,31},{..., dimensions={0} | all-to-all | bytes 131072 | tf_op jit(solution)/shard_map/all_to_all | solution.py:271
  40.9 0.7 %shard_map.83 = (bf16[196,256]{1,0:T(8,128)(2,1)}, bf16[196,256]{1,0:T(8,128)(2,1)}, f32[16,256]{1,0:T(8,128)}) custom-call(bf16[8,16,256]{2,1,0:T(8,128)(2,1)S(1)} %all_to_all.17.parts, bf16[196,256]{1,0:T(8,128)(2,1)S(1)} %get-tuple-element.46.mixed_here, bf16[196,256]{1,0:T(8,128)(2,1)S(1)} %get-tuple-element.47.grad_tokens_here), custom_call_target="tpu_custom_call" | custom-call | tf_op jit(solution)/shard_map/pallas_call | solution.py:180
Async XLA Ops:
  0.6 2.2 %collective-permute-start = (bf16[196,256]{1,0:T(8,128)(2,1)}, bf16[196,256]{1,0:T(8,128)(2,1)S(1)}, u32[]{:S(2)}, u32[]{:S(2)}) collective-permute-start(bf16[196,256]{1,0:T(8,128)(2,1)} %tokens.1), channel_id=1, source_target_pairs={{0,1},{1,0},{2,3},{3,2},{4,5},{5,4},{6,7},{7,6},{8,9},{9,8},{10,11... | collective-permute-start | bytes 301064 | tf_op jit(solution)/shard_map/ppermute | solution.py:16
  1.1 7.6 %collective-permute-start.3 = (bf16[196,256]{1,0:T(8,128)(2,1)}, bf16[196,256]{1,0:T(8,128)(2,1)S(1)}, u32[]{:S(2)}, u32[]{:S(2)}) collective-permute-start(bf16[196,256]{1,0:T(8,128)(2,1)} %cotangent.1), channel_id=1, source_target_pairs={{0,1},{1,0},{2,3},{3,2},{4,5},{5,4},{6,7},{7,6},{8,9},{9,8},{10,11... | collective-permute-start | bytes 301064 | tf_op jit(solution)/shard_map/ppermute | solution.py:16
  1.2 1.6 %collective-permute-start.1 = (bf16[16,256]{1,0:T(8,128)(2,1)}, bf16[16,256]{1,0:T(8,128)(2,1)S(1)}, u32[]{:S(2)}, u32[]{:S(2)}) collective-permute-start(bf16[16,256]{1,0:T(8,128)(2,1)} %bitcast.2), channel_id=1, source_target_pairs={{0,1},{1,0},{2,3},{3,2},{4,5},{5,4},{6,7},{7,6},{8,9},{9,8},{10,11... | collective-permute-start | bytes 24584 | tf_op jit(solution)/shard_map/ppermute | solution.py:16
  2.9 4.8 %collective-permute-start.2 = (f32[16,196]{1,0:T(8,128)S(1)}, f32[16,196]{1,0:T(8,128)S(1)}, u32[]{:S(2)}, u32[]{:S(2)}) collective-permute-start(f32[16,196]{1,0:T(8,128)S(1)} %shard_map.77.after.first), channel_id=1, source_target_pairs={{0,3},{1,2},{2,1},{3,0},{4,7},{5,6},{6,5},{7,4},{8,11},{9,10},{10,... | collective-permute-start | bytes 37640 | tf_op jit(solution)/shard_map/ppermute | solution.py:20
  7.8 13.3 %collective-permute-start.4 = (bf16[2,196,256]{2,1,0:T(8,128)(2,1)S(1)}, bf16[2,196,256]{2,1,0:T(8,128)(2,1)S(1)}, u32[]{:S(2)}, u32[]{:S(2)}) collective-permute-start(bf16[2,196,256]{2,1,0:T(8,128)(2,1)S(1)} %get-tuple-element.37.own), channel_id=1, source_target_pairs={{0,3},{1,2},{2,1},{3,0},{4,7},{5,6},{6,5},{7,4},{8,11},{9,10},{10,... | collective-permute-start | bytes 602120 | tf_op jit(solution)/shard_map/ppermute | solution.py:20
  21.1 1.7 %collective-permute-start.6 = (bf16[2,196,256]{2,1,0:T(8,128)(2,1)S(1)}, bf16[2,196,256]{2,1,0:T(8,128)(2,1)S(1)}, u32[]{:S(2)}, u32[]{:S(2)}) collective-permute-start(bf16[2,196,256]{2,1,0:T(8,128)(2,1)S(1)} %collective-permute-done.4.across), channel_id=1, source_target_pairs={{0,1},{1,0},{2,3},{3,2},{4,5},{5,4},{6,7},{7,6},{8,9},{9,8},{10,11... | collective-permute-start | bytes 602120 | tf_op jit(solution)/shard_map/ppermute | solution.py:16
  21.3 1.4 %collective-permute-start.5 = (bf16[2,16,1024]{2,1,0:T(8,128)(2,1)S(1)}, bf16[2,16,1024]{2,1,0:T(8,128)(2,1)S(1)}, u32[]{:S(2)}, u32[]{:S(2)}) collective-permute-start(bf16[2,16,1024]{2,1,0:T(8,128)(2,1)S(1)} %shard_map.80.first), channel_id=1, source_target_pairs={{0,1},{1,0},{2,3},{3,2},{4,5},{5,4},{6,7},{7,6},{8,9},{9,8},{10,11... | collective-permute-start | bytes 196616 | tf_op jit(solution)/shard_map/ppermute | solution.py:16

commit v11 on v10

--- a/solution.py
+++ b/solution.py
@@ -215,7 +215,7 @@
         functools.partial(add_kernel, slots, lead), [(table, F32)], logits, beside[0], swap(slot_params.T, "core")
     )
     other = cross(logits, halves)
-    chunks = 2
+    chunks = 4
     shapes = [w_up.shape[1:], w_down.shape[1:], w_up.shape[:0:-1]]
     weights = call(
         functools.partial(weight_kernel, chunks),

time: 42 us -> 42 us (level)
  no operation moved by 1% of the time
where the time goes in v11:
time: 42 us; the launch traced here: 41.6 us
  blocking collectives  27.9 us (66%)
  Pallas kernels  6.83 us (16%)
  starting transfers between devices  5.11 us (12%)
  waiting for transfers between devices  1.05 us (2%)
  between operations  0.7 us (2%)
    all_to_all x2, blocking collectives, local(): lax.all_to_all(blocks, axes, 0, 0, tiled=True, axis_index_groups=wide)  20.4 us
    all_to_all x1, blocking collectives, local(): lax.all_to_all(params_part, axes, 0, 0, tiled=True, axis_index_groups=nar...  7.53 us
    pallas_call x8, Pallas kernels, call(): run(*(pltpu.with_memory_space_constraint(arg, pltpu.HBM) if i in in_hbm e...  6.83 us
    ppermute x2, starting transfers between devices, cross(): lax.ppermute(array, ('x', 'core'), [(i, halves - 1 - i) for i in range(ha...  3.56 us
    ppermute x5, starting transfers between devices, swap(): return lax.ppermute(array, axis, [(0, 1), (1, 0)])  1.55 us
    ppermute x5, waiting for transfers between devices, swap(): return lax.ppermute(array, axis, [(0, 1), (1, 0)])  1.05 us
  transfers between devices with their start and end apart: 7, of which 1 were waited for; matrix products, arithmetic and copies ran while one was open for 0% of the time, Pallas kernels for 13%

profile of v11, /device:TPU:0, one launch (start us, length us, event | category | flops | bytes accessed | tf_op | source)
XLA Modules:
  0.0 41.6 jit_solution(2026067745654825897)
XLA Ops:
  0.6 0.5 %collective-permute-start = (bf16[196,256]{1,0:T(8,128)(2,1)}, bf16[196,256]{1,0:T(8,128)(2,1)S(1)}, u32[]{:S(2)}, u32[]{:S(2)}) collective-permute-start(bf16[196,256]{1,0:T(8,128)(2,1)} %tokens.1), channel_id=1, source_target_pairs={{0,1},{1,0},{2,3},{3,2},{4,5},{5,4},{6,7},{7,6},{8,9},{9,8},{10,11... | collective-permute-start | bytes 301064 | tf_op jit(solution)/shard_map/ppermute | solution.py:16
  1.1 0.1 collective-permute-start.3
  1.2 0.4 %collective-permute-start.1 = (bf16[16,256]{1,0:T(8,128)(2,1)}, bf16[16,256]{1,0:T(8,128)(2,1)S(1)}, u32[]{:S(2)}, u32[]{:S(2)}) collective-permute-start(bf16[16,256]{1,0:T(8,128)(2,1)} %bitcast.2), channel_id=1, source_target_pairs={{0,1},{1,0},{2,3},{3,2},{4,5},{5,4},{6,7},{7,6},{8,9},{9,8},{10,11... | collective-permute-start | bytes 24584 | tf_op jit(solution)/shard_map/ppermute | solution.py:16
  1.7 1.1 %shard_map.76 = (bf16[2,196,256]{2,1,0:T(8,128)(2,1)S(1)}, bf16[16,256]{1,0:T(8,128)(2,1)S(1)}, f32[16,196]{1,0:T(8,128)S(1)}) custom-call(bf16[196,256]{1,0:T(8,128)(2,1)} %tokens.1, bf16[196,256]{1,0:T(8,128)(2,1)} %cotangent.1, bf16[16,256]{1,0:T(8,128)(2,1)} %bitcast.3), custom_call_target="tpu_custom_call" | custom-call | tf_op jit(solution)/shard_map/pallas_call | solution.py:180
  2.8 0.0 collective-permute-done.1.params
  2.8 0.0 collective-permute-done.tokens
  2.8 0.1 shard_map.77.after.first
  2.9 2.6 %collective-permute-start.2 = (f32[16,196]{1,0:T(8,128)S(1)}, f32[16,196]{1,0:T(8,128)S(1)}, u32[]{:S(2)}, u32[]{:S(2)}) collective-permute-start(f32[16,196]{1,0:T(8,128)S(1)} %shard_map.77.after.first), channel_id=1, source_target_pairs={{0,3},{1,2},{2,1},{3,0},{4,7},{5,6},{6,5},{7,4},{8,11},{9,10},{10,... | collective-permute-start | bytes 37640 | tf_op jit(solution)/shard_map/ppermute | solution.py:20
  5.6 2.2 %shard_map.78 = (bf16[1024,1024]{1,0:T(8,128)(2,1)S(1)}, bf16[1024,1024]{1,0:T(8,128)(2,1)S(1)}, bf16[1024,1024]{1,0:T(8,128)(2,1)S(1)}) custom-call(f32[16,196]{1,0:T(8,128)S(1)} %shard_map.77.after.first, bf16[1,1024,1024]{2,1,0:T(8,128)(2,1)} %up_matrix.1, bf16[1,1024,1024]{2,1,0:T(8,128)(2,1)} %down_matrix.1), custom_call_target="tpu_custom_call" | custom-call | tf_op jit(solution)/shard_map/pallas_call | solution.py:180
  7.8 0.0 collective-permute-done.2.second
  7.8 0.9 %collective-permute-start.4 = (bf16[2,196,256]{2,1,0:T(8,128)(2,1)S(1)}, bf16[2,196,256]{2,1,0:T(8,128)(2,1)S(1)}, u32[]{:S(2)}, u32[]{:S(2)}) collective-permute-start(bf16[2,196,256]{2,1,0:T(8,128)(2,1)S(1)} %get-tuple-element.37.own), channel_id=1, source_target_pairs={{0,3},{1,2},{2,1},{3,0},{4,7},{5,6},{6,5},{7,4},{8,11},{9,10},{10,... | collective-permute-start | bytes 602120 | tf_op jit(solution)/shard_map/ppermute | solution.py:20
  8.7 0.0 collective-permute-done.3.cotangent
  8.7 0.3 shard_map.79
  9.1 10.6 %all_to_all.15.blocks = bf16[16,4,512]{2,1,0:T(4,128)(2,1)S(1)} all-to-all(bf16[16,4,512]{2,1,0:T(4,128)(2,1)S(1)} %get-tuple-element.33), channel_id=1, replica_groups={{21,25,29,1,5,9,13,17,22,26,30,2,6,10,14,18},{23,27,31,3,7,11,15,19,20,..., dimensions={0} | all-to-all | bytes 131072 | tf_op jit(solution)/shard_map/all_to_all | solution.py:240
  19.6 1.5 %shard_map.80.first = bf16[2,16,1024]{2,1,0:T(8,128)(2,1)S(1)} custom-call(bf16[16,4,512]{2,1,0:T(4,128)(2,1)S(1)} %all_to_all.15.blocks, bf16[1024,1024]{1,0:T(8,128)(2,1)S(1)} %get-tuple-element.34.up_matrix, bf16[1024,1024]{1,0:T(8,128)(2,1)S(1)} %get-tuple-element.35.down_matrix, bf16[1024,1024]{1,0:T(8,128)(2,1)S(1)} %get-tuple-element.36.up_turned), custom_call_target="tpu_custom_call" | custom-call | tf_op jit(solution)/shard_map/pallas_call | solution.py:180
  21.1 0.0 collective-permute-done.4.across
  21.1 0.1 collective-permute-start.6
  21.3 0.4 collective-permute-start.5
  21.6 1.0 %collective-permute-done.5.second = bf16[2,16,1024]{2,1,0:T(8,128)(2,1)S(1)} collective-permute-done((bf16[2,16,1024]{2,1,0:T(8,128)(2,1)S(1)}, bf16[2,16,1024]{2,1,0:T(8,128)(2,1)S(1)}, u32[]{:S(2)}, u32[]{:S(2)}) %collective-permute-start.5) | collective-permute-done | bytes 65568 | tf_op jit(solution)/shard_map/ppermute | solution.py:16
  22.7 0.1 shard_map.81
  22.8 0.0 collective-permute-done.6.corner
  22.8 9.8 %all_to_all.16.blocks = bf16[16,4,1024]{2,1,0:T(4,128)(2,1)S(1)} all-to-all(bf16[16,4,1024]{2,1,0:T(4,128)(2,1)S(1)} %shard_map.81), channel_id=1, replica_groups={{21,25,29,1,5,9,13,17,22,26,30,2,6,10,14,18},{23,27,31,3,7,11,15,19,20,..., dimensions={0} | all-to-all | bytes 262144 | tf_op jit(solution)/shard_map/all_to_all | solution.py:255
  32.6 0.7 %shard_map.82 = (bf16[8,16,256]{2,1,0:T(8,128)(2,1)S(1)}, bf16[196,256]{1,0:T(8,128)(2,1)S(1)}, bf16[196,256]{1,0:T(8,128)(2,1)S(1)}) custom-call(bf16[16,4,1024]{2,1,0:T(4,128)(2,1)S(1)} %all_to_all.16.blocks, bf16[2,196,256]{2,1,0:T(8,128)(2,1)S(1)} %get-tuple-element.37.own, bf16[196,256]{1,0:T(8,128)(2,1)S(1)} %collective-permute-done.tokens, ...), custom_call_target="tpu_custom_call" | custom-call | tf_op jit(solution)/shard_map/pallas_call | solution.py:180
  33.4 7.5 %all_to_all.17.parts = bf16[8,16,256]{2,1,0:T(8,128)(2,1)S(1)} all-to-all(bf16[8,16,256]{2,1,0:T(8,128)(2,1)S(1)} %get-tuple-element.45), channel_id=1, replica_groups={{21,0,4,8,12,17,25,29},{20,1,5,9,13,16,24,28},{23,2,6,10,14,19,27,31},{..., dimensions={0} | all-to-all | bytes 131072 | tf_op jit(solution)/shard_map/all_to_all | solution.py:271
  40.9 0.7 %shard_map.83 = (bf16[196,256]{1,0:T(8,128)(2,1)}, bf16[196,256]{1,0:T(8,128)(2,1)}, f32[16,256]{1,0:T(8,128)}) custom-call(bf16[8,16,256]{2,1,0:T(8,128)(2,1)S(1)} %all_to_all.17.parts, bf16[196,256]{1,0:T(8,128)(2,1)S(1)} %get-tuple-element.46.mixed_here, bf16[196,256]{1,0:T(8,128)(2,1)S(1)} %get-tuple-element.47.grad_tokens_here), custom_call_target="tpu_custom_call" | custom-call | tf_op jit(solution)/shard_map/pallas_call | solution.py:180
Async XLA Ops:
  0.6 2.2 %collective-permute-start = (bf16[196,256]{1,0:T(8,128)(2,1)}, bf16[196,256]{1,0:T(8,128)(2,1)S(1)}, u32[]{:S(2)}, u32[]{:S(2)}) collective-permute-start(bf16[196,256]{1,0:T(8,128)(2,1)} %tokens.1), channel_id=1, source_target_pairs={{0,1},{1,0},{2,3},{3,2},{4,5},{5,4},{6,7},{7,6},{8,9},{9,8},{10,11... | collective-permute-start | bytes 301064 | tf_op jit(solution)/shard_map/ppermute | solution.py:16
  1.1 7.6 %collective-permute-start.3 = (bf16[196,256]{1,0:T(8,128)(2,1)}, bf16[196,256]{1,0:T(8,128)(2,1)S(1)}, u32[]{:S(2)}, u32[]{:S(2)}) collective-permute-start(bf16[196,256]{1,0:T(8,128)(2,1)} %cotangent.1), channel_id=1, source_target_pairs={{0,1},{1,0},{2,3},{3,2},{4,5},{5,4},{6,7},{7,6},{8,9},{9,8},{10,11... | collective-permute-start | bytes 301064 | tf_op jit(solution)/shard_map/ppermute | solution.py:16
  1.2 1.6 %collective-permute-start.1 = (bf16[16,256]{1,0:T(8,128)(2,1)}, bf16[16,256]{1,0:T(8,128)(2,1)S(1)}, u32[]{:S(2)}, u32[]{:S(2)}) collective-permute-start(bf16[16,256]{1,0:T(8,128)(2,1)} %bitcast.2), channel_id=1, source_target_pairs={{0,1},{1,0},{2,3},{3,2},{4,5},{5,4},{6,7},{7,6},{8,9},{9,8},{10,11... | collective-permute-start | bytes 24584 | tf_op jit(solution)/shard_map/ppermute | solution.py:16
  2.9 4.9 %collective-permute-start.2 = (f32[16,196]{1,0:T(8,128)S(1)}, f32[16,196]{1,0:T(8,128)S(1)}, u32[]{:S(2)}, u32[]{:S(2)}) collective-permute-start(f32[16,196]{1,0:T(8,128)S(1)} %shard_map.77.after.first), channel_id=1, source_target_pairs={{0,3},{1,2},{2,1},{3,0},{4,7},{5,6},{6,5},{7,4},{8,11},{9,10},{10,... | collective-permute-start | bytes 37640 | tf_op jit(solution)/shard_map/ppermute | solution.py:20
  7.8 13.3 %collective-permute-start.4 = (bf16[2,196,256]{2,1,0:T(8,128)(2,1)S(1)}, bf16[2,196,256]{2,1,0:T(8,128)(2,1)S(1)}, u32[]{:S(2)}, u32[]{:S(2)}) collective-permute-start(bf16[2,196,256]{2,1,0:T(8,128)(2,1)S(1)} %get-tuple-element.37.own), channel_id=1, source_target_pairs={{0,3},{1,2},{2,1},{3,0},{4,7},{5,6},{6,5},{7,4},{8,11},{9,10},{10,... | collective-permute-start | bytes 602120 | tf_op jit(solution)/shard_map/ppermute | solution.py:20
  21.1 1.7 %collective-permute-start.6 = (bf16[2,196,256]{2,1,0:T(8,128)(2,1)S(1)}, bf16[2,196,256]{2,1,0:T(8,128)(2,1)S(1)}, u32[]{:S(2)}, u32[]{:S(2)}) collective-permute-start(bf16[2,196,256]{2,1,0:T(8,128)(2,1)S(1)} %collective-permute-done.4.across), channel_id=1, source_target_pairs={{0,1},{1,0},{2,3},{3,2},{4,5},{5,4},{6,7},{7,6},{8,9},{9,8},{10,11... | collective-permute-start | bytes 602120 | tf_op jit(solution)/shard_map/ppermute | solution.py:16
  21.3 1.4 %collective-permute-start.5 = (bf16[2,16,1024]{2,1,0:T(8,128)(2,1)S(1)}, bf16[2,16,1024]{2,1,0:T(8,128)(2,1)S(1)}, u32[]{:S(2)}, u32[]{:S(2)}) collective-permute-start(bf16[2,16,1024]{2,1,0:T(8,128)(2,1)S(1)} %shard_map.80.first), channel_id=1, source_target_pairs={{0,1},{1,0},{2,3},{3,2},{4,5},{5,4},{6,7},{7,6},{8,9},{9,8},{10,11... | collective-permute-start | bytes 196616 | tf_op jit(solution)/shard_map/ppermute | solution.py:16

commit v12 on v10

--- a/solution.py
+++ b/solution.py
@@ -189,7 +189,7 @@
     table = (columns, seq)
     lead, middle = experts * 5 // 8, experts // 2
     order = [(lead + i) % experts for i in range(experts)]
-    near = [lead] + [i for i in range(experts) if i != lead]
+    near = [(lead - i) % experts for i in range(experts)]
     wide = [
         [(expert * x_size + (x if core else 1 - x)) * 2 + core for core in (1, 0) for expert in order]
         for x in range(x_size)

time: 42 us -> 41.9 us (level)
  no operation moved by 1% of the time
where the time goes in v12:
time: 41.9 us; the launch traced here: 41.6 us
  blocking collectives  27.9 us (67%)
  Pallas kernels  6.82 us (16%)
  starting transfers between devices  5.12 us (12%)
  waiting for transfers between devices  1.05 us (3%)
  between operations  0.7 us (2%)
    all_to_all x2, blocking collectives, local(): lax.all_to_all(blocks, axes, 0, 0, tiled=True, axis_index_groups=wide)  20.4 us
    all_to_all x1, blocking collectives, local(): lax.all_to_all(params_part, axes, 0, 0, tiled=True, axis_index_groups=nar...  7.52 us
    pallas_call x8, Pallas kernels, call(): run(*(pltpu.with_memory_space_constraint(arg, pltpu.HBM) if i in in_hbm e...  6.82 us
    ppermute x2, starting transfers between devices, cross(): lax.ppermute(array, ('x', 'core'), [(i, halves - 1 - i) for i in range(ha...  3.57 us
    ppermute x5, starting transfers between devices, swap(): return lax.ppermute(array, axis, [(0, 1), (1, 0)])  1.55 us
    ppermute x5, waiting for transfers between devices, swap(): return lax.ppermute(array, axis, [(0, 1), (1, 0)])  1.05 us
  transfers between devices with their start and end apart: 7, of which 1 were waited for; matrix products, arithmetic and copies ran while one was open for 0% of the time, Pallas kernels for 13%

profile of v12, /device:TPU:0, one launch (start us, length us, event | category | flops | bytes accessed | tf_op | source)
XLA Modules:
  0.0 41.6 jit_solution(2785476189629731786)
XLA Ops:
  0.6 0.5 %collective-permute-start = (bf16[196,256]{1,0:T(8,128)(2,1)}, bf16[196,256]{1,0:T(8,128)(2,1)S(1)}, u32[]{:S(2)}, u32[]{:S(2)}) collective-permute-start(bf16[196,256]{1,0:T(8,128)(2,1)} %tokens.1), channel_id=1, source_target_pairs={{0,1},{1,0},{2,3},{3,2},{4,5},{5,4},{6,7},{7,6},{8,9},{9,8},{10,11... | collective-permute-start | bytes 301064 | tf_op jit(solution)/shard_map/ppermute | solution.py:16
  1.1 0.1 collective-permute-start.3
  1.2 0.4 %collective-permute-start.1 = (bf16[16,256]{1,0:T(8,128)(2,1)}, bf16[16,256]{1,0:T(8,128)(2,1)S(1)}, u32[]{:S(2)}, u32[]{:S(2)}) collective-permute-start(bf16[16,256]{1,0:T(8,128)(2,1)} %bitcast.2), channel_id=1, source_target_pairs={{0,1},{1,0},{2,3},{3,2},{4,5},{5,4},{6,7},{7,6},{8,9},{9,8},{10,11... | collective-permute-start | bytes 24584 | tf_op jit(solution)/shard_map/ppermute | solution.py:16
  1.7 1.1 %shard_map.76 = (bf16[2,196,256]{2,1,0:T(8,128)(2,1)S(1)}, bf16[16,256]{1,0:T(8,128)(2,1)S(1)}, f32[16,196]{1,0:T(8,128)S(1)}) custom-call(bf16[196,256]{1,0:T(8,128)(2,1)} %tokens.1, bf16[196,256]{1,0:T(8,128)(2,1)} %cotangent.1, bf16[16,256]{1,0:T(8,128)(2,1)} %bitcast.3), custom_call_target="tpu_custom_call" | custom-call | tf_op jit(solution)/shard_map/pallas_call | solution.py:180
  2.8 0.0 collective-permute-done.1.params
  2.8 0.0 collective-permute-done.tokens
  2.8 0.1 shard_map.77.after.first
  2.9 2.6 %collective-permute-start.2 = (f32[16,196]{1,0:T(8,128)S(1)}, f32[16,196]{1,0:T(8,128)S(1)}, u32[]{:S(2)}, u32[]{:S(2)}) collective-permute-start(f32[16,196]{1,0:T(8,128)S(1)} %shard_map.77.after.first), channel_id=1, source_target_pairs={{0,3},{1,2},{2,1},{3,0},{4,7},{5,6},{6,5},{7,4},{8,11},{9,10},{10,... | collective-permute-start | bytes 37640 | tf_op jit(solution)/shard_map/ppermute | solution.py:20
  5.6 2.2 %shard_map.78 = (bf16[1024,1024]{1,0:T(8,128)(2,1)S(1)}, bf16[1024,1024]{1,0:T(8,128)(2,1)S(1)}, bf16[1024,1024]{1,0:T(8,128)(2,1)S(1)}) custom-call(f32[16,196]{1,0:T(8,128)S(1)} %shard_map.77.after.first, bf16[1,1024,1024]{2,1,0:T(8,128)(2,1)} %up_matrix.1, bf16[1,1024,1024]{2,1,0:T(8,128)(2,1)} %down_matrix.1), custom_call_target="tpu_custom_call" | custom-call | tf_op jit(solution)/shard_map/pallas_call | solution.py:180
  7.8 0.0 collective-permute-done.2.second
  7.8 0.9 %collective-permute-start.4 = (bf16[2,196,256]{2,1,0:T(8,128)(2,1)S(1)}, bf16[2,196,256]{2,1,0:T(8,128)(2,1)S(1)}, u32[]{:S(2)}, u32[]{:S(2)}) collective-permute-start(bf16[2,196,256]{2,1,0:T(8,128)(2,1)S(1)} %get-tuple-element.37.own), channel_id=1, source_target_pairs={{0,3},{1,2},{2,1},{3,0},{4,7},{5,6},{6,5},{7,4},{8,11},{9,10},{10,... | collective-permute-start | bytes 602120 | tf_op jit(solution)/shard_map/ppermute | solution.py:20
  8.7 0.0 collective-permute-done.3.cotangent
  8.7 0.3 shard_map.79
  9.1 10.6 %all_to_all.15.blocks = bf16[16,4,512]{2,1,0:T(4,128)(2,1)S(1)} all-to-all(bf16[16,4,512]{2,1,0:T(4,128)(2,1)S(1)} %get-tuple-element.33), channel_id=1, replica_groups={{21,25,29,1,5,9,13,17,22,26,30,2,6,10,14,18},{23,27,31,3,7,11,15,19,20,..., dimensions={0} | all-to-all | bytes 131072 | tf_op jit(solution)/shard_map/all_to_all | solution.py:240
  19.6 1.5 %shard_map.80.first = bf16[2,16,1024]{2,1,0:T(8,128)(2,1)S(1)} custom-call(bf16[16,4,512]{2,1,0:T(4,128)(2,1)S(1)} %all_to_all.15.blocks, bf16[1024,1024]{1,0:T(8,128)(2,1)S(1)} %get-tuple-element.34.up_matrix, bf16[1024,1024]{1,0:T(8,128)(2,1)S(1)} %get-tuple-element.35.down_matrix, bf16[1024,1024]{1,0:T(8,128)(2,1)S(1)} %get-tuple-element.36.up_turned), custom_call_target="tpu_custom_call" | custom-call | tf_op jit(solution)/shard_map/pallas_call | solution.py:180
  21.1 0.0 collective-permute-done.4.across
  21.1 0.1 collective-permute-start.6
  21.3 0.4 collective-permute-start.5
  21.6 1.0 %collective-permute-done.5.second = bf16[2,16,1024]{2,1,0:T(8,128)(2,1)S(1)} collective-permute-done((bf16[2,16,1024]{2,1,0:T(8,128)(2,1)S(1)}, bf16[2,16,1024]{2,1,0:T(8,128)(2,1)S(1)}, u32[]{:S(2)}, u32[]{:S(2)}) %collective-permute-start.5) | collective-permute-done | bytes 65568 | tf_op jit(solution)/shard_map/ppermute | solution.py:16
  22.7 0.1 shard_map.81
  22.8 0.0 collective-permute-done.6.corner
  22.8 9.8 %all_to_all.16.blocks = bf16[16,4,1024]{2,1,0:T(4,128)(2,1)S(1)} all-to-all(bf16[16,4,1024]{2,1,0:T(4,128)(2,1)S(1)} %shard_map.81), channel_id=1, replica_groups={{21,25,29,1,5,9,13,17,22,26,30,2,6,10,14,18},{23,27,31,3,7,11,15,19,20,..., dimensions={0} | all-to-all | bytes 262144 | tf_op jit(solution)/shard_map/all_to_all | solution.py:255
  32.6 0.7 %shard_map.82 = (bf16[8,16,256]{2,1,0:T(8,128)(2,1)S(1)}, bf16[196,256]{1,0:T(8,128)(2,1)S(1)}, bf16[196,256]{1,0:T(8,128)(2,1)S(1)}) custom-call(bf16[16,4,1024]{2,1,0:T(4,128)(2,1)S(1)} %all_to_all.16.blocks, bf16[2,196,256]{2,1,0:T(8,128)(2,1)S(1)} %get-tuple-element.37.own, bf16[196,256]{1,0:T(8,128)(2,1)S(1)} %collective-permute-done.tokens, ...), custom_call_target="tpu_custom_call" | custom-call | tf_op jit(solution)/shard_map/pallas_call | solution.py:180
  33.4 7.5 %all_to_all.17.parts = bf16[8,16,256]{2,1,0:T(8,128)(2,1)S(1)} all-to-all(bf16[8,16,256]{2,1,0:T(8,128)(2,1)S(1)} %get-tuple-element.45), channel_id=1, replica_groups={{21,17,12,8,4,0,29,25},{20,16,13,9,5,1,28,24},{23,19,14,10,6,2,31,27},{..., dimensions={0} | all-to-all | bytes 131072 | tf_op jit(solution)/shard_map/all_to_all | solution.py:271
  40.9 0.7 %shard_map.83 = (bf16[196,256]{1,0:T(8,128)(2,1)}, bf16[196,256]{1,0:T(8,128)(2,1)}, f32[16,256]{1,0:T(8,128)}) custom-call(bf16[8,16,256]{2,1,0:T(8,128)(2,1)S(1)} %all_to_all.17.parts, bf16[196,256]{1,0:T(8,128)(2,1)S(1)} %get-tuple-element.46.mixed_here, bf16[196,256]{1,0:T(8,128)(2,1)S(1)} %get-tuple-element.47.grad_tokens_here), custom_call_target="tpu_custom_call" | custom-call | tf_op jit(solution)/shard_map/pallas_call | solution.py:180
Async XLA Ops:
  0.6 2.2 %collective-permute-start = (bf16[196,256]{1,0:T(8,128)(2,1)}, bf16[196,256]{1,0:T(8,128)(2,1)S(1)}, u32[]{:S(2)}, u32[]{:S(2)}) collective-permute-start(bf16[196,256]{1,0:T(8,128)(2,1)} %tokens.1), channel_id=1, source_target_pairs={{0,1},{1,0},{2,3},{3,2},{4,5},{5,4},{6,7},{7,6},{8,9},{9,8},{10,11... | collective-permute-start | bytes 301064 | tf_op jit(solution)/shard_map/ppermute | solution.py:16
  1.1 7.6 %collective-permute-start.3 = (bf16[196,256]{1,0:T(8,128)(2,1)}, bf16[196,256]{1,0:T(8,128)(2,1)S(1)}, u32[]{:S(2)}, u32[]{:S(2)}) collective-permute-start(bf16[196,256]{1,0:T(8,128)(2,1)} %cotangent.1), channel_id=1, source_target_pairs={{0,1},{1,0},{2,3},{3,2},{4,5},{5,4},{6,7},{7,6},{8,9},{9,8},{10,11... | collective-permute-start | bytes 301064 | tf_op jit(solution)/shard_map/ppermute | solution.py:16
  1.2 1.6 %collective-permute-start.1 = (bf16[16,256]{1,0:T(8,128)(2,1)}, bf16[16,256]{1,0:T(8,128)(2,1)S(1)}, u32[]{:S(2)}, u32[]{:S(2)}) collective-permute-start(bf16[16,256]{1,0:T(8,128)(2,1)} %bitcast.2), channel_id=1, source_target_pairs={{0,1},{1,0},{2,3},{3,2},{4,5},{5,4},{6,7},{7,6},{8,9},{9,8},{10,11... | collective-permute-start | bytes 24584 | tf_op jit(solution)/shard_map/ppermute | solution.py:16
  2.9 4.8 %collective-permute-start.2 = (f32[16,196]{1,0:T(8,128)S(1)}, f32[16,196]{1,0:T(8,128)S(1)}, u32[]{:S(2)}, u32[]{:S(2)}) collective-permute-start(f32[16,196]{1,0:T(8,128)S(1)} %shard_map.77.after.first), channel_id=1, source_target_pairs={{0,3},{1,2},{2,1},{3,0},{4,7},{5,6},{6,5},{7,4},{8,11},{9,10},{10,... | collective-permute-start | bytes 37640 | tf_op jit(solution)/shard_map/ppermute | solution.py:20
  7.8 13.3 %collective-permute-start.4 = (bf16[2,196,256]{2,1,0:T(8,128)(2,1)S(1)}, bf16[2,196,256]{2,1,0:T(8,128)(2,1)S(1)}, u32[]{:S(2)}, u32[]{:S(2)}) collective-permute-start(bf16[2,196,256]{2,1,0:T(8,128)(2,1)S(1)} %get-tuple-element.37.own), channel_id=1, source_target_pairs={{0,3},{1,2},{2,1},{3,0},{4,7},{5,6},{6,5},{7,4},{8,11},{9,10},{10,... | collective-permute-start | bytes 602120 | tf_op jit(solution)/shard_map/ppermute | solution.py:20
  21.1 1.7 %collective-permute-start.6 = (bf16[2,196,256]{2,1,0:T(8,128)(2,1)S(1)}, bf16[2,196,256]{2,1,0:T(8,128)(2,1)S(1)}, u32[]{:S(2)}, u32[]{:S(2)}) collective-permute-start(bf16[2,196,256]{2,1,0:T(8,128)(2,1)S(1)} %collective-permute-done.4.across), channel_id=1, source_target_pairs={{0,1},{1,0},{2,3},{3,2},{4,5},{5,4},{6,7},{7,6},{8,9},{9,8},{10,11... | collective-permute-start | bytes 602120 | tf_op jit(solution)/shard_map/ppermute | solution.py:16
  21.3 1.4 %collective-permute-start.5 = (bf16[2,16,1024]{2,1,0:T(8,128)(2,1)S(1)}, bf16[2,16,1024]{2,1,0:T(8,128)(2,1)S(1)}, u32[]{:S(2)}, u32[]{:S(2)}) collective-permute-start(bf16[2,16,1024]{2,1,0:T(8,128)(2,1)S(1)} %shard_map.80.first), channel_id=1, source_target_pairs={{0,1},{1,0},{2,3},{3,2},{4,5},{5,4},{6,7},{7,6},{8,9},{9,8},{10,11... | collective-permute-start | bytes 196616 | tf_op jit(solution)/shard_map/ppermute | solution.py:16
